TPU v7x, 256 devices: a whole 4x4x8 slice. The times are simulated.
256 devices in a mesh: tm: 4 (over y), space: 64 (over z, x, core).
Axes of the slice: x: 4, y: 4, z: 8, core: 2. Of those that a mesh axis runs over, the one named last changes fastest.
Arguments:
- latents: bfloat16 [4, 64, 8, 40, 384], P('tm', 'space'), may hold values from -8 to 8
- gain_first: float32 [384], replicated, may hold values from 0.5 to 2
- shift_first: float32 [384], replicated, may hold values from -3 to 3
- kernel_first: bfloat16 [3, 3, 3, 384, 384], P(None, None, None, 'space', 'tm'), may hold values from -0.0625 to 0.0625
- bias_first: float32 [384], replicated, may hold values from -3 to 3
- gain_second: float32 [384], replicated, may hold values from 0.5 to 2
- shift_second: float32 [384], replicated, may hold values from -3 to 3
- kernel_second: bfloat16 [3, 3, 3, 384, 384], P(None, None, None, 'space', 'tm'), may hold values from -0.0625 to 0.0625
- bias_second: float32 [384], replicated, may hold values from -3 to 3
Outputs:
- decoded: bfloat16 [4, 64, 8, 40, 384], P('tm', 'space')
All inputs are finite; a program needn't handle non-finite values.
Results may differ from a plain program's by a relative error of at most 0.0085.
Values may be sent and summed in bfloat16 or wider, within the bound.
No kernel may reach another device: no remote copies, remote signals or barrier semaphores. Data moves between devices by JAX's collectives and lax.ppermute only.
A program may use at most 128 MiB of HBM per device.

v0:
```python
import jax
import jax.numpy as jnp
from jax import lax
from jax.sharding import PartitionSpec as P

GROUPS = 32
GX = 8


EPS = 1e-06


def shifted(value, axis, steps):
    count = lax.axis_size(axis)
    initial, last = (max(0, -steps), min(count, count - steps))
    return lax.ppermute(value, axis, [(source, source + steps) for source in range(initial, last)])


def spatial_halo(tile):
    column = lax.axis_index("space") % GX
    from_west = shifted(tile[:, -1:, :], "space", 1)
    from_east = shifted(tile[:, :1, :], "space", -1)
    from_west = jnp.where(column > 0, from_west, jnp.zeros_like(from_west))
    from_east = jnp.where(column < GX - 1, from_east, jnp.zeros_like(from_east))
    widened = jnp.concatenate([from_west, tile, from_east], axis=1)
    from_north = shifted(widened[-1:], "space", GX)
    from_south = shifted(widened[:1], "space", -GX)
    return jnp.concatenate([from_north, widened, from_south], axis=0)


def group_act(field, gain, shift, count):
    width = field.shape[-1] // GROUPS
    grouped = field.reshape(-1, GROUPS, width)
    total = lax.psum(jnp.sum(grouped, axis=(0, 2)), ("tm", "space"))
    mean = total / count
    centered = grouped - mean[None, :, None]
    squares = lax.psum(jnp.sum(centered * centered, axis=(0, 2)), ("tm", "space"))
    spread = squares / count
    normed = (centered * lax.rsqrt(spread + EPS)[None, :, None]).reshape(field.shape)
    return jax.nn.silu(normed * gain + shift).astype(jnp.bfloat16)


def apply_taps(stack, kernel, frames_out, rows, cols):
    width = kernel.shape[3]
    total = None
    for step_t in range(3):
        for step_y in range(3):
            for step_x in range(3):
                window = stack[
                    step_t : step_t + frames_out, step_y : step_y + rows, step_x : step_x + cols, :
                ]
                term = jnp.dot(
                    window.reshape(-1, width),
                    kernel[step_t, step_y, step_x],
                    preferred_element_type=jnp.float32,
                )
                total = term if total is None else total + term
    return total


def relay_frame(padded):
    return shifted(padded, "tm", 1)


def conv_near(act, kernel_cols, bias):
    rows, cols, channels = act.shape
    padded = spatial_halo(act)
    previous = relay_frame(padded)
    earlier = relay_frame(previous)
    stack = jnp.stack([earlier, previous, padded])
    kernel_full = lax.all_gather(kernel_cols, "space", axis=3, tiled=True)
    total = apply_taps(stack, kernel_full, 1, rows, cols)
    return total.reshape(rows, cols, channels) + bias


def shards(
    latents,
    gain_first,
    shift_first,
    kernel_first,
    bias_first,
    gain_second,
    shift_second,
    kernel_second,
    bias_second,
):
    tile = latents[0, 0].astype(jnp.float32)
    rows, cols, channels = tile.shape
    count = float(lax.axis_size("tm") * lax.axis_size("space") * rows * cols * (channels // GROUPS))
    first_act = group_act(tile, gain_first, shift_first, count)
    cols_first, cols_second = (
        lax.all_gather(kernel_first, "tm", axis=4, tiled=True),
        lax.all_gather(kernel_second, "tm", axis=4, tiled=True),
    )
    first_out = conv_near(first_act, cols_first, bias_first)
    second_act = group_act(first_out, gain_second, shift_second, count)
    second_out = conv_near(second_act, cols_second, bias_second)
    return (tile + second_out).astype(jnp.bfloat16)[None, None]


def solution(mesh):
    placed = (
        P("tm", "space", None, None, None),
        P(),
        P(),
        P(None, None, None, "space", "tm"),
        P(),
        P(),
        P(),
        P(None, None, None, "space", "tm"),
        P(),
    )
    return jax.shard_map(
        shards,
        mesh=mesh,
        in_specs=placed,
        out_specs=P("tm", "space", None, None, None),
        check_vma=False,
    )
```

profile of v0, /device:TPU:32, one launch (start us, length us, event | category | flops | bytes accessed | tf_op | source)
XLA Modules:
  0.0 538.4 jit_solution(8671705609608427689)
XLA Ops:
  8.8 33.4 %all_gather.12 = bf16[3,3,3,6,384]{3,2,1,0,4:T(4,128)(2,1)S(1)} all-gather(bf16[3,3,3,6,96]{3,2,1,0,4:T(4,128)(2,1)} %copy.14), channel_id=1, replica_groups=mesh['tm'=4,'space'=64] {'tm'}, dimensions={4}, use_global_device_ids=true | all-gather | bytes 155520 | tf_op jit(solution)/shard_map/all_gather | solution.py:92
  42.2 4.8 copy.15
  49.3 32.1 %all_gather.14 = bf16[3,3,3,6,384]{3,2,1,0,4:T(4,128)(2,1)S(1)} all-gather(bf16[3,3,3,6,96]{3,2,1,0,4:T(4,128)(2,1)} %copy.43), channel_id=1, replica_groups=mesh['tm'=4,'space'=64] {'tm'}, dimensions={4}, use_global_device_ids=true | all-gather | bytes 155520 | tf_op jit(solution)/shard_map/all_gather | solution.py:93
  81.3 4.8 copy.44
  87.4 78.3 %psum.28 = f32[32]{0:T(128)S(1)} all-reduce(f32[32]{0:T(128)S(1)} %reduce_sum.51), channel_id=1, replica_groups=mesh['tm'=4,'space'=64] {'tm','space'}, use_global_device_ids=true, to_apply=%region_2.0 | all-reduce | flops 32 | bytes 256 | tf_op jit(solution)/shard_map/psum | solution.py:34
  167.2 75.1 %psum.29 = f32[32]{0:T(128)S(1)} all-reduce(f32[32]{0:T(128)S(1)} %reduce_sum.54), channel_id=1, replica_groups=mesh['tm'=4,'space'=64] {'tm','space'}, use_global_device_ids=true, to_apply=%region_5.6 | all-reduce | flops 32 | bytes 256 | tf_op jit(solution)/shard_map/psum | solution.py:37
  245.6 5.8 %collective-permute-start.1 = (bf16[8,1,384]{2,1,0:T(2,128)(2,1)S(1)}, bf16[8,1,384]{2,1,0:T(2,128)(2,1)S(1)}, u32[]{:S(2)}, u32[]{:S(2)}) collective-permute-start(bf16[8,1,384]{2,1,0:T(2,128)(2,1)S(1)} %get-tuple-element.120), channel_id=1, source_target_pairs={{1,0},{2,1},{3,2},{4,3},{5,4},{6,5},{7,6},{8,7},{9,8},{10,9},{11,1... | collective-permute-start | bytes 18440 | tf_op jit(solution)/shard_map/ppermute | solution.py:16
  254.7 3.9 collective-permute-start.3
  260.7 3.3 collective-permute-start.4
  264.1 4.9 collective-permute-done.4
  269.0 4.4 collective-permute-start.5
  275.2 3.3 collective-permute-done.5
  279.6 16.8 %fusion.85 = (bf16[1,1,1,384,384]{4,2,1,0,3:T(2,128)(2,1)S(1)}, bf16[1,1,1,384,384]{4,2,1,0,3:T(2,128)(2,1)S(1)}, bf16[1,1,1,384,384]{4,2,1,0,3:T(2,128)(2,1)S(1...) fusion(bf16[3,3,3,384,384]{4,2,1,0,3:T(4,128)(2,1)} %all-gather, ...), kind=kLoop, calls=%fused_computation.180 | loop fusion | bytes 11206656 | tf_op jit(solution)/shard_map/slice | solution.py:54
  300.2 7.0 %fusion.86 = (bf16[1,1,1,384,384]{4,2,1,0,3:T(2,128)(2,1)S(1)}, bf16[1,1,1,384,384]{4,2,1,0,3:T(2,128)(2,1)S(1)}, bf16[1,1,1,384,384]{4,2,1,0,3:T(2,128)(2,1)S(1...) fusion(bf16[3,3,3,384,384]{4,2,1,0,3:T(4,128)(2,1)} %all-gather, ...), kind=kLoop, calls=%fused_computation.181 | loop fusion | bytes 4718592 | tf_op jit(solution)/shard_map/slice | solution.py:54
  313.4 80.4 %psum.30 = f32[32]{0:T(128)S(1)} all-reduce(f32[32]{0:T(128)S(1)} %reduce_sum.72), channel_id=1, replica_groups=mesh['tm'=4,'space'=64] {'tm','space'}, use_global_device_ids=true, to_apply=%region_8.9 | all-reduce | flops 32 | bytes 256 | tf_op jit(solution)/shard_map/psum | solution.py:34
  394.3 72.8 %psum.31 = f32[32]{0:T(128)S(1)} all-reduce(f32[32]{0:T(128)S(1)} %reduce_sum.75), channel_id=1, replica_groups=mesh['tm'=4,'space'=64] {'tm','space'}, use_global_device_ids=true, to_apply=%region_11.12 | all-reduce | flops 32 | bytes 256 | tf_op jit(solution)/shard_map/psum | solution.py:37
  469.4 5.8 %collective-permute-start.7 = (bf16[8,1,384]{2,1,0:T(2,128)(2,1)S(1)}, bf16[8,1,384]{2,1,0:T(2,128)(2,1)S(1)}, u32[]{:S(2)}, u32[]{:S(2)}) collective-permute-start(bf16[8,1,384]{2,1,0:T(2,128)(2,1)S(1)} %get-tuple-element.118), channel_id=1, source_target_pairs={{1,0},{2,1},{3,2},{4,3},{5,4},{6,5},{7,6},{8,7},{9,8},{10,9},{11,1... | collective-permute-start | bytes 18440 | tf_op jit(solution)/shard_map/ppermute | solution.py:16
  475.2 16.3 %fusion.83 = (bf16[1,1,1,384,384]{4,2,1,0,3:T(2,128)(2,1)S(1)}, bf16[1,1,1,384,384]{4,2,1,0,3:T(2,128)(2,1)S(1)}, bf16[1,1,1,384,384]{4,2,1,0,3:T(2,128)(2,1)S(1...) fusion(bf16[3,3,3,384,384]{4,2,1,0,3:T(4,128)(2,1)} %all-gather, ...), kind=kLoop, calls=%fused_computation.178 | loop fusion | bytes 11206656 | tf_op jit(solution)/shard_map/slice | solution.py:54
  493.6 3.9 collective-permute-start.9
  497.5 6.9 %fusion.84 = (bf16[1,1,1,384,384]{4,2,1,0,3:T(2,128)(2,1)S(1)}, bf16[1,1,1,384,384]{4,2,1,0,3:T(2,128)(2,1)S(1)}, bf16[1,1,1,384,384]{4,2,1,0,3:T(2,128)(2,1)S(1...) fusion(bf16[3,3,3,384,384]{4,2,1,0,3:T(4,128)(2,1)} %all-gather, ...), kind=kLoop, calls=%fused_computation.179 | loop fusion | bytes 4718592 | tf_op jit(solution)/shard_map/slice | solution.py:54
  504.6 2.8 collective-permute-start.10
  508.1 4.3 collective-permute-done.10
  515.0 4.7 collective-permute-start.11
  520.3 4.1 collective-permute-done.11
  (158 shorter events, 44.4 us)
Async XLA Ops:
  6.5 236.0 %copy-start.16 = (f32[384]{0:T(512)S(1)}, f32[384]{0:T(512)}, u32[]{:S(2)}) copy-start(f32[384]{0:T(512)} %param.10) | copy-start | bytes 4612
  6.5 236.0 %copy-start.15 = (f32[384]{0:T(512)S(1)}, f32[384]{0:T(512)}, u32[]{:S(2)}) copy-start(f32[384]{0:T(512)} %param.11) | copy-start | bytes 4612
  6.5 273.0 %all-gather.3.cloned.1.call-start = ((), (), s32[]{:S(2)}) async-start(), calls=%async_computation | async-start | bytes 10782720 | tf_op jit(solution)/shard_map/all_gather | solution.py:71
  47.0 428.2 %all-gather.5.cloned.1.call-start = ((), (), s32[]{:S(2)}) async-start(), calls=%async_computation.1 | async-start | bytes 10782720 | tf_op jit(solution)/shard_map/all_gather | solution.py:71
  243.7 7.7 %collective-permute-start = (bf16[8,1,384]{2,1,0:T(2,128)(2,1)S(1)}, bf16[8,1,384]{2,1,0:T(2,128)(2,1)S(1)}, u32[]{:S(2)}, u32[]{:S(2)}) collective-permute-start(bf16[8,1,384]{2,1,0:T(2,128)(2,1)S(1)} %get-tuple-element.119), channel_id=1, source_target_pairs={{0,1},{1,2},{2,3},{3,4},{4,5},{5,6},{6,7},{7,8},{8,9},{9,10},{10,1... | collective-permute-start | bytes 18440 | tf_op jit(solution)/shard_map/ppermute | solution.py:16
  245.6 7.1 %collective-permute-start.1 = (bf16[8,1,384]{2,1,0:T(2,128)(2,1)S(1)}, bf16[8,1,384]{2,1,0:T(2,128)(2,1)S(1)}, u32[]{:S(2)}, u32[]{:S(2)}) collective-permute-start(bf16[8,1,384]{2,1,0:T(2,128)(2,1)S(1)} %get-tuple-element.120), channel_id=1, source_target_pairs={{1,0},{2,1},{3,2},{4,3},{5,4},{6,5},{7,6},{8,7},{9,8},{10,9},{11,1... | collective-permute-start | bytes 18440 | tf_op jit(solution)/shard_map/ppermute | solution.py:16
  252.8 5.9 %collective-permute-start.2 = (bf16[1,42,384]{2,1,0:T(8,128)(2,1)S(1)}, bf16[1,42,384]{2,1,0:T(8,128)(2,1)S(1)}, u32[]{:S(2)}, u32[]{:S(2)}) collective-permute-start(bf16[1,42,384]{2,1,0:T(8,128)(2,1)S(1)} %get-tuple-element.115), channel_id=1, source_target_pairs={{0,8},{1,9},{2,10},{3,11},{4,12},{5,13},{6,14},{7,15},{8,16},{9,17... | collective-permute-start | bytes 96776 | tf_op jit(solution)/shard_map/ppermute | solution.py:16
  254.7 5.9 %collective-permute-start.3 = (bf16[1,42,384]{2,1,0:T(8,128)(2,1)S(1)}, bf16[1,42,384]{2,1,0:T(8,128)(2,1)S(1)}, u32[]{:S(2)}, u32[]{:S(2)}) collective-permute-start(bf16[1,42,384]{2,1,0:T(8,128)(2,1)S(1)} %get-tuple-element.116), channel_id=1, source_target_pairs={{8,0},{9,1},{10,2},{11,3},{12,4},{13,5},{14,6},{15,7},{16,8},{17,9... | collective-permute-start | bytes 96776 | tf_op jit(solution)/shard_map/ppermute | solution.py:16
  260.7 8.3 %collective-permute-start.4 = (bf16[10,42,384]{2,1,0:T(8,128)(2,1)S(1)}, bf16[10,42,384]{2,1,0:T(8,128)(2,1)S(1)}, u32[]{:S(2)}, u32[]{:S(2)}) collective-permute-start(bf16[10,42,384]{2,1,0:T(8,128)(2,1)S(1)} %pad_maximum_fusion), channel_id=1, source_target_pairs={{0,64},{64,128},{128,192},{1,65},{65,129},{129,193},{2,66},{66,130... | collective-permute-start | bytes 967688 | tf_op jit(solution)/shard_map/ppermute | solution.py:16
  269.0 9.4 %collective-permute-start.5 = (bf16[10,42,384]{2,1,0:T(8,128)(2,1)S(1)}, bf16[10,42,384]{2,1,0:T(8,128)(2,1)S(1)}, u32[]{:S(2)}, u32[]{:S(2)}) collective-permute-start(bf16[10,42,384]{2,1,0:T(8,128)(2,1)S(1)} %collective-permute-done.4), channel_id=1, source_target_pairs={{0,64},{64,128},{128,192},{1,65},{65,129},{129,193},{2,66},{66,130... | collective-permute-start | bytes 967688 | tf_op jit(solution)/shard_map/ppermute | solution.py:16
  279.6 18.3 %copy-start.9 = (bf16[1,8,40,384]{3,2,1,0:T(8,128)(2,1)S(1)}, bf16[1,8,40,384]{3,2,1,0:T(8,128)(2,1)}, u32[]{:S(2)}) copy-start(bf16[1,8,40,384]{3,2,1,0:T(8,128)(2,1)} %get-tuple-element.108) | copy-start | bytes 737284
  279.6 18.6 %copy-start.8 = (bf16[1,8,40,384]{3,2,1,0:T(8,128)(2,1)S(1)}, bf16[1,8,40,384]{3,2,1,0:T(8,128)(2,1)}, u32[]{:S(2)}) copy-start(bf16[1,8,40,384]{3,2,1,0:T(8,128)(2,1)} %get-tuple-element.109) | copy-start | bytes 737284
  279.6 18.9 %copy-start.7 = (bf16[1,8,40,384]{3,2,1,0:T(8,128)(2,1)S(1)}, bf16[1,8,40,384]{3,2,1,0:T(8,128)(2,1)}, u32[]{:S(2)}) copy-start(bf16[1,8,40,384]{3,2,1,0:T(8,128)(2,1)} %get-tuple-element.110) | copy-start | bytes 737284
  279.6 19.3 %copy-start.6 = (bf16[1,8,40,384]{3,2,1,0:T(8,128)(2,1)S(1)}, bf16[1,8,40,384]{3,2,1,0:T(8,128)(2,1)}, u32[]{:S(2)}) copy-start(bf16[1,8,40,384]{3,2,1,0:T(8,128)(2,1)} %get-tuple-element.111) | copy-start | bytes 737284
  279.6 19.6 %copy-start.5 = (bf16[1,8,40,384]{3,2,1,0:T(8,128)(2,1)S(1)}, bf16[1,8,40,384]{3,2,1,0:T(8,128)(2,1)}, u32[]{:S(2)}) copy-start(bf16[1,8,40,384]{3,2,1,0:T(8,128)(2,1)} %get-tuple-element.112) | copy-start | bytes 737284
  279.6 20.0 %copy-start.4 = (bf16[1,8,40,384]{3,2,1,0:T(8,128)(2,1)S(1)}, bf16[1,8,40,384]{3,2,1,0:T(8,128)(2,1)}, u32[]{:S(2)}) copy-start(bf16[1,8,40,384]{3,2,1,0:T(8,128)(2,1)} %get-tuple-element.104) | copy-start | bytes 737284
  309.7 157.6 %copy-start.17 = (f32[384]{0:T(512)S(1)}, f32[384]{0:T(512)}, u32[]{:S(2)}) copy-start(f32[384]{0:T(512)} %param.15) | copy-start | bytes 4612
  309.7 157.6 %copy-start.18 = (f32[384]{0:T(512)S(1)}, f32[384]{0:T(512)}, u32[]{:S(2)}) copy-start(f32[384]{0:T(512)} %param.14) | copy-start | bytes 4612
  467.5 24.0 %collective-permute-start.6 = (bf16[8,1,384]{2,1,0:T(2,128)(2,1)S(1)}, bf16[8,1,384]{2,1,0:T(2,128)(2,1)S(1)}, u32[]{:S(2)}, u32[]{:S(2)}) collective-permute-start(bf16[8,1,384]{2,1,0:T(2,128)(2,1)S(1)} %get-tuple-element.117), channel_id=1, source_target_pairs={{0,1},{1,2},{2,3},{3,4},{4,5},{5,6},{6,7},{7,8},{8,9},{9,10},{10,1... | collective-permute-start | bytes 18440 | tf_op jit(solution)/shard_map/ppermute | solution.py:16
  469.4 22.1 %collective-permute-start.7 = (bf16[8,1,384]{2,1,0:T(2,128)(2,1)S(1)}, bf16[8,1,384]{2,1,0:T(2,128)(2,1)S(1)}, u32[]{:S(2)}, u32[]{:S(2)}) collective-permute-start(bf16[8,1,384]{2,1,0:T(2,128)(2,1)S(1)} %get-tuple-element.118), channel_id=1, source_target_pairs={{1,0},{2,1},{3,2},{4,3},{5,4},{6,5},{7,6},{8,7},{9,8},{10,9},{11,1... | collective-permute-start | bytes 18440 | tf_op jit(solution)/shard_map/ppermute | solution.py:16
  491.6 12.8 %collective-permute-start.8 = (bf16[1,42,384]{2,1,0:T(8,128)(2,1)S(1)}, bf16[1,42,384]{2,1,0:T(8,128)(2,1)S(1)}, u32[]{:S(2)}, u32[]{:S(2)}) collective-permute-start(bf16[1,42,384]{2,1,0:T(8,128)(2,1)S(1)} %get-tuple-element.113), channel_id=1, source_target_pairs={{0,8},{1,9},{2,10},{3,11},{4,12},{5,13},{6,14},{7,15},{8,16},{9,17... | collective-permute-start | bytes 96776 | tf_op jit(solution)/shard_map/ppermute | solution.py:16
  493.6 10.9 %collective-permute-start.9 = (bf16[1,42,384]{2,1,0:T(8,128)(2,1)S(1)}, bf16[1,42,384]{2,1,0:T(8,128)(2,1)S(1)}, u32[]{:S(2)}, u32[]{:S(2)}) collective-permute-start(bf16[1,42,384]{2,1,0:T(8,128)(2,1)S(1)} %get-tuple-element.114), channel_id=1, source_target_pairs={{8,0},{9,1},{10,2},{11,3},{12,4},{13,5},{14,6},{15,7},{16,8},{17,9... | collective-permute-start | bytes 96776 | tf_op jit(solution)/shard_map/ppermute | solution.py:16
  504.6 7.8 %collective-permute-start.10 = (bf16[10,42,384]{2,1,0:T(8,128)(2,1)S(1)}, bf16[10,42,384]{2,1,0:T(8,128)(2,1)S(1)}, u32[]{:S(2)}, u32[]{:S(2)}) collective-permute-start(bf16[10,42,384]{2,1,0:T(8,128)(2,1)S(1)} %pad_maximum_fusion.1), channel_id=1, source_target_pairs={{0,64},{64,128},{128,192},{1,65},{65,129},{129,193},{2,66},{66,130... | collective-permute-start | bytes 967688 | tf_op jit(solution)/shard_map/ppermute | solution.py:16
  515.0 9.4 %collective-permute-start.11 = (bf16[10,42,384]{2,1,0:T(8,128)(2,1)S(1)}, bf16[10,42,384]{2,1,0:T(8,128)(2,1)S(1)}, u32[]{:S(2)}, u32[]{:S(2)}) collective-permute-start(bf16[10,42,384]{2,1,0:T(8,128)(2,1)S(1)} %collective-permute-done.10), channel_id=1, source_target_pairs={{0,64},{64,128},{128,192},{1,65},{65,129},{129,193},{2,66},{66,130... | collective-permute-start | bytes 967688 | tf_op jit(solution)/shard_map/ppermute | solution.py:16
  (10 other events, 112.5 us)
Sparse Core Ops, SparseCore 0:
  47.1 88.9 all-gather.2
  138.8 83.6 all-gather.4
where the time goes:
time: 542 us; the launch traced here: 538 us
  blocking collectives  372 us (69%)
  local copies, waits for them, and re-layouts  66 us (12%)
  starting transfers between devices  42.3 us (8%)
  waiting for transfers between devices  19.8 us (4%)
  matrix products  18.7 us (3%)
  between operations  14.3 us (3%)
    psum x2, blocking collectives, group_act(): total = lax.psum(jnp.sum(grouped, axis=(0, 2)), ('tm', 'space'))  159 us
    psum x2, blocking collectives, group_act(): lax.psum(jnp.sum(centered * centered, axis=(0, 2)), ('tm', 'space'))  148 us
    slice x4, local copies, waits for them, and re-layouts, apply_taps(): kernel[step_t, step_y, step_x]  47.1 us
    ppermute x12, starting transfers between devices, shifted(): lax.ppermute(value, axis, [(source, source + steps) for source in range(i...  42.2 us
    all_gather x1, blocking collectives, shards(): lax.all_gather(kernel_first, 'tm', axis=4, tiled=True)  33.4 us
    all_gather x1, blocking collectives, shards(): lax.all_gather(kernel_second, 'tm', axis=4, tiled=True)  32.1 us
    ppermute x12, waiting for transfers between devices, shifted(): lax.ppermute(value, axis, [(source, source + steps) for source in range(i...  19.7 us
    dot_general x54, matrix products, apply_taps(): jnp.dot(window.reshape(-1, width), kernel[step_t, step_y, step_x], prefer...  18.7 us
  transfers between devices with their start and end apart: 14, of which 6 were waited for; matrix products, arithmetic and copies ran while one was open for 14% of the time, Pallas kernels for 0%

commit v1 on v0

v1 whole, which is shorter than its diff:
```python
import functools

import jax
import jax.numpy as jnp
import numpy as np
from jax import lax
from jax.experimental import pallas as pl
from jax.experimental.pallas import tpu as pltpu
from jax.sharding import PartitionSpec as P

EPS = 1e-06
BF = jnp.bfloat16
F32 = jnp.float32
VM = pl.BlockSpec(memory_space=pltpu.VMEM)
SM = pl.BlockSpec(memory_space=pltpu.SMEM)
HIGH = lax.Precision.HIGHEST

NZ, NX, NC, NY = 8, 4, 2, 4
COLS = NX * NC
SPACE = NZ * COLS
ROWS, WIDE, PITCH = 8, 40, 48
CH, PART, WG = 384, 96, 12
FLAT = (ROWS + 2) * PITCH
GUARD = 16
BOTH = ("tm", "space")
ALONG_Z = [[z * COLS + q for z in range(NZ)] for q in range(COLS)]
ALONG_X = [[z * COLS + x * NC + c for x in range(NX)] for z in range(NZ) for c in range(NC)]
Y_CORE = [
    [y * SPACE + z * COLS + x * NC + c for y in range(NY) for c in range(NC)]
    for z in range(NZ)
    for x in range(NX)
]
SIBLING = [(s, s ^ 1) for s in range(SPACE)]
EAST = [(s, (s + 1) % SPACE) for s in range(SPACE)]
WEST = [(s, (s - 1) % SPACE) for s in range(SPACE)]
SOUTH = [(s, (s + COLS) % SPACE) for s in range(SPACE)]
NORTH = [(s, (s - COLS) % SPACE) for s in range(SPACE)]
SWAP = [
    (y * SPACE + z * COLS + q, (z // 2) * SPACE + (2 * y + z % 2) * COLS + q)
    for y in range(NY)
    for z in range(NZ)
    for q in range(COLS)
]


def one_hot(rows, cols, pairs):
    out = np.zeros((rows, cols), np.float32)
    for r, c in pairs:
        out[r, c] = 1.0
    return out


CHANNEL_LANES = one_hot(
    CH, CH, [(6 * (8 * z + q) + i, 48 * q + 6 * z + i) for z in range(8) for q in range(8) for i in range(6)]
)
GROUPS_OF = one_hot(CH, 128, [(c, c // WG) for c in range(CH)])
GROUPS_OF_LANES = CHANNEL_LANES.T @ GROUPS_OF
PART_GROUPS = one_hot(128, 128, [(c, c // WG) for c in range(PART)])
EDGES = one_hot(16, 320, [(r, 40 * r) for r in range(8)] + [(8 + r, 40 * r + 39) for r in range(8)])
FIRST_ROWS = one_hot(
    432, 512, [(48 * k + 6 * z + i, 64 * z + 6 * k + i) for k in range(9) for z in range(8) for i in range(6)]
)
SECOND_ROWS = one_hot(
    144, 128, [(16 * k + 6 * h + i, 64 * h + 6 * k + i) for k in range(9) for h in range(2) for i in range(6)]
)
SECOND_LANES = one_hot(512, CH, [(128 * y + o, PART * y + o) for y in range(4) for o in range(PART)])
PART_LANES = one_hot(
    128, 128, [(48 * h + 6 * q + i, 16 * q + 6 * h + i) for h in range(2) for q in range(8) for i in range(6)]
)


def dot(a, b):
    return jnp.dot(a, b, preferred_element_type=F32)


def exact(a, b):
    return jnp.dot(a, b, preferred_element_type=F32, precision=HIGH)


def split(x):
    hi = x.astype(BF).astype(F32)
    mid = (x - hi).astype(BF).astype(F32)
    return hi, mid, x - hi - mid


def moment_rows(mean, squares):
    rows = [*split(mean), *split(squares)]
    return jnp.concatenate(rows + [jnp.zeros((10, 128), F32)], axis=0).astype(BF)


def merge(means, squares, count):
    mean = jnp.mean(means, axis=0, keepdims=True)
    off = means - mean
    return mean, jnp.sum(squares, axis=0, keepdims=True) + count * jnp.sum(off * off, axis=0, keepdims=True)


def read_moments(blocks):
    means = [b[0:1] + b[1:2] + b[2:3] for b in blocks]
    squares = [b[3:4] + b[4:5] + b[5:6] for b in blocks]
    return jnp.concatenate(means, axis=0), jnp.concatenate(squares, axis=0)


def tall(row):
    return jnp.broadcast_to(row, (8, row.shape[1]))


def silu(u):
    return u / (1.0 + jnp.exp(-u))


def measure_tile(tile_ref, lanes_ref, groups_ref, groups_t_ref, edges_ref, placed_ref, edge_ref, moments_ref):
    tile = tile_ref[...]
    placed = dot(tile, lanes_ref[...]).astype(BF)
    placed_ref[...] = placed
    edge_ref[...] = dot(edges_ref[...], placed).astype(BF)
    wide = tile.astype(F32)
    per = 1.0 / (320 * WG)
    mean = exact(tall(jnp.sum(wide, axis=0, keepdims=True)), groups_ref[...]) * per
    off = wide - exact(mean, groups_t_ref[...])[0:1]
    squares = exact(tall(jnp.sum(off * off, axis=0, keepdims=True)), groups_ref[...])
    moments_ref[...] = moment_rows(mean[0:1], squares[0:1])


def arrange_first(got_ref, rows_ref, out_ref):
    parts = [
        jnp.concatenate([got_ref[z, 64 * d : 64 * d + 64, :] for z in range(NZ)], axis=0) for d in range(3)
    ]
    ordered = dot(rows_ref[...], jnp.concatenate(parts, axis=1)).astype(BF)
    means, squares = read_moments([got_ref[z, 192:208, :].astype(F32) for z in range(NZ)])
    mean, total = merge(means, squares, 320.0 * WG)
    moments = moment_rows(mean, total)
    for copy in range(NX):
        for d in range(3):
            for k in range(9):
                out_ref[copy, 48 * d : 48 * d + 48, 128 * k : 128 * k + 128] = ordered[
                    48 * k : 48 * k + 48, 128 * d : 128 * d + 128
                ]
        out_ref[copy, 144:160, 0:128] = moments
        out_ref[copy, 144:160, 128:] = jnp.zeros((16, 1024), BF)


def arrange_second(got_ref, rows_ref, lanes_ref, out_ref):
    by_part = []
    for y in range(NY):
        parts = [
            jnp.concatenate([got_ref[2 * y + h, 64 * d : 64 * d + 64, :] for h in range(2)], axis=0)
            for d in range(3)
        ]
        by_part.append(dot(rows_ref[...], jnp.concatenate(parts, axis=1)).astype(BF))
    tall_parts = [
        jnp.concatenate([by_part[y][:, 128 * d : 128 * d + 128] for y in range(NY)], axis=1) for d in range(3)
    ]
    out_ref[...] = dot(jnp.concatenate(tall_parts, axis=0), lanes_ref[...]).astype(BF)


def first_conv(
    pos_ref, lat_ref, own_ref, other_ref, moments_ref, gain_ref, shift_ref, bias_ref, lanes_ref, groups_ref,
    part_ref, part_t_ref, out_ref, west_ref, east_ref, sums_ref, weights, flat, stack,
):
    row, col, core = pos_ref[0], pos_ref[1], pos_ref[2]
    for mine in range(NC):

        @pl.when(core == mine)
        def _():
            for x in range(NX):
                for d in range(3):
                    at = CH * d + 48 * (NC * x + mine)
                    weights[at : at + 48, :] = own_ref[x, 48 * d : 48 * d + 48, :]
                    at = CH * d + 48 * (NC * x + 1 - mine)
                    weights[at : at + 48, :] = other_ref[x, 48 * d : 48 * d + 48, :]

    blocks = [moments_ref[g, x].astype(F32) for g in range(NY * NC) for x in range(NX)]
    means, squares = read_moments(blocks)
    mean, total = merge(means, squares, 320.0 * WG * NZ)
    spread = total * (1.0 / (320 * WG * NZ * NX * NC * NY))
    both = jnp.concatenate([mean, lax.rsqrt(spread + EPS), jnp.zeros((6, 128), F32)], axis=0)
    by_lane = exact(both, groups_ref[...])
    affine = exact(
        jnp.concatenate([gain_ref[...], shift_ref[...], jnp.zeros((6, CH), F32)], axis=0), lanes_ref[...]
    )
    mean_l, scale_l = by_lane[0:1], by_lane[1:2] * affine[0:1]
    shift_l = affine[1:2]
    has_w = (col > 0).astype(F32)
    has_e = (col < COLS - 1).astype(F32)
    has_n = (row > 0).astype(F32)
    has_s = (row < NZ - 1).astype(F32)
    at = lax.broadcasted_iota(jnp.int32, (PITCH, 1), 0)
    side = jnp.where(at == WIDE, has_e, jnp.where(at == PITCH - 1, has_w, jnp.where(at < WIDE, 1.0, 0.0)))
    flat[...] = jnp.zeros_like(flat)
    for t in range(NY):
        act = silu((lat_ref[t].astype(F32) - mean_l) * scale_l + shift_l)
        north, south = act[336:384] * (side * has_n), act[384:432] * (side * has_s)
        flat[GUARD : GUARD + PITCH, :] = north
        flat[GUARD - 8 : GUARD, :] = north[40:48]
        for r in range(ROWS):
            base = GUARD + PITCH * (r + 1)
            flat[base : base + WIDE, :] = act[WIDE * r : WIDE * r + WIDE]
            flat[base + WIDE : base + WIDE + 1, :] = act[328 + r : 329 + r] * has_e
            flat[base - 1 : base, :] = act[320 + r : 321 + r] * has_w
        base = GUARD + PITCH * (ROWS + 1)
        flat[base : base + PITCH, :] = south
        flat[base - 1 : base, :] = south[47:48]
        for d in range(3):
            stack[t, :, CH * d : CH * d + CH] = flat[GUARD + d - 1 : GUARD + d - 1 + FLAT, :].astype(BF)
    totals = [None] * NY
    for t in range(NY):
        for dt in range(3):
            to = t + 2 - dt
            if to >= NY:
                continue
            part = dot(stack[t], weights[:, CH * dt : CH * dt + CH])
            term = part[0:384, 0:128] + part[48:432, 128:256] + part[96:480, 256:384]
            totals[to] = term if totals[to] is None else totals[to] + term
    inside = (lax.broadcasted_iota(jnp.int32, (384, 1), 0) % PITCH < WIDE).astype(F32)
    sums = None
    for t in range(NY):
        totals[t] = totals[t] + bias_ref[...]
        line = jnp.sum(totals[t] * inside, axis=0, keepdims=True)
        sums = line if sums is None else sums + line
        for r in range(ROWS):
            out_ref[t, r] = totals[t][PITCH * r : PITCH * r + PITCH]
            west_ref[t, r : r + 1, :] = totals[t][PITCH * r : PITCH * r + 1]
            east_ref[t, r : r + 1, :] = totals[t][PITCH * r + WIDE - 1 : PITCH * r + WIDE]
    mean = exact(tall(sums), part_ref[...]) * (1.0 / (320 * NY * WG))
    mean_l = exact(mean, part_t_ref[...])[0:1]
    sums = None
    for t in range(NY):
        off = (totals[t] - mean_l) * inside
        line = jnp.sum(off * off, axis=0, keepdims=True)
        sums = line if sums is None else sums + line
    squares = exact(tall(sums), part_ref[...])
    sums_ref[:, 0:128] = jnp.broadcast_to(mean[0:1], (SPACE, 128))
    sums_ref[:, 128:256] = jnp.broadcast_to(squares[0:1], (SPACE, 128))


def second_conv(
    pos_ref, field_ref, west_ref, east_ref, north_ref, south_ref, sums_ref, gain_ref, shift_ref, own_ref, other_ref,
    part_t_ref, order_ref, out_ref, weights, flat, stack,
):
    row, col, core = pos_ref[0], pos_ref[1], pos_ref[2]
    for mine in range(NC):

        @pl.when(core == mine)
        def _():
            for x in range(NX):
                for d in range(3):
                    for k in range(9):
                        tap = 9 * (k // 3) + 3 * (k % 3) + d
                        source = 144 * d + 16 * k
                        at = 128 * tap + 16 * (NC * x + mine)
                        weights[at : at + 16, :] = own_ref[x, source : source + 16, :]
                        at = 128 * tap + 16 * (NC * x + 1 - mine)
                        weights[at : at + 16, :] = other_ref[x, source : source + 16, :]

    mean, total = merge(sums_ref[:, 0:128], sums_ref[:, 128:256], 320.0 * NY * WG)
    spread = total * (1.0 / (320 * NY * WG * SPACE))
    both = jnp.concatenate([mean, lax.rsqrt(spread + EPS), jnp.zeros((6, 128), F32)], axis=0)
    by_lane = exact(both, part_t_ref[...])
    mean_l, scale_l = by_lane[0:1], by_lane[1:2] * gain_ref[...]
    shift_l = shift_ref[...]

    def act_of(v):
        act = silu((v - mean_l) * scale_l + shift_l).astype(BF)
        return dot(act, order_ref[...])

    has_w = (col > 0).astype(F32)
    has_e = (col < COLS - 1).astype(F32)
    has_n = (row > 0).astype(F32)
    has_s = (row < NZ - 1).astype(F32)
    at = lax.broadcasted_iota(jnp.int32, (PITCH, 1), 0)
    side = jnp.where(at == WIDE, has_e, jnp.where(at == PITCH - 1, has_w, jnp.where(at < WIDE, 1.0, 0.0)))
    flat[...] = jnp.zeros_like(flat)
    for t in range(NY):
        north, south = act_of(north_ref[t]) * (side * has_n), act_of(south_ref[t]) * (side * has_s)
        left, right = act_of(west_ref[t]) * has_w, act_of(east_ref[t]) * has_e
        flat[GUARD : GUARD + PITCH, :] = north
        flat[GUARD - 8 : GUARD, :] = north[40:48]
        for r in range(ROWS):
            base = GUARD + PITCH * (r + 1)
            flat[base : base + WIDE, :] = act_of(field_ref[t, r])[0:WIDE]
            flat[base + WIDE : base + WIDE + 1, :] = right[r : r + 1]
            flat[base - 1 : base, :] = left[r : r + 1]
        base = GUARD + PITCH * (ROWS + 1)
        flat[base : base + PITCH, :] = south
        flat[base - 1 : base, :] = south[47:48]
        for dy in range(3):
            for dx in range(3):
                start = GUARD + PITCH * dy + dx - 1
                lane = 128 * (3 * dy + dx)
                stack[t, :, lane : lane + 128] = flat[start : start + 384, :].astype(BF)
    for t in range(NY):
        total = None
        for dt in range(3):
            source = t - 2 + dt
            if source < 0:
                continue
            term = dot(stack[source], weights[1152 * dt : 1152 * dt + 1152, :])
            total = term if total is None else total + term
        for r in range(ROWS):
            out_ref[t, r] = total[PITCH * r : PITCH * r + WIDE].astype(BF)


def call(body, outs, scratch, smem, *args):
    return pl.pallas_call(
        body,
        out_shape=outs,
        in_specs=[SM] * smem + [VM] * (len(args) - smem),
        out_specs=jax.tree.map(lambda _: VM, outs),
        scratch_shapes=scratch,
        compiler_params=pltpu.CompilerParams(vmem_limit_bytes=56 * 1024 * 1024),
    )(*args)


def shape(dims, dtype):
    return jax.ShapeDtypeStruct(dims, dtype)


def edge_row(row, west, east):
    gap = jnp.zeros(row.shape[:-2] + (PITCH - WIDE - 2, row.shape[-1]), row.dtype)
    return jnp.concatenate([row, east, gap, west], axis=-2)


def by_column(kernel):
    rows = jnp.transpose(kernel, (2, 0, 1, 3, 4)).reshape(3, 54, PART)
    return jnp.pad(rows, ((0, 0), (0, 10), (0, 32))).reshape(192, 128)


def shards(
    latents,
    gain_first,
    shift_first,
    kernel_first,
    bias_first,
    gain_second,
    shift_second,
    kernel_second,
    bias_second,
):
    space = lax.axis_index("space")
    frame = lax.axis_index("tm")
    pos = jnp.stack([space // COLS, space % COLS, space % NC]).astype(jnp.int32)
    tile = latents[0, 0]
    flat_tile = tile.reshape(ROWS * WIDE, CH)

    swapped = lax.ppermute(by_column(kernel_second), BOTH, SWAP)
    placed, edges, moments = call(
        measure_tile,
        (shape((320, CH), BF), shape((16, CH), BF), shape((16, 128), BF)),
        [],
        0,
        flat_tile,
        jnp.asarray(CHANNEL_LANES, BF),
        jnp.asarray(GROUPS_OF),
        jnp.asarray(GROUPS_OF.T),
        jnp.asarray(EDGES, BF),
    )
    from_west = lax.ppermute(edges[8:16], "space", EAST)
    from_east = lax.ppermute(edges[0:8], "space", WEST)

    letter = jnp.concatenate([by_column(kernel_first), moments], axis=0)
    got = lax.all_to_all(
        jnp.broadcast_to(letter[None], (NZ, 208, 128)), "space", 0, 0, tiled=True, axis_index_groups=ALONG_Z
    )
    from_north = lax.ppermute(edge_row(placed[280:320], from_west[7:8], from_east[7:8]), "space", SOUTH)
    from_south = lax.ppermute(edge_row(placed[0:40], from_west[0:1], from_east[0:1]), "space", NORTH)
    parcel = jnp.concatenate([placed, from_west, from_east, from_north, from_south], axis=0)
    frames = lax.all_gather(parcel, "tm")

    ordered = call(arrange_first, shape((NX, 160, 1152), BF), [], 0, got, jnp.asarray(FIRST_ROWS, BF))
    own = lax.all_to_all(ordered, "space", 0, 0, tiled=True, axis_index_groups=ALONG_X)
    other = lax.ppermute(own, "space", SIBLING)
    all_moments = lax.all_gather(own[:, 144:160, 0:128], BOTH, axis_index_groups=Y_CORE)

    swapped, all_moments = lax.optimization_barrier((swapped, all_moments))
    got_second = lax.all_to_all(
        jnp.broadcast_to(swapped[None], (NZ, 192, 128)), "space", 0, 0, tiled=True, axis_index_groups=ALONG_Z
    )
    ordered_second = call(
        arrange_second,
        shape((432, CH), BF),
        [],
        0,
        got_second,
        jnp.asarray(SECOND_ROWS, BF),
        jnp.asarray(SECOND_LANES, BF),
    )
    own_second = lax.all_gather(ordered_second, "space", axis_index_groups=ALONG_X)
    other_second = lax.ppermute(own_second, "space", SIBLING)

    def part_of(vector):
        mine = lax.dynamic_slice(vector, (frame * PART,), (PART,))
        return jnp.pad(mine, (0, 128 - PART))[None]

    field, west, east, sums = call(
        first_conv,
        (
            shape((NY, ROWS, PITCH, 128), F32),
            shape((NY, ROWS, 128), F32),
            shape((NY, ROWS, 128), F32),
            shape((SPACE, 256), F32),
        ),
        [
            pltpu.VMEM((3 * CH, 9 * 128), BF),
            pltpu.VMEM((GUARD + FLAT + GUARD, CH), F32),
            pltpu.VMEM((NY, FLAT, 3 * CH), BF),
        ],
        1,
        pos,
        frames,
        own,
        other,
        all_moments,
        gain_first[None],
        shift_first[None],
        part_of(bias_first),
        jnp.asarray(CHANNEL_LANES),
        jnp.asarray(GROUPS_OF_LANES.T),
        jnp.asarray(PART_GROUPS),
        jnp.asarray(PART_GROUPS.T),
    )
    west_side = lax.ppermute(east, "space", EAST)
    east_side = lax.ppermute(west, "space", WEST)
    north_side = lax.ppermute(
        edge_row(field[:, 7, :WIDE], west_side[:, 7:8], east_side[:, 7:8]), "space", SOUTH
    )
    south_side = lax.ppermute(
        edge_row(field[:, 0, :WIDE], west_side[:, 0:1], east_side[:, 0:1]), "space", NORTH
    )
    all_sums = lax.all_to_all(sums, "space", 0, 0, tiled=True)
    partial = call(
        second_conv,
        shape((NY, ROWS, WIDE, CH), BF),
        [
            pltpu.VMEM((27 * 128, CH), BF),
            pltpu.VMEM((GUARD + FLAT + GUARD, 128), F32),
            pltpu.VMEM((NY, 384, 9 * 128), BF),
        ],
        1,
        pos,
        field,
        west_side,
        east_side,
        north_side,
        south_side,
        all_sums,
        part_of(gain_second),
        part_of(shift_second),
        own_second,
        other_second,
        jnp.asarray(PART_GROUPS.T),
        jnp.asarray(PART_LANES, BF),
    )
    parts = lax.all_to_all(partial, "tm", 0, 0, tiled=True)
    second_out = jnp.sum(parts.astype(F32), axis=0) + bias_second
    return (tile.astype(F32) + second_out).astype(BF)[None, None]


def solution(mesh):
    placed = (
        P("tm", "space", None, None, None),
        P(),
        P(),
        P(None, None, None, "space", "tm"),
        P(),
        P(),
        P(),
        P(None, None, None, "space", "tm"),
        P(),
    )
    return jax.shard_map(
        shards,
        mesh=mesh,
        in_specs=placed,
        out_specs=P("tm", "space", None, None, None),
        check_vma=False,
    )
```

time: 542 us -> 221 us (0.41)
  blocking collectives: 372 us -> 74 us
  local copies, waits for them, and re-layouts: 66 us -> 11.4 us
  waiting for transfers between devices: 19.8 us -> 66 us
  Pallas kernels: 0 us -> 27.7 us
  matrix products: 18.7 us -> 0 us
  starting transfers between devices: 42.3 us -> 23.7 us
    psum x4 -> x0, blocking collectives: 307 us -> none  [the longest x2 159 us: group_act(): total = lax.psum(jnp.sum(grouped, axis=(0, 2)), ('tm', 'space'))]
    all_to_all x0 -> x3, blocking collectives: none -> 59.6 us  [the longest x1 22.4 us: shards(): lax.all_to_all(jnp.broadcast_to(letter[None], (NZ, 208, 128)), 'space', 0...]
    all_gather x2 -> x1, blocking collectives: 65.5 us -> 14.3 us  [shards(): lax.all_gather(own[:, 144:160, 0:128], BOTH, axis_index_groups=Y_CORE)]
    slice x12 -> x7, local copies, waits for them, and re-layouts: 50.7 us -> 0.04 us  [the longest x1 0.01 us: shards(): placed[0:40]]
    all_gather x2, waiting for transfers between devices: 0.02 us -> 35.7 us  [the longest x1 25.4 us: shards(): frames = lax.all_gather(parcel, 'tm')]
    ppermute x12 -> x11, starting transfers between devices: 42.2 us -> 7.78 us  [the longest x1 2.01 us: shards(): lax.ppermute(edge_row(placed[0:40], from_west[0:1], from_east[0:1]), 'spa...]
    pallas_call x0 -> x5, Pallas kernels: none -> 27.7 us  [call(): pl.pallas_call(body, out_shape=outs, in_specs=[SM] * smem + [VM] * (len(a...]
    all_to_all x0 -> x2, waiting for transfers between devices: none -> 23.3 us  [the longest x1 17 us: shards(): lax.all_to_all(ordered, 'space', 0, 0, tiled=True, axis_index_groups=ALON...]
  transfers between devices with their start and end apart: 14 -> 15, of which waited for: 6 -> 8; matrix products, arithmetic and copies ran while one was open for 14% -> 4% of each run, Pallas kernels for 0% -> 5%
where the time goes in v1:
time: 221 us; the launch traced here: 219 us
  blocking collectives  74 us (33%)
  waiting for transfers between devices  66 us (30%)
  Pallas kernels  27.7 us (13%)
  starting transfers between devices  23.7 us (11%)
  between operations  13.7 us (6%)
  local copies, waits for them, and re-layouts  11.4 us (5%)
  other arithmetic  2.35 us (1%)
    pallas_call x5, Pallas kernels, call(): pl.pallas_call(body, out_shape=outs, in_specs=[SM] * smem + [VM] * (len(a...  27.7 us
    all_gather x1, waiting for transfers between devices, shards(): frames = lax.all_gather(parcel, 'tm')  25.4 us
    all_to_all x1, blocking collectives, shards(): lax.all_to_all(jnp.broadcast_to(letter[None], (NZ, 208, 128)), 'space', 0...  22.4 us
    all_to_all x1, blocking collectives, shards(): parts = lax.all_to_all(partial, 'tm', 0, 0, tiled=True)  18.7 us
    all_to_all x1, blocking collectives, shards(): lax.all_to_all(jnp.broadcast_to(swapped[None], (NZ, 192, 128)), 'space',...  18.5 us
    all_to_all x1, waiting for transfers between devices, shards(): lax.all_to_all(ordered, 'space', 0, 0, tiled=True, axis_index_groups=ALON...  17 us
    all_gather x1, blocking collectives, shards(): lax.all_gather(own[:, 144:160, 0:128], BOTH, axis_index_groups=Y_CORE)  14.3 us
    all_to_all x1, starting transfers between devices, shards(): all_sums = lax.all_to_all(sums, 'space', 0, 0, tiled=True)  11.4 us
  transfers between devices with their start and end apart: 15, of which 8 were waited for; matrix products, arithmetic and copies ran while one was open for 4% of the time, Pallas kernels for 5%

profile of v1, /device:TPU:32, one launch (start us, length us, event | category | flops | bytes accessed | tf_op | source)
XLA Modules:
  0.0 218.8 jit_solution(14775121844777194204)
XLA Ops:
  7.4 2.8 %shard_map.208 = (bf16[320,384]{1,0:T(8,128)(2,1)}, bf16[16,384]{1,0:T(8,128)(2,1)}, bf16[16,128]{1,0:T(8,128)(2,1)}) custom-call(bf16[320,384]{1,0:T(8,128)(2,1)} %bitcast.34, bf16[384,384]{1,0:T(8,128)(2,1)} %constant.80.clone.lanes_ref, f32[384,128]{1,0:T(8,128)} %constant.81.clone.groups_ref, f32[128,384]{1,0:T(8,128)} %constant.82.clone.groups_t_ref, ...), custom_call_target="tpu_custom_call" | custom-call | tf_op jit(solution)/shard_map/pallas_call | solution.py:304
  11.0 22.4 %all_to_all.31.got_ref = bf16[8,208,128]{2,1,0:T(8,128)(2,1)} all-to-all(bf16[8,208,128]{2,1,0:T(8,128)(2,1)S(1)} %broadcast_in_dim.14), channel_id=1, replica_groups={{0,8,16,24,32,40,48,56},{1,9,17,25,33,41,49,57},{2,10,18,26,34,42,50,58..., dimensions={0} | all-to-all | bytes 851968 | tf_op jit(solution)/shard_map/all_to_all | solution.py:361
  33.4 2.8 %shard_map.209 = bf16[4,160,1152]{2,1,0:T(8,128)(2,1)} custom-call(bf16[8,208,128]{2,1,0:T(8,128)(2,1)} %all_to_all.31.got_ref, bf16[432,512]{1,0:T(8,128)(2,1)} %constant.84.clone.rows_ref), custom_call_target="tpu_custom_call" | custom-call | tf_op jit(solution)/shard_map/pallas_call | solution.py:304
  36.2 4.4 %all-to-all-start.1 = ((bf16[4,160,1152]{2,1,0:T(8,128)(2,1)}), bf16[4,160,1152]{2,1,0:T(8,128)(2,1)S(1)}, u32[]{:S(2)}, u32[]{:S(2)}) async-start(bf16[4,160,1152]{2,1,0:T(8,128)(2,1)} %shard_map.209), calls=%async_computation.1 | async-start | bytes 2949120 | tf_op jit(solution)/shard_map/all_to_all | solution.py:370
  41.5 17.0 %all-to-all-done.1.own_ref = bf16[4,160,1152]{2,1,0:T(8,128)(2,1)S(1)} async-done(((bf16[4,160,1152]{2,1,0:T(8,128)(2,1)}), bf16[4,160,1152]{2,1,0:T(8,128)(2,1)S(1)}, u32[]{:S(2)}, u32[]{:S(2)}) %all-to-all-start.1) | async-done | bytes 1474592 | tf_op jit(solution)/shard_map/all_to_all | solution.py:370
  58.4 14.3 %all-gather.1 = bf16[32,16,128]{2,1,0:T(8,128)(2,1)} all-gather(bf16[4,16,128]{2,1,0:T(8,128)(2,1)S(1)} %slice.64), channel_id=3, replica_groups={{0,1,64,65,128,129,192,193},{2,3,66,67,130,131,194,195},{4,5,68,69,132,..., dimensions={0}, use_global_device_ids=true | all-gather | bytes 147456 | tf_op jit(solution)/shard_map/all_gather | solution.py:372
  72.8 18.5 %all_to_all.32.got_ref = bf16[8,192,128]{2,1,0:T(8,128)(2,1)} all-to-all(bf16[8,192,128]{2,1,0:T(8,128)(2,1)S(1)} %broadcast_in_dim.35), channel_id=1, replica_groups={{0,8,16,24,32,40,48,56},{1,9,17,25,33,41,49,57},{2,10,18,26,34,42,50,58..., dimensions={0} | all-to-all | bytes 786432 | tf_op jit(solution)/shard_map/all_to_all | solution.py:375
  91.4 2.4 %shard_map.211 = bf16[432,384]{1,0:T(8,128)(2,1)} custom-call(bf16[8,192,128]{2,1,0:T(8,128)(2,1)} %all_to_all.32.got_ref, bf16[144,128]{1,0:T(8,128)(2,1)} %constant.85.clone.rows_ref, bf16[512,384]{1,0:T(8,128)(2,1)} %constant.86.clone.lanes_ref), custom_call_target="tpu_custom_call" | custom-call | tf_op jit(solution)/shard_map/pallas_call | solution.py:304
  93.9 1.8 collective-permute-start.1
  95.8 1.2 collective-permute-done.1
  97.0 3.8 %collective-permute-done = bf16[8,384]{1,0:T(8,128)(2,1)S(1)} collective-permute-done((bf16[8,384]{1,0:T(8,128)(2,1)S(1)}, bf16[8,384]{1,0:T(8,128)(2,1)S(1)}, u32[]{:S(2)}, u32[]{:S(2)}) %collective-permute-start) | collective-permute-done | bytes 6176 | tf_op jit(solution)/shard_map/ppermute | solution.py:357
  101.0 2.0 collective-permute-start.3
  103.0 1.9 collective-permute-done.2
  105.9 10.3 %all-gather.8.cloned.1.call-done = bf16[1728,384]{1,0:T(8,128)(2,1)} async-done(((bf16[432,384]{1,0:T(8,128)(2,1)}), bf16[1728,384]{1,0:T(8,128)(2,1)}) %all-gather.8.cloned.1.call-update) | async-done | bytes 1327120 | tf_op jit(solution)/shard_map/all_gather | solution.py:387
  120.9 25.4 %all-gather.6.cloned.1.call-done = bf16[1728,384]{1,0:T(8,128)(2,1)} async-done(((bf16[432,384]{1,0:T(8,128)(2,1)}), bf16[1728,384]{1,0:T(8,128)(2,1)}) %all-gather.6.cloned.1.call-update) | async-done | bytes 1327120 | tf_op jit(solution)/shard_map/all_gather | solution.py:367
  146.2 1.1 copy-done.1
  147.4 10.8 %shard_map.210 = (f32[4,8,48,128]{3,2,1,0:T(8,128)}, f32[4,8,128]{2,1,0:T(8,128)}, f32[4,8,128]{2,1,0:T(8,128)}, f32[64,256]{1,0:T(8,128)}) custom-call(s32[3]{0:T(128)} %pad_add_fusion.pos_ref, bf16[4,432,384]{2,1,0:T(8,128)(2,1)} %bitcast.33, bf16[4,160,1152]{2,1,0:T(8,128)(2,1)} %copy-done, bf16[4,160,1152]{2,1,0:T(8,128)(2,1)} %copy-done.1, ...), custom_call_target="tpu_custom_call" | custom-call | tf_op jit(solution)/shard_map/pallas_call | solution.py:304
  159.0 0.9 slice_bitcast_fusion
  160.0 1.5 copy.33
  161.6 11.4 %all-to-all-start.2 = ((f32[64,1,256]{2,1,0:T(1,128)}), f32[64,1,256]{2,1,0:T(1,128)S(1)}, u32[]{:S(2)}, u32[]{:S(2)}) async-start(f32[64,1,256]{2,1,0:T(1,128)} %copy.33), calls=%async_computation.2 | async-start | bytes 131072 | tf_op jit(solution)/shard_map/all_to_all | solution.py:429
  173.1 1.5 collective-permute-start.8
  175.8 6.3 %all-to-all-done.2 = f32[64,1,256]{2,1,0:T(1,128)S(1)} async-done(((f32[64,1,256]{2,1,0:T(1,128)}), f32[64,1,256]{2,1,0:T(1,128)S(1)}, u32[]{:S(2)}, u32[]{:S(2)}) %all-to-all-start.2) | async-done | bytes 65568 | tf_op jit(solution)/shard_map/all_to_all | solution.py:429
  183.4 8.9 %shard_map.212 = bf16[4,8,40,384]{3,2,1,0:T(8,128)(2,1)} custom-call(s32[3]{0:T(128)} %pad_add_fusion.pos_ref, f32[4,8,48,128]{3,2,1,0:T(8,128)} %get-tuple-element.18.field_ref, f32[4,8,128]{2,1,0:T(8,128)} %copy-done.9, f32[4,8,128]{2,1,0:T(8,128)} %copy-done.8, f32[4,48,128]{2,1,0:T(8,128)} %copy-done.5, f32[4,48,128]{2,1,0:T(8,128)} %copy-done.6, ...), custom_call_target="tpu_custom_call" | custom-call | tf_op jit(solution)/shard_map/pallas_call | solution.py:304
  192.3 18.7 %all_to_all.33 = bf16[4,8,40,384]{3,2,1,0:T(8,128)(2,1)S(1)} all-to-all(bf16[4,8,40,384]{3,2,1,0:T(8,128)(2,1)} %shard_map.212), channel_id=1, replica_groups=mesh['tm'=4,'space'=64] {'tm'}, dimensions={0} | all-to-all | bytes 1966080 | tf_op jit(solution)/shard_map/all_to_all | solution.py:453
  (85 shorter events, 12.8 us)
Async XLA Ops:
  36.2 22.3 %all-to-all-start.1 = ((bf16[4,160,1152]{2,1,0:T(8,128)(2,1)}), bf16[4,160,1152]{2,1,0:T(8,128)(2,1)S(1)}, u32[]{:S(2)}, u32[]{:S(2)}) async-start(bf16[4,160,1152]{2,1,0:T(8,128)(2,1)} %shard_map.209), calls=%async_computation.1 | async-start | bytes 2949120 | tf_op jit(solution)/shard_map/all_to_all | solution.py:370
  40.6 75.7 %all-gather.8.cloned.1.call-start = ((), (), s32[]{:S(2)}) async-start(), calls=%async_computation.6 | async-start | bytes 1658880 | tf_op jit(solution)/shard_map/all_gather | solution.py:387
  40.7 53.2 %copy-start.10 = (bf16[16,384]{1,0:T(8,128)(2,1)S(1)}, bf16[16,384]{1,0:T(8,128)(2,1)}, u32[]{:S(2)}) copy-start(bf16[16,384]{1,0:T(8,128)(2,1)} %get-tuple-element.15) | copy-start | bytes 36868
  40.7 55.0 %copy-start.4 = (bf16[320,384]{1,0:T(8,128)(2,1)S(1)}, bf16[320,384]{1,0:T(8,128)(2,1)}, u32[]{:S(2)}) copy-start(bf16[320,384]{1,0:T(8,128)(2,1)} %get-tuple-element.14) | copy-start | bytes 737284
  40.7 32.1 %collective-permute-start.5 = (bf16[192,128]{1,0:T(8,128)(2,1)S(1)}, bf16[192,128]{1,0:T(8,128)(2,1)S(1)}, u32[]{:S(2)}, u32[]{:S(2)}) collective-permute-start(bf16[192,128]{1,0:T(8,128)(2,1)S(1)} %bitcast.41), channel_id=1, source_target_pairs={{0,0},{1,1},{2,2},{3,3},{4,4},{5,5},{6,6},{7,7},{8,8},{9,9},{10,10... | collective-permute-start | bytes 147464 | tf_op jit(solution)/shard_map/ppermute | solution.py:345
  58.4 47.4 %copy-start = (bf16[4,160,1152]{2,1,0:T(8,128)(2,1)}, bf16[4,160,1152]{2,1,0:T(8,128)(2,1)S(1)}, u32[]{:S(2)}) copy-start(bf16[4,160,1152]{2,1,0:T(8,128)(2,1)S(1)} %all-to-all-done.1.own_ref) | copy-start | bytes 4423684
  91.4 24.9 %copy-start.12 = (f32[384]{0:T(512)S(1)}, f32[384]{0:T(512)}, u32[]{:S(2)}) copy-start(f32[384]{0:T(512)} %param.23) | copy-start | bytes 4612
  91.4 25.5 %copy-start.13 = (f32[384]{0:T(512)S(1)}, f32[384]{0:T(512)}, u32[]{:S(2)}) copy-start(f32[384]{0:T(512)} %param.24) | copy-start | bytes 4612
  93.8 52.4 %all-gather.6.cloned.1.call-start = ((), (), s32[]{:S(2)}) async-start(), calls=%async_computation.5 | async-start | bytes 1658880 | tf_op jit(solution)/shard_map/all_gather | solution.py:367
  93.9 3.1 %collective-permute-start.1 = (bf16[8,384]{1,0:T(8,128)(2,1)S(1)}, bf16[8,384]{1,0:T(8,128)(2,1)S(1)}, u32[]{:S(2)}, u32[]{:S(2)}) collective-permute-start(bf16[8,384]{1,0:T(8,128)(2,1)S(1)} %get-tuple-element.31), channel_id=1, source_target_pairs={{0,63},{1,0},{2,1},{3,2},{4,3},{5,4},{6,5},{7,6},{8,7},{9,8},{10,9... | collective-permute-start | bytes 18440 | tf_op jit(solution)/shard_map/ppermute | solution.py:358
  95.7 5.2 %collective-permute-start = (bf16[8,384]{1,0:T(8,128)(2,1)S(1)}, bf16[8,384]{1,0:T(8,128)(2,1)S(1)}, u32[]{:S(2)}, u32[]{:S(2)}) collective-permute-start(bf16[8,384]{1,0:T(8,128)(2,1)S(1)} %get-tuple-element.32), channel_id=1, source_target_pairs={{0,1},{1,2},{2,3},{3,4},{4,5},{5,6},{6,7},{7,8},{8,9},{9,10},{10,1... | collective-permute-start | bytes 18440 | tf_op jit(solution)/shard_map/ppermute | solution.py:357
  100.9 4.0 %collective-permute-start.2 = (bf16[48,384]{1,0:T(8,128)(2,1)S(1)}, bf16[48,384]{1,0:T(8,128)(2,1)S(1)}, u32[]{:S(2)}, u32[]{:S(2)}) collective-permute-start(bf16[48,384]{1,0:T(8,128)(2,1)S(1)} %get-tuple-element.40), channel_id=1, source_target_pairs={{0,8},{1,9},{2,10},{3,11},{4,12},{5,13},{6,14},{7,15},{8,16},{9,17... | collective-permute-start | bytes 110600 | tf_op jit(solution)/shard_map/ppermute | solution.py:364
  101.0 4.0 %collective-permute-start.3 = (bf16[48,384]{1,0:T(8,128)(2,1)S(1)}, bf16[48,384]{1,0:T(8,128)(2,1)S(1)}, u32[]{:S(2)}, u32[]{:S(2)}) collective-permute-start(bf16[48,384]{1,0:T(8,128)(2,1)S(1)} %get-tuple-element.39), channel_id=1, source_target_pairs={{0,56},{1,57},{2,58},{3,59},{4,60},{5,61},{6,62},{7,63},{8,0},{9,1... | collective-permute-start | bytes 110600 | tf_op jit(solution)/shard_map/ppermute | solution.py:365
  105.8 40.4 %collective-permute-start.4 = (bf16[4,160,1152]{2,1,0:T(8,128)(2,1)S(1)}, bf16[4,160,1152]{2,1,0:T(8,128)(2,1)S(1)}, u32[]{:S(2)}, u32[]{:S(2)}) collective-permute-start(bf16[4,160,1152]{2,1,0:T(8,128)(2,1)S(1)} %all-to-all-done.1.own_ref), channel_id=1, source_target_pairs={{0,1},{1,0},{2,3},{3,2},{4,5},{5,4},{6,7},{7,6},{8,9},{9,8},{10,11... | collective-permute-start | bytes 4423688 | tf_op jit(solution)/shard_map/ppermute | solution.py:371
  116.2 66.5 %collective-permute-start.10 = (bf16[4,432,384]{2,1,0:T(8,128)(2,1)}, bf16[4,432,384]{2,1,0:T(8,128)(2,1)}, u32[]{:S(2)}, u32[]{:S(2)}) collective-permute-start(bf16[4,432,384]{2,1,0:T(8,128)(2,1)} %bitcast.31), channel_id=1, source_target_pairs={{0,1},{1,0},{2,3},{3,2},{4,5},{5,4},{6,7},{7,6},{8,9},{9,8},{10,11... | collective-permute-start | bytes 3981320 | tf_op jit(solution)/shard_map/ppermute | solution.py:388
  158.2 14.8 %collective-permute-start.7 = (f32[4,8,128]{2,1,0:T(8,128)}, f32[4,8,128]{2,1,0:T(8,128)S(1)}, u32[]{:S(2)}, u32[]{:S(2)}) collective-permute-start(f32[4,8,128]{2,1,0:T(8,128)} %get-tuple-element.20), channel_id=1, source_target_pairs={{0,63},{1,0},{2,1},{3,2},{4,3},{5,4},{6,5},{7,6},{8,7},{9,8},{10,9... | collective-permute-start | bytes 49160 | tf_op jit(solution)/shard_map/ppermute | solution.py:422
  159.9 13.1 %collective-permute-start.6 = (f32[4,8,128]{2,1,0:T(8,128)}, f32[4,8,128]{2,1,0:T(8,128)S(1)}, u32[]{:S(2)}, u32[]{:S(2)}) collective-permute-start(f32[4,8,128]{2,1,0:T(8,128)} %get-tuple-element.19), channel_id=1, source_target_pairs={{0,1},{1,2},{2,3},{3,4},{4,5},{5,6},{6,7},{7,8},{8,9},{9,10},{10,1... | collective-permute-start | bytes 49160 | tf_op jit(solution)/shard_map/ppermute | solution.py:421
  161.6 20.6 %all-to-all-start.2 = ((f32[64,1,256]{2,1,0:T(1,128)}), f32[64,1,256]{2,1,0:T(1,128)S(1)}, u32[]{:S(2)}, u32[]{:S(2)}) async-start(f32[64,1,256]{2,1,0:T(1,128)} %copy.33), calls=%async_computation.2 | async-start | bytes 131072 | tf_op jit(solution)/shard_map/all_to_all | solution.py:429
  173.0 9.8 %copy-start.8 = (f32[4,8,128]{2,1,0:T(8,128)}, f32[4,8,128]{2,1,0:T(8,128)S(1)}, u32[]{:S(2)}) copy-start(f32[4,8,128]{2,1,0:T(8,128)S(1)} %collective-permute-done.7.east_ref) | copy-start | bytes 49156
  173.0 9.8 %copy-start.9 = (f32[4,8,128]{2,1,0:T(8,128)}, f32[4,8,128]{2,1,0:T(8,128)S(1)}, u32[]{:S(2)}) copy-start(f32[4,8,128]{2,1,0:T(8,128)S(1)} %collective-permute-done.6.west_ref) | copy-start | bytes 49156
  173.1 9.6 %collective-permute-start.8 = (f32[4,48,128]{2,1,0:T(8,128)S(1)}, f32[4,48,128]{2,1,0:T(8,128)S(1)}, u32[]{:S(2)}, u32[]{:S(2)}) collective-permute-start(f32[4,48,128]{2,1,0:T(8,128)S(1)} %get-tuple-element.38), channel_id=1, source_target_pairs={{0,8},{1,9},{2,10},{3,11},{4,12},{5,13},{6,14},{7,15},{8,16},{9,17... | collective-permute-start | bytes 294920 | tf_op jit(solution)/shard_map/ppermute | solution.py:423
  174.7 8.1 %collective-permute-start.9 = (f32[4,48,128]{2,1,0:T(8,128)S(1)}, f32[4,48,128]{2,1,0:T(8,128)S(1)}, u32[]{:S(2)}, u32[]{:S(2)}) collective-permute-start(f32[4,48,128]{2,1,0:T(8,128)S(1)} %get-tuple-element.37), channel_id=1, source_target_pairs={{0,56},{1,57},{2,58},{3,59},{4,60},{5,61},{6,62},{7,63},{8,0},{9,1... | collective-permute-start | bytes 294920 | tf_op jit(solution)/shard_map/ppermute | solution.py:426
  192.3 18.9 %copy-start.3 = (bf16[1,1,8,40,384]{4,3,2,1,0:T(8,128)(2,1)S(1)}, bf16[1,1,8,40,384]{4,3,2,1,0:T(8,128)(2,1)}, u32[]{:S(2)}) copy-start(bf16[1,1,8,40,384]{4,3,2,1,0:T(8,128)(2,1)} %param.22) | copy-start | bytes 737284
  192.3 18.9 %copy-start.11 = (f32[384]{0:T(512)S(1)}, f32[384]{0:T(512)}, u32[]{:S(2)}) copy-start(f32[384]{0:T(512)} %param.30) | copy-start | bytes 4612
  (5 other events, 7.6 us)
Sparse Core Ops, SparseCore 0:
  93.9 22.2 all-gather.7
  118.0 28.1 all-gather.5

commit v2 on v1

v2 whole, which is shorter than its diff:
```python
import functools

import jax
import jax.numpy as jnp
import numpy as np
from jax import lax
from jax.experimental import pallas as pl
from jax.experimental.pallas import tpu as pltpu
from jax.sharding import PartitionSpec as P

EPS = 1e-06
BF = jnp.bfloat16
F32 = jnp.float32
VM = pl.BlockSpec(memory_space=pltpu.VMEM)
SM = pl.BlockSpec(memory_space=pltpu.SMEM)
HIGH = lax.Precision.HIGHEST

NZ, NX, NC, NY = 8, 4, 2, 4
COLS = NX * NC
SPACE = NZ * COLS
ROWS, WIDE, PITCH = 8, 40, 48
CH, PART, WG = 384, 96, 12
FLAT = (ROWS + 2) * PITCH
GUARD = 16
BOTH = ("tm", "space")
ALONG_Z = [[z * COLS + q for z in range(NZ)] for q in range(COLS)]
ALONG_X = [[z * COLS + x * NC + c for x in range(NX)] for z in range(NZ) for c in range(NC)]
Y_CORE = [
    [y * SPACE + z * COLS + x * NC + c for y in range(NY) for c in range(NC)]
    for z in range(NZ)
    for x in range(NX)
]
SIBLING = [(s, s ^ 1) for s in range(SPACE)]


def moved(down, right):
    return [(s, (s + COLS * down + right) % SPACE) for s in range(SPACE)]


SWAP = [
    (y * SPACE + z * COLS + q, (z // 2) * SPACE + (2 * y + z % 2) * COLS + q)
    for y in range(NY)
    for z in range(NZ)
    for q in range(COLS)
]


def one_hot(rows, cols, pairs):
    out = np.zeros((rows, cols), np.float32)
    for r, c in pairs:
        out[r, c] = 1.0
    return out


CHANNEL_LANES = one_hot(
    CH, CH, [(6 * (8 * z + q) + i, 48 * q + 6 * z + i) for z in range(8) for q in range(8) for i in range(6)]
)
GROUPS_OF = one_hot(CH, 128, [(c, c // WG) for c in range(CH)])
SQUARES_OF = np.roll(GROUPS_OF, 64, axis=1)
GROUPS_OF_LANES = (CHANNEL_LANES.T @ GROUPS_OF).T
SQUARES_OF_LANES = (CHANNEL_LANES.T @ SQUARES_OF).T
PART_GROUPS = one_hot(128, 128, [(c, c // WG) for c in range(PART)])
PART_SQUARES = np.roll(PART_GROUPS, 64, axis=1)
CORNERS = ((0, 0), (0, WIDE - 1), (ROWS - 1, 0), (ROWS - 1, WIDE - 1))
EDGES = one_hot(
    48,
    320,
    [(r, 40 * r) for r in range(8)]
    + [(8 + r, 40 * r + 39) for r in range(8)]
    + [(16 + 8 * n, 40 * r + c) for n, (r, c) in enumerate(CORNERS)],
)
FIRST_ROWS = one_hot(
    432, 512, [(48 * k + 6 * z + i, 64 * z + 6 * k + i) for k in range(9) for z in range(8) for i in range(6)]
)
SECOND_ROWS = one_hot(
    144, 128, [(16 * k + 6 * h + i, 64 * h + 6 * k + i) for k in range(9) for h in range(2) for i in range(6)]
)
SECOND_LANES = one_hot(512, CH, [(128 * y + o, PART * y + o) for y in range(4) for o in range(PART)])
PART_LANES = one_hot(
    128, 128, [(48 * h + 6 * q + i, 16 * q + 6 * h + i) for h in range(2) for q in range(8) for i in range(6)]
)


def dot(a, b):
    return jnp.dot(a, b, preferred_element_type=F32)


def exact(a, b):
    return jnp.dot(a, b, preferred_element_type=F32, precision=HIGH)


def merge(sums, count, groups_t, squares_t):
    mean = jnp.mean(sums, axis=0, keepdims=True)
    off = sums - mean
    between = count * jnp.sum(off * off, axis=0, keepdims=True)
    within = jnp.sum(sums, axis=0, keepdims=True)
    rows = jnp.concatenate([mean, between, jnp.zeros((6, 128), F32)], axis=0)
    by_lane = exact(rows, groups_t)
    spread = (by_lane[1:2] + exact(tall(within), squares_t)[0:1]) * (1.0 / (count * sums.shape[0]))
    return by_lane[0:1], lax.rsqrt(spread + EPS)


def split_rows(row):
    hi = row.astype(BF).astype(F32)
    mid = (row - hi).astype(BF).astype(F32)
    return jnp.concatenate([hi, mid, row - hi - mid, jnp.zeros((13, 128), F32)], axis=0).astype(BF)


def pool(blocks, count):
    wide = [b.astype(F32) for b in blocks]
    rows = jnp.concatenate([b[0:1] + b[1:2] + b[2:3] for b in wide], axis=0)
    mean = jnp.mean(rows, axis=0, keepdims=True)
    off = rows - mean
    between = count * jnp.sum(off * off, axis=0, keepdims=True)
    squares = jnp.sum(rows, axis=0, keepdims=True) + pltpu.roll(tall(between), 64, axis=1)[0:1]
    return jnp.where(lax.broadcasted_iota(jnp.int32, (1, 128), 1) < 64, mean, squares)


def tall(row):
    return jnp.broadcast_to(row, (8, row.shape[1]))


def chosen(part):
    channel = lax.broadcasted_iota(jnp.int32, (CH, 128), 0)
    lane = lax.broadcasted_iota(jnp.int32, (CH, 128), 1)
    return ((channel == part * PART + lane) & (lane < PART)).astype(F32)


def silu(u):
    return u / (1.0 + jnp.exp(-u))


def measure_tile(
    tile_ref, lanes_ref, groups_ref, groups_t_ref, squares_ref, edges_ref,
    placed_ref, west_ref, east_ref, nw_ref, ne_ref, sw_ref, se_ref, sums_ref,
):
    tile = tile_ref[...]
    placed = dot(tile, lanes_ref[...]).astype(BF)
    placed_ref[...] = placed
    edges = dot(edges_ref[...], placed).astype(BF)
    for n, ref in enumerate((west_ref, east_ref, nw_ref, ne_ref, sw_ref, se_ref)):
        ref[...] = edges[8 * n : 8 * n + 8]
    wide = tile.astype(F32)
    mean = exact(tall(jnp.sum(wide, axis=0, keepdims=True)), groups_ref[...]) * (1.0 / (320 * WG))
    off = wide - exact(mean, groups_t_ref[...])[0:1]
    squares = exact(tall(jnp.sum(off * off, axis=0, keepdims=True)), squares_ref[...])
    sums_ref[...] = split_rows((mean + squares)[0:1])


def gather_sums(own_ref, out_ref):
    out_ref[...] = tall(pool([own_ref[x] for x in range(NX)], 320.0 * WG * NZ))


def arrange_first(got_ref, rows_ref, out_ref):
    parts = [
        jnp.concatenate([got_ref[z, 64 * d : 64 * d + 64, :] for z in range(NZ)], axis=0) for d in range(3)
    ]
    ordered = dot(rows_ref[...], jnp.concatenate(parts, axis=1)).astype(BF)
    sums = split_rows(pool([got_ref[z, 384:400, :] for z in range(NZ)], 320.0 * WG))
    for copy in range(NX):
        out_ref[copy, 144:160, 0:128] = sums
        out_ref[copy, 144:160, 128:] = jnp.zeros((16, 1024), BF)
        for d in range(3):
            for k in range(9):
                out_ref[copy, 48 * d : 48 * d + 48, 128 * k : 128 * k + 128] = ordered[
                    48 * k : 48 * k + 48, 128 * d : 128 * d + 128
                ]


def arrange_second(got_ref, rows_ref, lanes_ref, out_ref):
    by_part = []
    for y in range(NY):
        parts = [
            jnp.concatenate([got_ref[2 * y + h, 192 + 64 * d : 256 + 64 * d, :] for h in range(2)], axis=0)
            for d in range(3)
        ]
        by_part.append(dot(rows_ref[...], jnp.concatenate(parts, axis=1)).astype(BF))
    tall_parts = [
        jnp.concatenate([by_part[y][:, 128 * d : 128 * d + 128] for y in range(NY)], axis=1) for d in range(3)
    ]
    out_ref[...] = dot(jnp.concatenate(tall_parts, axis=0), lanes_ref[...]).astype(BF)


def first_act(
    pos_ref, lat_ref, sums_ref, vectors_ref, lanes_ref, groups_t_ref, squares_t_ref, stack, flat
):
    row, col = pos_ref[0] // COLS, pos_ref[0] % COLS
    mean_l, scale_l = merge(sums_ref[...], 320.0 * WG * NZ * NX, groups_t_ref[...], squares_t_ref[...])
    affine = exact(vectors_ref[...], lanes_ref[...])
    scale_l = scale_l * affine[0:1]
    shift_l = affine[1:2]
    has_w = (col > 0).astype(F32)
    has_e = (col < COLS - 1).astype(F32)
    has_n = (row > 0).astype(F32)
    has_s = (row < NZ - 1).astype(F32)
    flat[...] = jnp.zeros_like(flat)
    for t in range(NY):
        act = silu((lat_ref[t].astype(F32) - mean_l) * scale_l + shift_l)
        base = GUARD
        flat[base : base + WIDE, :] = act[336:376] * has_n
        flat[base - 1 : base, :] = act[416:417] * (has_n * has_w)
        flat[base + WIDE : base + WIDE + 1, :] = act[424:425] * (has_n * has_e)
        for r in range(ROWS):
            base = GUARD + PITCH * (r + 1)
            flat[base : base + WIDE, :] = act[WIDE * r : WIDE * r + WIDE]
            flat[base + WIDE : base + WIDE + 1, :] = act[328 + r : 329 + r] * has_e
            flat[base - 1 : base, :] = act[320 + r : 321 + r] * has_w
        base = GUARD + PITCH * (ROWS + 1)
        flat[base : base + WIDE, :] = act[376:416] * has_s
        flat[base - 1 : base, :] = act[432:433] * (has_s * has_w)
        flat[base + WIDE : base + WIDE + 1, :] = act[440:441] * (has_s * has_e)
        for d in range(3):
            stack[t, :, CH * d : CH * d + CH] = flat[GUARD + d - 1 : GUARD + d - 1 + FLAT, :].astype(BF)


def first_conv(
    pos_ref, stack, own_ref, other_ref, vectors_ref, part_ref, part_t_ref, part_squares_ref,
    out_ref, west_ref, east_ref, north_ref, south_ref, nw_ref, ne_ref, sw_ref, se_ref, sums_ref, weights,
):
    core = pos_ref[0] % NC
    bias = exact(vectors_ref[...], chosen(pos_ref[1]))[2:3]
    for mine in range(NC):

        @pl.when(core == mine)
        def _():
            for x in range(NX):
                for d in range(3):
                    at = CH * d + 48 * (NC * x + mine)
                    weights[at : at + 48, :] = own_ref[x, 48 * d : 48 * d + 48, :]
                    at = CH * d + 48 * (NC * x + 1 - mine)
                    weights[at : at + 48, :] = other_ref[x, 48 * d : 48 * d + 48, :]

    totals = [None] * NY
    for t in range(NY):
        for dt in range(3):
            to = t + 2 - dt
            if to >= NY:
                continue
            part = dot(stack[t], weights[:, CH * dt : CH * dt + CH])
            term = part[0:384, 0:128] + part[48:432, 128:256] + part[96:480, 256:384]
            totals[to] = term if totals[to] is None else totals[to] + term
    inside = (lax.broadcasted_iota(jnp.int32, (384, 1), 0) % PITCH < WIDE).astype(F32)
    sums = None
    for t in range(NY):
        totals[t] = totals[t] + bias
        line = jnp.sum(totals[t] * inside, axis=0, keepdims=True)
        sums = line if sums is None else sums + line
        for r in range(ROWS):
            out_ref[t, r] = totals[t][PITCH * r : PITCH * r + PITCH]
            west_ref[t, r : r + 1, :] = totals[t][PITCH * r : PITCH * r + 1]
            east_ref[t, r : r + 1, :] = totals[t][PITCH * r + WIDE - 1 : PITCH * r + WIDE]
        north_ref[t] = totals[t][0:WIDE]
        south_ref[t] = totals[t][PITCH * (ROWS - 1) : PITCH * (ROWS - 1) + WIDE]
        for ref, (r, c) in zip((nw_ref, ne_ref, sw_ref, se_ref), CORNERS):
            ref[t : t + 1, :] = totals[t][PITCH * r + c : PITCH * r + c + 1]
    mean = exact(tall(sums), part_ref[...]) * (1.0 / (320 * NY * WG))
    mean_l = exact(mean, part_t_ref[...])[0:1]
    sums = None
    for t in range(NY):
        off = (totals[t] - mean_l) * inside
        line = jnp.sum(off * off, axis=0, keepdims=True)
        sums = line if sums is None else sums + line
    squares = exact(tall(sums), part_squares_ref[...])
    sums_ref[...] = jnp.broadcast_to((mean + squares)[0:1], (SPACE, 128))


def assemble_second(pos_ref, own_ref, other_ref, weights):
    core = pos_ref[0] % NC
    for mine in range(NC):

        @pl.when(core == mine)
        def _():
            for x in range(NX):
                for d in range(3):
                    for k in range(9):
                        tap = 9 * (k // 3) + 3 * (k % 3) + d
                        source = 144 * d + 16 * k
                        at = 128 * tap + 16 * (NC * x + mine)
                        weights[at : at + 16, :] = own_ref[x, source : source + 16, :]
                        at = 128 * tap + 16 * (NC * x + 1 - mine)
                        weights[at : at + 16, :] = other_ref[x, source : source + 16, :]


def second_conv(
    pos_ref, field_ref, west_ref, east_ref, north_ref, south_ref, nw_ref, ne_ref, sw_ref, se_ref, sums_ref,
    vectors_ref, weights,
    groups_t_ref, squares_t_ref, order_ref, out_ref, flat, stack,
):
    row, col = pos_ref[0] // COLS, pos_ref[0] % COLS
    mean_l, scale_l = merge(sums_ref[...], 320.0 * NY * WG, groups_t_ref[...], squares_t_ref[...])
    affine = exact(vectors_ref[...], chosen(pos_ref[1]))
    scale_l = scale_l * affine[3:4]
    shift_l = affine[4:5]

    def act_of(v):
        act = silu((v - mean_l) * scale_l + shift_l).astype(BF)
        return dot(act, order_ref[...])

    has_w = (col > 0).astype(F32)
    has_e = (col < COLS - 1).astype(F32)
    has_n = (row > 0).astype(F32)
    has_s = (row < NZ - 1).astype(F32)
    flat[...] = jnp.zeros_like(flat)
    nw, ne = act_of(nw_ref[...]) * (has_n * has_w), act_of(ne_ref[...]) * (has_n * has_e)
    sw, se = act_of(sw_ref[...]) * (has_s * has_w), act_of(se_ref[...]) * (has_s * has_e)
    for t in range(NY):
        left, right = act_of(west_ref[t]) * has_w, act_of(east_ref[t]) * has_e
        base = GUARD
        flat[base : base + WIDE, :] = act_of(north_ref[t]) * has_n
        flat[base - 1 : base, :] = nw[t : t + 1]
        flat[base + WIDE : base + WIDE + 1, :] = ne[t : t + 1]
        for r in range(ROWS):
            base = GUARD + PITCH * (r + 1)
            flat[base : base + WIDE, :] = act_of(field_ref[t, r])[0:WIDE]
            flat[base + WIDE : base + WIDE + 1, :] = right[r : r + 1]
            flat[base - 1 : base, :] = left[r : r + 1]
        base = GUARD + PITCH * (ROWS + 1)
        flat[base : base + WIDE, :] = act_of(south_ref[t]) * has_s
        flat[base - 1 : base, :] = sw[t : t + 1]
        flat[base + WIDE : base + WIDE + 1, :] = se[t : t + 1]
        for dy in range(3):
            for dx in range(3):
                start = GUARD + PITCH * dy + dx - 1
                lane = 128 * (3 * dy + dx)
                stack[t, :, lane : lane + 128] = flat[start : start + 384, :].astype(BF)
    for t in range(NY):
        total = None
        for dt in range(3):
            source = t - 2 + dt
            if source < 0:
                continue
            term = dot(stack[source], weights[1152 * dt : 1152 * dt + 1152, :])
            total = term if total is None else total + term
        for r in range(ROWS):
            out_ref[t, r] = total[PITCH * r : PITCH * r + WIDE].astype(BF)


def call(body, outs, scratch, smem, *args):
    return pl.pallas_call(
        body,
        out_shape=outs,
        in_specs=[SM] * smem + [VM] * (len(args) - smem),
        out_specs=jax.tree.map(lambda _: VM, outs),
        scratch_shapes=scratch,
        compiler_params=pltpu.CompilerParams(vmem_limit_bytes=56 * 1024 * 1024),
    )(*args)


def shape(dims, dtype):
    return jax.ShapeDtypeStruct(dims, dtype)


def neighbours(west, east, north, south, nw, ne, sw, se):
    send = functools.partial(lax.ppermute, axis_name="space")
    return (
        send(east, perm=moved(0, 1)),
        send(west, perm=moved(0, -1)),
        send(south, perm=moved(1, 0)),
        send(north, perm=moved(-1, 0)),
        send(se, perm=moved(1, 1)),
        send(sw, perm=moved(1, -1)),
        send(ne, perm=moved(-1, 1)),
        send(nw, perm=moved(-1, -1)),
    )


def by_column(kernel):
    rows = jnp.transpose(kernel, (2, 0, 1, 3, 4)).reshape(3, 54, PART)
    return jnp.pad(rows, ((0, 0), (0, 10), (0, 32))).reshape(192, 128)


def shards(
    latents,
    gain_first,
    shift_first,
    kernel_first,
    bias_first,
    gain_second,
    shift_second,
    kernel_second,
    bias_second,
):
    space = lax.axis_index("space")
    frame = lax.axis_index("tm")
    pos = jnp.stack([space, frame]).astype(jnp.int32)
    vectors = jnp.stack(
        [gain_first, shift_first, bias_first, gain_second, shift_second, bias_second, bias_second, bias_second]
    )
    tile = latents[0, 0]
    flat_tile = tile.reshape(ROWS * WIDE, CH)

    swapped = lax.ppermute(by_column(kernel_second), BOTH, SWAP)
    small = shape((8, CH), BF)
    placed, west, east, nw, ne, sw, se, sums = call(
        measure_tile,
        (shape((320, CH), BF), small, small, small, small, small, small, shape((16, 128), BF)),
        [],
        0,
        flat_tile,
        jnp.asarray(CHANNEL_LANES, BF),
        jnp.asarray(GROUPS_OF),
        jnp.asarray(GROUPS_OF.T),
        jnp.asarray(SQUARES_OF),
        jnp.asarray(EDGES, BF),
    )
    letter = jnp.concatenate([by_column(kernel_first), swapped, sums], axis=0)
    got = lax.all_to_all(
        jnp.broadcast_to(letter[None], (NZ, 400, 128)), "space", 0, 0, tiled=True, axis_index_groups=ALONG_Z
    )
    around = neighbours(west, east, placed[0:40], placed[280:320], nw, ne, sw, se)
    parcel = jnp.concatenate([placed, *around], axis=0)
    frames = lax.all_gather(parcel, "tm")
    got, _ = lax.optimization_barrier((got, parcel))

    ordered = call(arrange_first, shape((NX, 160, 1152), BF), [], 0, got, jnp.asarray(FIRST_ROWS, BF))
    own = lax.all_to_all(ordered, "space", 0, 0, tiled=True, axis_index_groups=ALONG_X)
    x_sums = pl.pallas_call(
        gather_sums,
        grid=(1,),
        in_specs=[pl.BlockSpec((NX, 16, 128), lambda i: (0, 9, 0))],
        out_specs=pl.BlockSpec((8, 128), lambda i: (0, 0)),
        out_shape=shape((8, 128), F32),
    )(own)
    all_sums = lax.all_to_all(x_sums, BOTH, 0, 0, tiled=True, axis_index_groups=Y_CORE)
    got_second, _ = lax.optimization_barrier((got, own))
    stack = call(
        first_act,
        shape((NY, FLAT, 3 * CH), BF),
        [pltpu.VMEM((GUARD + FLAT + GUARD, CH), F32)],
        1,
        pos,
        frames,
        all_sums,
        vectors,
        jnp.asarray(CHANNEL_LANES),
        jnp.asarray(GROUPS_OF_LANES),
        jnp.asarray(SQUARES_OF_LANES),
    )
    other = lax.ppermute(own, "space", SIBLING)

    ordered_second = call(
        arrange_second,
        shape((432, CH), BF),
        [],
        0,
        got_second,
        jnp.asarray(SECOND_ROWS, BF),
        jnp.asarray(SECOND_LANES, BF),
    )
    stack, _ = lax.optimization_barrier((stack, ordered_second))
    cells = shape((8, 128), F32)
    field, *edges, sums = call(
        first_conv,
        (
            shape((NY, ROWS, PITCH, 128), F32),
            shape((NY, ROWS, 128), F32),
            shape((NY, ROWS, 128), F32),
            shape((NY, WIDE, 128), F32),
            shape((NY, WIDE, 128), F32),
            cells,
            cells,
            cells,
            cells,
            shape((SPACE, 128), F32),
        ),
        [pltpu.VMEM((3 * CH, 9 * 128), BF)],
        1,
        pos,
        stack,
        own,
        other,
        vectors,
        jnp.asarray(PART_GROUPS),
        jnp.asarray(PART_GROUPS.T),
        jnp.asarray(PART_SQUARES),
    )
    around = neighbours(*edges)
    own_second = lax.all_gather(ordered_second, "space", axis_index_groups=ALONG_X)
    own_second, _ = lax.optimization_barrier((own_second, around[0]))
    other_second = lax.ppermute(own_second, "space", SIBLING)
    weights_second = call(assemble_second, shape((27 * 128, CH), BF), [], 1, pos, own_second, other_second)
    all_sums = lax.all_to_all(sums, "space", 0, 0, tiled=True)
    partial = call(
        second_conv,
        shape((NY, ROWS, WIDE, CH), BF),
        [
            pltpu.VMEM((GUARD + FLAT + GUARD, 128), F32),
            pltpu.VMEM((NY, 384, 9 * 128), BF),
        ],
        1,
        pos,
        field,
        *around,
        all_sums,
        vectors,
        weights_second,
        jnp.asarray(PART_GROUPS.T),
        jnp.asarray(PART_SQUARES.T),
        jnp.asarray(PART_LANES, BF),
    )
    parts = lax.all_to_all(partial, "tm", 0, 0, tiled=True)
    second_out = jnp.sum(parts.astype(F32), axis=0) + bias_second
    return (tile.astype(F32) + second_out).astype(BF)[None, None]


def solution(mesh):
    placed = (
        P("tm", "space", None, None, None),
        P(),
        P(),
        P(None, None, None, "space", "tm"),
        P(),
        P(),
        P(),
        P(None, None, None, "space", "tm"),
        P(),
    )
    return jax.shard_map(
        shards,
        mesh=mesh,
        in_specs=placed,
        out_specs=P("tm", "space", None, None, None),
        check_vma=False,
    )
```

time: 221 us -> 202 us (0.914)
  blocking collectives: 74 us -> 40 us
  starting transfers between devices: 23.7 us -> 56.8 us
  waiting for transfers between devices: 66 us -> 41.5 us
  Pallas kernels: 27.7 us -> 39.8 us
  local copies, waits for them, and re-layouts: 11.4 us -> 7.62 us
    ppermute x8 -> x16, starting transfers between devices: 6.89 us -> 36.1 us  [the longest x2 15.9 us: neighbours(): send(nw, perm=moved(-1, -1))]
    all_gather x1, waiting for transfers between devices: 25.4 us -> 0.01 us  [shards(): frames = lax.all_gather(parcel, 'tm')]
    all_to_all x2 -> x1, blocking collectives: 40.9 us -> 22.1 us  [shards(): lax.all_to_all(ordered, 'space', 0, 0, tiled=True, axis_index_groups=ALON...]
    all_gather x1 -> x0, blocking collectives: 14.3 us -> none  [shards(): lax.all_gather(own[:, 144:160, 0:128], BOTH, axis_index_groups=Y_CORE)]
    pallas_call x5 -> x7, Pallas kernels: 27.7 us -> 38.4 us  [call(): pl.pallas_call(body, out_shape=outs, in_specs=[SM] * smem + [VM] * (len(a...]
    all_gather x1, waiting for transfers between devices: 10.3 us -> 0.01 us  [shards(): lax.all_gather(ordered_second, 'space', axis_index_groups=ALONG_X)]
    ppermute x8 -> x16, waiting for transfers between devices: 7.02 us -> 16.2 us  [the longest x2 7.46 us: neighbours(): send(se, perm=moved(1, 1))]
    all_to_all x1 -> x2, waiting for transfers between devices: 17 us -> 25.2 us  [the longest x1 21.4 us: shards(): lax.all_to_all(jnp.broadcast_to(letter[None], (NZ, 400, 128)), 'space', 0...]
  transfers between devices with their start and end apart: 15 -> 24, of which waited for: 8 -> 5; matrix products, arithmetic and copies ran while one was open for 4% -> 2% of each run, Pallas kernels for 5% -> 14%
where the time goes in v2:
time: 202 us
  starting transfers between devices  56.8 us (28%)
  waiting for transfers between devices  41.5 us (21%)
  blocking collectives  40 us (20%)
  Pallas kernels  39.8 us (20%)
  between operations  13.8 us (7%)
  local copies, waits for them, and re-layouts  7.62 us (4%)
  other arithmetic  2.18 us (1%)
    pallas_call x7, Pallas kernels, call(): pl.pallas_call(body, out_shape=outs, in_specs=[SM] * smem + [VM] * (len(a...  38.4 us
    all_to_all x1, blocking collectives, shards(): lax.all_to_all(ordered, 'space', 0, 0, tiled=True, axis_index_groups=ALON...  22.1 us
    all_to_all x1, waiting for transfers between devices, shards(): lax.all_to_all(jnp.broadcast_to(letter[None], (NZ, 400, 128)), 'space', 0...  21.4 us
    all_to_all x1, blocking collectives, shards(): parts = lax.all_to_all(partial, 'tm', 0, 0, tiled=True)  17.8 us
    ppermute x2, starting transfers between devices, neighbours(): send(nw, perm=moved(-1, -1))  15.9 us
    ppermute x2, waiting for transfers between devices, neighbours(): send(se, perm=moved(1, 1))  7.46 us
    all_to_all x1, starting transfers between devices, shards(): all_sums = lax.all_to_all(sums, 'space', 0, 0, tiled=True)  7.4 us
    all_to_all x1, starting transfers between devices, shards(): lax.all_to_all(jnp.broadcast_to(letter[None], (NZ, 400, 128)), 'space', 0...  7.01 us
  transfers between devices with their start and end apart: 24, of which 5 were waited for; matrix products, arithmetic and copies ran while one was open for 2% of the time, Pallas kernels for 14%

profile of v2, /device:TPU:32, one launch (start us, length us, event | category | flops | bytes accessed | tf_op | source)
XLA Modules:
  0.0 201.7 jit_solution(16587434160260882270)
XLA Ops:
  6.5 3.1 %shard_map.244 = (bf16[320,384]{1,0:T(8,128)(2,1)}, bf16[8,384]{1,0:T(8,128)(2,1)}, bf16[8,384]{1,0:T(8,128)(2,1)}, bf16[8,384]{1,0:T(8,128)(2,1)}, bf16[8,384]{...) custom-call(bf16[320,384]{1,0:T(8,128)(2,1)} %bitcast.26, ...), custom_call_target="tpu_custom_call" | custom-call | tf_op jit(solution)/shard_map/pallas_call | solution.py:339
  9.6 3.9 %collective-permute-start.1 = (bf16[8,384]{1,0:T(8,128)(2,1)}, bf16[8,384]{1,0:T(8,128)(2,1)S(1)}, u32[]{:S(2)}, u32[]{:S(2)}) collective-permute-start(bf16[8,384]{1,0:T(8,128)(2,1)} %get-tuple-element.29), channel_id=1, source_target_pairs={{0,63},{1,0},{2,1},{3,2},{4,3},{5,4},{6,5},{7,6},{8,7},{9,8},{10,9... | collective-permute-start | bytes 18440 | tf_op jit(solution)/shard_map/ppermute | solution.py:357
  14.3 2.0 collective-permute-start.2
  19.3 6.2 %collective-permute-start.5 = (bf16[8,384]{1,0:T(8,128)(2,1)}, bf16[8,384]{1,0:T(8,128)(2,1)S(1)}, u32[]{:S(2)}, u32[]{:S(2)}) collective-permute-start(bf16[8,384]{1,0:T(8,128)(2,1)} %get-tuple-element.31), channel_id=1, source_target_pairs={{0,7},{1,8},{2,9},{3,10},{4,11},{5,12},{6,13},{7,14},{8,15},{9,16}... | collective-permute-start | bytes 18440 | tf_op jit(solution)/shard_map/ppermute | solution.py:361
  26.3 11.4 %collective-permute-start.7 = (bf16[8,384]{1,0:T(8,128)(2,1)}, bf16[8,384]{1,0:T(8,128)(2,1)S(1)}, u32[]{:S(2)}, u32[]{:S(2)}) collective-permute-start(bf16[8,384]{1,0:T(8,128)(2,1)} %get-tuple-element.33), channel_id=1, source_target_pairs={{0,55},{1,56},{2,57},{3,58},{4,59},{5,60},{6,61},{7,62},{8,63},{9,... | collective-permute-start | bytes 18440 | tf_op jit(solution)/shard_map/ppermute | solution.py:363
  39.4 7.0 %all-to-all-start = ((bf16[8,400,128]{2,1,0:T(8,128)(2,1)}), bf16[8,400,128]{2,1,0:T(8,128)(2,1)S(1)}, u32[]{:S(2)}, u32[]{:S(2)}) async-start(bf16[8,400,128]{2,1,0:T(8,128)(2,1)} %broadcast_in_dim.2), calls=%async_computation | async-start | bytes 1638400 | tf_op jit(solution)/shard_map/all_to_all | solution.py:407
  47.4 21.4 %all-to-all-done.got_ref = bf16[8,400,128]{2,1,0:T(8,128)(2,1)S(1)} async-done(((bf16[8,400,128]{2,1,0:T(8,128)(2,1)}), bf16[8,400,128]{2,1,0:T(8,128)(2,1)S(1)}, u32[]{:S(2)}, u32[]{:S(2)}) %all-to-all-start) | async-done | bytes 819232 | tf_op jit(solution)/shard_map/all_to_all | solution.py:407
  69.7 2.9 %shard_map.245 = bf16[4,160,1152]{2,1,0:T(8,128)(2,1)} custom-call(bf16[8,400,128]{2,1,0:T(8,128)(2,1)} %copy-done.1, bf16[432,512]{1,0:T(8,128)(2,1)} %constant.51.clone.rows_ref), custom_call_target="tpu_custom_call" | custom-call | tf_op jit(solution)/shard_map/pallas_call | solution.py:339
  72.5 22.1 %all_to_all.37.own_ref = bf16[4,160,1152]{2,1,0:T(8,128)(2,1)S(1)} all-to-all(bf16[4,160,1152]{2,1,0:T(8,128)(2,1)} %shard_map.245), channel_id=1, replica_groups={{0,2,4,6},{1,3,5,7},{8,10,12,14},{9,11,13,15},{16,18,20,22},{17,19,21,2..., dimensions={0} | all-to-all | bytes 2949120 | tf_op jit(solution)/shard_map/all_to_all | solution.py:416
  94.7 3.1 %shard_map.248 = bf16[432,384]{1,0:T(8,128)(2,1)} custom-call(bf16[8,400,128]{2,1,0:T(8,128)(2,1)} %copy-done.1, bf16[144,128]{1,0:T(8,128)(2,1)} %constant.55.clone.rows_ref, bf16[512,384]{1,0:T(8,128)(2,1)} %constant.56.clone.lanes_ref), custom_call_target="tpu_custom_call" | custom-call | tf_op jit(solution)/shard_map/pallas_call | solution.py:339
  99.4 5.6 %all-to-all-start.2 = ((f32[8,1,128]{2,1,0:T(1,128)}), f32[8,1,128]{2,1,0:T(1,128)S(1)}, u32[]{:S(2)}, u32[]{:S(2)}) async-start(f32[8,1,128]{2,1,0:T(1,128)} %bitcast.33), calls=%async_computation.2 | async-start | bytes 8192 | tf_op jit(solution)/shard_map/all_to_all | solution.py:424
  106.3 3.9 %all-to-all-done.2 = f32[8,1,128]{2,1,0:T(1,128)S(1)} async-done(((f32[8,1,128]{2,1,0:T(1,128)}), f32[8,1,128]{2,1,0:T(1,128)S(1)}, u32[]{:S(2)}, u32[]{:S(2)}) %all-to-all-start.2) | async-done | bytes 4128 | tf_op jit(solution)/shard_map/all_to_all | solution.py:424
  110.7 6.7 %shard_map.247.stack = bf16[4,480,1152]{2,1,0:T(8,128)(2,1)} custom-call(s32[2]{0:T(128)} %pad_add_fusion.pos_ref, bf16[4,448,384]{2,1,0:T(8,128)(2,1)} %bitcast.23, f32[8,128]{1,0:T(8,128)} %bitcast.34, f32[8,384]{1,0:T(8,128)} %stack.41.vectors_ref, f32[384,384]{1,0:T(8,128)} %constant.52.clone.lanes_ref, f32[128,384]{1,0:T(8,128)} %constant.53.clone.groups_t_ref, ...), custom_call_target="tpu_custom_call" | custom-call | tf_op jit(solution)/shard_map/pallas_call | solution.py:339
  118.5 10.6 %shard_map.249 = (f32[4,8,48,128]{3,2,1,0:T(8,128)}, f32[4,8,128]{2,1,0:T(8,128)}, f32[4,8,128]{2,1,0:T(8,128)}, f32[4,40,128]{2,1,0:T(8,128)}, f32[4,40,128]{2,...) custom-call(s32[2]{0:T(128)} %pad_add_fusion.pos_ref, ...), custom_call_target="tpu_custom_call" | custom-call | tf_op jit(solution)/shard_map/pallas_call | solution.py:339
  129.1 5.5 %collective-permute-done.10.west_ref = f32[4,8,128]{2,1,0:T(8,128)S(1)} collective-permute-done((f32[4,8,128]{2,1,0:T(8,128)}, f32[4,8,128]{2,1,0:T(8,128)S(1)}, u32[]{:S(2)}, u32[]{:S(2)}) %collective-permute-start.10) | collective-permute-done | bytes 16416 | tf_op jit(solution)/shard_map/ppermute | solution.py:356
  134.7 3.0 %collective-permute-start.13 = (f32[4,40,128]{2,1,0:T(8,128)}, f32[4,40,128]{2,1,0:T(8,128)S(1)}, u32[]{:S(2)}, u32[]{:S(2)}) collective-permute-start(f32[4,40,128]{2,1,0:T(8,128)} %get-tuple-element.42), channel_id=1, source_target_pairs={{0,56},{1,57},{2,58},{3,59},{4,60},{5,61},{6,62},{7,63},{8,0},{9,1... | collective-permute-start | bytes 245768 | tf_op jit(solution)/shard_map/ppermute | solution.py:359
  137.7 7.4 %all-to-all-start.3 = ((f32[64,1,128]{2,1,0:T(1,128)}), f32[64,1,128]{2,1,0:T(1,128)S(1)}, u32[]{:S(2)}, u32[]{:S(2)}) async-start(f32[64,1,128]{2,1,0:T(1,128)} %bitcast.32), calls=%async_computation.3 | async-start | bytes 65536 | tf_op jit(solution)/shard_map/all_to_all | solution.py:482
  145.1 2.5 %collective-permute-start.11 = (f32[4,8,128]{2,1,0:T(8,128)}, f32[4,8,128]{2,1,0:T(8,128)S(1)}, u32[]{:S(2)}, u32[]{:S(2)}) collective-permute-start(f32[4,8,128]{2,1,0:T(8,128)} %get-tuple-element.40), channel_id=1, source_target_pairs={{0,63},{1,0},{2,1},{3,2},{4,3},{5,4},{6,5},{7,6},{8,7},{9,8},{10,9... | collective-permute-start | bytes 49160 | tf_op jit(solution)/shard_map/ppermute | solution.py:357
  147.6 7.5 %collective-permute-done.14.nw_ref = f32[8,128]{1,0:T(8,128)S(1)} collective-permute-done((f32[8,128]{1,0:T(8,128)}, f32[8,128]{1,0:T(8,128)S(1)}, u32[]{:S(2)}, u32[]{:S(2)}) %collective-permute-start.14) | collective-permute-done | bytes 4128 | tf_op jit(solution)/shard_map/ppermute | solution.py:360
  155.0 3.2 %collective-permute-done.15.ne_ref = f32[8,128]{1,0:T(8,128)S(1)} collective-permute-done((f32[8,128]{1,0:T(8,128)}, f32[8,128]{1,0:T(8,128)S(1)}, u32[]{:S(2)}, u32[]{:S(2)}) %collective-permute-start.15) | collective-permute-done | bytes 4128 | tf_op jit(solution)/shard_map/ppermute | solution.py:361
  158.9 4.5 %collective-permute-start.17 = (f32[8,128]{1,0:T(8,128)}, f32[8,128]{1,0:T(8,128)S(1)}, u32[]{:S(2)}, u32[]{:S(2)}) collective-permute-start(f32[8,128]{1,0:T(8,128)} %get-tuple-element.46), channel_id=1, source_target_pairs={{0,55},{1,56},{2,57},{3,58},{4,59},{5,60},{6,61},{7,62},{8,63},{9,... | collective-permute-start | bytes 12296 | tf_op jit(solution)/shard_map/ppermute | solution.py:363
  163.4 3.5 %shard_map.250.weights = bf16[3456,384]{1,0:T(8,128)(2,1)} custom-call(s32[2]{0:T(128)} %pad_add_fusion.pos_ref, bf16[4,432,384]{2,1,0:T(8,128)(2,1)} %bitcast.25, bf16[4,432,384]{2,1,0:T(8,128)(2,1)} %copy-done.3), custom_call_target="tpu_custom_call" | custom-call | tf_op jit(solution)/shard_map/pallas_call | solution.py:339
  167.6 8.6 %shard_map.251 = bf16[4,8,40,384]{3,2,1,0:T(8,128)(2,1)} custom-call(s32[2]{0:T(128)} %pad_add_fusion.pos_ref, f32[4,8,48,128]{3,2,1,0:T(8,128)} %get-tuple-element.38.field_ref, f32[4,8,128]{2,1,0:T(8,128)} %copy-done.11, f32[4,8,128]{2,1,0:T(8,128)} %copy-done.12, f32[4,40,128]{2,1,0:T(8,128)} %copy-done.7, f32[4,40,128]{2,1,0:T(8,128)} %copy-done.8, ...), custom_call_target="tpu_custom_call" | custom-call | tf_op jit(solution)/shard_map/pallas_call | solution.py:339
  176.1 17.8 %all_to_all.38 = bf16[4,8,40,384]{3,2,1,0:T(8,128)(2,1)S(1)} all-to-all(bf16[4,8,40,384]{3,2,1,0:T(8,128)(2,1)} %shard_map.251), channel_id=1, replica_groups=mesh['tm'=4,'space'=64] {'tm'}, dimensions={0} | all-to-all | bytes 1966080 | tf_op jit(solution)/shard_map/all_to_all | solution.py:501
  (112 shorter events, 14.7 us)
Async XLA Ops:
  9.6 9.7 %collective-permute-start = (bf16[8,384]{1,0:T(8,128)(2,1)}, bf16[8,384]{1,0:T(8,128)(2,1)S(1)}, u32[]{:S(2)}, u32[]{:S(2)}) collective-permute-start(bf16[8,384]{1,0:T(8,128)(2,1)} %get-tuple-element.28), channel_id=1, source_target_pairs={{0,1},{1,2},{2,3},{3,4},{4,5},{5,6},{6,7},{7,8},{8,9},{9,10},{10,1... | collective-permute-start | bytes 18440 | tf_op jit(solution)/shard_map/ppermute | solution.py:356
  9.6 15.9 %collective-permute-start.1 = (bf16[8,384]{1,0:T(8,128)(2,1)}, bf16[8,384]{1,0:T(8,128)(2,1)S(1)}, u32[]{:S(2)}, u32[]{:S(2)}) collective-permute-start(bf16[8,384]{1,0:T(8,128)(2,1)} %get-tuple-element.29), channel_id=1, source_target_pairs={{0,63},{1,0},{2,1},{3,2},{4,3},{5,4},{6,5},{7,6},{8,7},{9,8},{10,9... | collective-permute-start | bytes 18440 | tf_op jit(solution)/shard_map/ppermute | solution.py:357
  14.3 11.3 %collective-permute-start.2 = (bf16[40,384]{1,0:T(8,128)(2,1)S(1)}, bf16[40,384]{1,0:T(8,128)(2,1)S(1)}, u32[]{:S(2)}, u32[]{:S(2)}) collective-permute-start(bf16[40,384]{1,0:T(8,128)(2,1)S(1)} %get-tuple-element.50), channel_id=1, source_target_pairs={{0,8},{1,9},{2,10},{3,11},{4,12},{5,13},{6,14},{7,15},{8,16},{9,17... | collective-permute-start | bytes 92168 | tf_op jit(solution)/shard_map/ppermute | solution.py:358
  16.2 30.2 %collective-permute-start.3 = (bf16[40,384]{1,0:T(8,128)(2,1)S(1)}, bf16[40,384]{1,0:T(8,128)(2,1)S(1)}, u32[]{:S(2)}, u32[]{:S(2)}) collective-permute-start(bf16[40,384]{1,0:T(8,128)(2,1)S(1)} %get-tuple-element.49), channel_id=1, source_target_pairs={{0,56},{1,57},{2,58},{3,59},{4,60},{5,61},{6,62},{7,63},{8,0},{9,1... | collective-permute-start | bytes 92168 | tf_op jit(solution)/shard_map/ppermute | solution.py:359
  18.2 28.3 %collective-permute-start.4 = (bf16[8,384]{1,0:T(8,128)(2,1)}, bf16[8,384]{1,0:T(8,128)(2,1)S(1)}, u32[]{:S(2)}, u32[]{:S(2)}) collective-permute-start(bf16[8,384]{1,0:T(8,128)(2,1)} %get-tuple-element.30), channel_id=1, source_target_pairs={{0,9},{1,10},{2,11},{3,12},{4,13},{5,14},{6,15},{7,16},{8,17},{9,1... | collective-permute-start | bytes 18440 | tf_op jit(solution)/shard_map/ppermute | solution.py:360
  19.3 27.2 %collective-permute-start.5 = (bf16[8,384]{1,0:T(8,128)(2,1)}, bf16[8,384]{1,0:T(8,128)(2,1)S(1)}, u32[]{:S(2)}, u32[]{:S(2)}) collective-permute-start(bf16[8,384]{1,0:T(8,128)(2,1)} %get-tuple-element.31), channel_id=1, source_target_pairs={{0,7},{1,8},{2,9},{3,10},{4,11},{5,12},{6,13},{7,14},{8,15},{9,16}... | collective-permute-start | bytes 18440 | tf_op jit(solution)/shard_map/ppermute | solution.py:361
  25.6 20.9 %collective-permute-start.6 = (bf16[8,384]{1,0:T(8,128)(2,1)}, bf16[8,384]{1,0:T(8,128)(2,1)S(1)}, u32[]{:S(2)}, u32[]{:S(2)}) collective-permute-start(bf16[8,384]{1,0:T(8,128)(2,1)} %get-tuple-element.32), channel_id=1, source_target_pairs={{0,57},{1,58},{2,59},{3,60},{4,61},{5,62},{6,63},{7,0},{8,1},{9,2}... | collective-permute-start | bytes 18440 | tf_op jit(solution)/shard_map/ppermute | solution.py:362
  25.6 0.7 collective-permute-start.8
  26.3 20.2 %collective-permute-start.7 = (bf16[8,384]{1,0:T(8,128)(2,1)}, bf16[8,384]{1,0:T(8,128)(2,1)S(1)}, u32[]{:S(2)}, u32[]{:S(2)}) collective-permute-start(bf16[8,384]{1,0:T(8,128)(2,1)} %get-tuple-element.33), channel_id=1, source_target_pairs={{0,55},{1,56},{2,57},{3,58},{4,59},{5,60},{6,61},{7,62},{8,63},{9,... | collective-permute-start | bytes 18440 | tf_op jit(solution)/shard_map/ppermute | solution.py:363
  39.4 29.3 %all-to-all-start = ((bf16[8,400,128]{2,1,0:T(8,128)(2,1)}), bf16[8,400,128]{2,1,0:T(8,128)(2,1)S(1)}, u32[]{:S(2)}, u32[]{:S(2)}) async-start(bf16[8,400,128]{2,1,0:T(8,128)(2,1)} %broadcast_in_dim.2), calls=%async_computation | async-start | bytes 1638400 | tf_op jit(solution)/shard_map/all_to_all | solution.py:407
  46.4 59.8 %all-gather.5.cloned.1.call-start = ((), (), s32[]{:S(2)}) async-start(), calls=%async_computation.5 | async-start | bytes 1720320 | tf_op jit(solution)/shard_map/all_gather | solution.py:412
  47.3 87.3 %all-gather.7.cloned.1.call-start = ((), (), s32[]{:S(2)}) async-start(), calls=%async_computation.6 | async-start | bytes 1658880 | tf_op jit(solution)/shard_map/all_gather | solution.py:478
  97.9 19.5 %collective-permute-start.9 = (bf16[4,160,1152]{2,1,0:T(8,128)(2,1)S(1)}, bf16[4,160,1152]{2,1,0:T(8,128)(2,1)S(1)}, u32[]{:S(2)}, u32[]{:S(2)}) collective-permute-start(bf16[4,160,1152]{2,1,0:T(8,128)(2,1)S(1)} %all_to_all.37.own_ref), channel_id=1, source_target_pairs={{0,1},{1,0},{2,3},{3,2},{4,5},{5,4},{6,7},{7,6},{8,9},{9,8},{10,11... | collective-permute-start | bytes 4423688 | tf_op jit(solution)/shard_map/ppermute | solution.py:439
  99.4 10.8 %all-to-all-start.2 = ((f32[8,1,128]{2,1,0:T(1,128)}), f32[8,1,128]{2,1,0:T(1,128)S(1)}, u32[]{:S(2)}, u32[]{:S(2)}) async-start(f32[8,1,128]{2,1,0:T(1,128)} %bitcast.33), calls=%async_computation.2 | async-start | bytes 8192 | tf_op jit(solution)/shard_map/all_to_all | solution.py:424
  129.1 5.5 %collective-permute-start.10 = (f32[4,8,128]{2,1,0:T(8,128)}, f32[4,8,128]{2,1,0:T(8,128)S(1)}, u32[]{:S(2)}, u32[]{:S(2)}) collective-permute-start(f32[4,8,128]{2,1,0:T(8,128)} %get-tuple-element.39), channel_id=1, source_target_pairs={{0,1},{1,2},{2,3},{3,4},{4,5},{5,6},{6,7},{7,8},{8,9},{9,10},{10,1... | collective-permute-start | bytes 49160 | tf_op jit(solution)/shard_map/ppermute | solution.py:356
  134.6 24.3 %collective-permute-start.18 = (bf16[4,432,384]{2,1,0:T(8,128)(2,1)}, bf16[4,432,384]{2,1,0:T(8,128)(2,1)S(1)}, u32[]{:S(2)}, u32[]{:S(2)}) collective-permute-start(bf16[4,432,384]{2,1,0:T(8,128)(2,1)} %bitcast.24), channel_id=1, source_target_pairs={{0,1},{1,0},{2,3},{3,2},{4,5},{5,4},{6,7},{7,6},{8,9},{9,8},{10,11... | collective-permute-start | bytes 3981320 | tf_op jit(solution)/shard_map/ppermute | solution.py:480
  134.6 32.3 %collective-permute-start.12 = (f32[4,40,128]{2,1,0:T(8,128)}, f32[4,40,128]{2,1,0:T(8,128)S(1)}, u32[]{:S(2)}, u32[]{:S(2)}) collective-permute-start(f32[4,40,128]{2,1,0:T(8,128)} %get-tuple-element.41), channel_id=1, source_target_pairs={{0,8},{1,9},{2,10},{3,11},{4,12},{5,13},{6,14},{7,15},{8,16},{9,17... | collective-permute-start | bytes 245768 | tf_op jit(solution)/shard_map/ppermute | solution.py:358
  134.7 32.2 %collective-permute-start.13 = (f32[4,40,128]{2,1,0:T(8,128)}, f32[4,40,128]{2,1,0:T(8,128)S(1)}, u32[]{:S(2)}, u32[]{:S(2)}) collective-permute-start(f32[4,40,128]{2,1,0:T(8,128)} %get-tuple-element.42), channel_id=1, source_target_pairs={{0,56},{1,57},{2,58},{3,59},{4,60},{5,61},{6,62},{7,63},{8,0},{9,1... | collective-permute-start | bytes 245768 | tf_op jit(solution)/shard_map/ppermute | solution.py:359
  137.7 29.2 %all-to-all-start.3 = ((f32[64,1,128]{2,1,0:T(1,128)}), f32[64,1,128]{2,1,0:T(1,128)S(1)}, u32[]{:S(2)}, u32[]{:S(2)}) async-start(f32[64,1,128]{2,1,0:T(1,128)} %bitcast.32), calls=%async_computation.3 | async-start | bytes 65536 | tf_op jit(solution)/shard_map/all_to_all | solution.py:482
  145.1 21.8 %collective-permute-start.11 = (f32[4,8,128]{2,1,0:T(8,128)}, f32[4,8,128]{2,1,0:T(8,128)S(1)}, u32[]{:S(2)}, u32[]{:S(2)}) collective-permute-start(f32[4,8,128]{2,1,0:T(8,128)} %get-tuple-element.40), channel_id=1, source_target_pairs={{0,63},{1,0},{2,1},{3,2},{4,3},{5,4},{6,5},{7,6},{8,7},{9,8},{10,9... | collective-permute-start | bytes 49160 | tf_op jit(solution)/shard_map/ppermute | solution.py:357
  147.6 7.5 %collective-permute-start.14 = (f32[8,128]{1,0:T(8,128)}, f32[8,128]{1,0:T(8,128)S(1)}, u32[]{:S(2)}, u32[]{:S(2)}) collective-permute-start(f32[8,128]{1,0:T(8,128)} %get-tuple-element.43), channel_id=1, source_target_pairs={{0,9},{1,10},{2,11},{3,12},{4,13},{5,14},{6,15},{7,16},{8,17},{9,1... | collective-permute-start | bytes 12296 | tf_op jit(solution)/shard_map/ppermute | solution.py:360
  155.0 3.2 %collective-permute-start.15 = (f32[8,128]{1,0:T(8,128)}, f32[8,128]{1,0:T(8,128)S(1)}, u32[]{:S(2)}, u32[]{:S(2)}) collective-permute-start(f32[8,128]{1,0:T(8,128)} %get-tuple-element.44), channel_id=1, source_target_pairs={{0,7},{1,8},{2,9},{3,10},{4,11},{5,12},{6,13},{7,14},{8,15},{9,16}... | collective-permute-start | bytes 12296 | tf_op jit(solution)/shard_map/ppermute | solution.py:361
  158.3 8.6 %collective-permute-start.16 = (f32[8,128]{1,0:T(8,128)}, f32[8,128]{1,0:T(8,128)S(1)}, u32[]{:S(2)}, u32[]{:S(2)}) collective-permute-start(f32[8,128]{1,0:T(8,128)} %get-tuple-element.45), channel_id=1, source_target_pairs={{0,57},{1,58},{2,59},{3,60},{4,61},{5,62},{6,63},{7,0},{8,1},{9,2}... | collective-permute-start | bytes 12296 | tf_op jit(solution)/shard_map/ppermute | solution.py:362
  158.9 7.9 %collective-permute-start.17 = (f32[8,128]{1,0:T(8,128)}, f32[8,128]{1,0:T(8,128)S(1)}, u32[]{:S(2)}, u32[]{:S(2)}) collective-permute-start(f32[8,128]{1,0:T(8,128)} %get-tuple-element.46), channel_id=1, source_target_pairs={{0,55},{1,56},{2,57},{3,58},{4,59},{5,60},{6,61},{7,62},{8,63},{9,... | collective-permute-start | bytes 12296 | tf_op jit(solution)/shard_map/ppermute | solution.py:363
  (24 other events, 176.1 us)
Sparse Core Ops, SparseCore 0:
  49.1 30.2 all-gather.4
  98.0 24.2 all-gather.6

commit v3 on v2

v3 whole, which is shorter than its diff:
```python
import functools

import jax
import jax.numpy as jnp
import numpy as np
from jax import lax
from jax.experimental import pallas as pl
from jax.experimental.pallas import tpu as pltpu
from jax.sharding import PartitionSpec as P

EPS = 1e-06
BF = jnp.bfloat16
F32 = jnp.float32
VM = pl.BlockSpec(memory_space=pltpu.VMEM)
SM = pl.BlockSpec(memory_space=pltpu.SMEM)
HIGH = lax.Precision.HIGHEST

NZ, NX, NC, NY = 8, 4, 2, 4
COLS = NX * NC
SPACE = NZ * COLS
ROWS, WIDE, PITCH = 8, 40, 48
CH, PART, WG = 384, 96, 12
GUARD = 16
LEAD = 8
RING = LEAD + (ROWS + 2) * PITCH + 8
FIELD = RING + 2 * PITCH
BOTH = ("tm", "space")
ALONG_Z = [[z * COLS + q for z in range(NZ)] for q in range(COLS)]
ALONG_X = [[z * COLS + x * NC + c for x in range(NX)] for z in range(NZ) for c in range(NC)]
PLANE = [[y * SPACE + z * COLS + q for y in range(NY) for q in range(COLS)] for z in range(NZ)]
SIBLING = [(s, s ^ 1) for s in range(SPACE)]


def moved(down, right):
    return [(s, (s + COLS * down + right) % SPACE) for s in range(SPACE)]


SWAP = [
    (y * SPACE + z * COLS + q, (z // 2) * SPACE + (2 * y + z % 2) * COLS + q)
    for y in range(NY)
    for z in range(NZ)
    for q in range(COLS)
]


def one_hot(rows, cols, pairs):
    out = np.zeros((rows, cols), np.float32)
    for r, c in pairs:
        out[r, c] = 1.0
    return out


CHANNEL_LANES = one_hot(
    CH, CH, [(6 * (8 * z + q) + i, 48 * q + 6 * z + i) for z in range(8) for q in range(8) for i in range(6)]
)
GROUPS_OF = one_hot(CH, 128, [(c, c // WG) for c in range(CH)])
SQUARES_OF = np.roll(GROUPS_OF, 64, axis=1)
GROUPS_OF_LANES = (CHANNEL_LANES.T @ GROUPS_OF).T
SQUARES_OF_LANES = (CHANNEL_LANES.T @ SQUARES_OF).T
PART_GROUPS = one_hot(128, 128, [(c, c // WG) for c in range(PART)])
PART_SQUARES = np.roll(PART_GROUPS, 64, axis=1)
EDGES = one_hot(
    32,
    320,
    [(2 * r + c, 40 * r + c) for r in range(8) for c in range(2)]
    + [(16 + 2 * r + c, 40 * r + 38 + c) for r in range(8) for c in range(2)],
)
FIRST_ROWS = one_hot(
    336, 384, [(48 * g + 6 * z + i, 48 * z + 6 * g + i) for g in range(7) for z in range(8) for i in range(6)]
)
SECOND_ROWS = one_hot(
    144, 128, [(16 * k + 6 * h + i, 64 * h + 6 * k + i) for k in range(9) for h in range(2) for i in range(6)]
)
SECOND_LANES = one_hot(512, CH, [(128 * y + o, PART * y + o) for y in range(4) for o in range(PART)])
PART_LANES = one_hot(
    128, 128, [(48 * h + 6 * q + i, 16 * q + 6 * h + i) for h in range(2) for q in range(8) for i in range(6)]
)


def dot(a, b):
    return jnp.dot(a, b, preferred_element_type=F32)


def exact(a, b):
    return jnp.dot(a, b, preferred_element_type=F32, precision=HIGH)


def merge(sums, count, groups_t, squares_t):
    mean = jnp.mean(sums, axis=0, keepdims=True)
    off = sums - mean
    between = count * jnp.sum(off * off, axis=0, keepdims=True)
    within = jnp.sum(sums, axis=0, keepdims=True)
    rows = jnp.concatenate([mean, between, jnp.zeros((6, 128), F32)], axis=0)
    by_lane = exact(rows, groups_t)
    spread = (by_lane[1:2] + exact(tall(within), squares_t)[0:1]) * (1.0 / (count * sums.shape[0]))
    return by_lane[0:1], lax.rsqrt(spread + EPS)


def pool(rows, count):
    mean = jnp.mean(rows, axis=0, keepdims=True)
    off = rows - mean
    between = count * jnp.sum(off * off, axis=0, keepdims=True)
    squares = jnp.sum(rows, axis=0, keepdims=True) + pltpu.roll(tall(between), 64, axis=1)[0:1]
    return jnp.where(lax.broadcasted_iota(jnp.int32, (1, 128), 1) < 64, mean, squares)


def tall(row):
    return jnp.broadcast_to(row, (8, row.shape[1]))


def chosen(part):
    channel = lax.broadcasted_iota(jnp.int32, (CH, 128), 0)
    lane = lax.broadcasted_iota(jnp.int32, (CH, 128), 1)
    return ((channel == part * PART + lane) & (lane < PART)).astype(F32)


def silu(u):
    return u / (1.0 + jnp.exp(-u))


def measure_tile(
    tile_ref, lanes_ref, groups_ref, groups_t_ref, squares_ref, edges_ref,
    placed_ref, west_ref, east_ref, sums_ref,
):
    tile = tile_ref[...]
    placed = dot(tile, lanes_ref[...]).astype(BF)
    placed_ref[...] = placed
    edges = dot(edges_ref[...], placed).astype(BF)
    west_ref[...] = edges[0:16]
    east_ref[...] = edges[16:32]
    wide = tile.astype(F32)
    mean = exact(tall(jnp.sum(wide, axis=0, keepdims=True)), groups_ref[...]) * (1.0 / (320 * WG))
    off = wide - exact(mean, groups_t_ref[...])[0:1]
    squares = exact(tall(jnp.sum(off * off, axis=0, keepdims=True)), squares_ref[...])
    sums_ref[...] = jnp.broadcast_to((mean + squares)[0:1], sums_ref.shape)


def pool_plane(sums_ref, out_ref):
    row = pool(sums_ref[...], 320.0 * WG)
    hi = row.astype(BF).astype(F32)
    mid = (row - hi).astype(BF).astype(F32)
    rows = jnp.concatenate([hi, mid, row - hi - mid, jnp.zeros((5, 128), F32)], axis=0)
    out_ref[...] = jnp.concatenate([rows, jnp.zeros((8, CH - 128), F32)], axis=1).astype(BF)


def arrange_first(got_ref, rows_ref, out_ref, sums_ref):
    blocks = [got_ref[z, 0:48, :] for z in range(NZ)]
    ordered = dot(rows_ref[...], jnp.concatenate(blocks, axis=0)).astype(BF)
    for copy in range(NX):
        out_ref[copy] = ordered
    wide = [b[:, 0:128].astype(F32) for b in blocks]
    sums_ref[...] = jnp.concatenate([b[42:43] + b[43:44] + b[44:45] for b in wide], axis=0)


def arrange_second(got_ref, rows_ref, lanes_ref, out_ref):
    by_part = []
    for y in range(NY):
        pair = jnp.concatenate([got_ref[2 * y + h, 48:112, :] for h in range(2)], axis=0)
        by_part.append(dot(rows_ref[...], pair).astype(BF))
    tall_parts = [
        jnp.concatenate([by_part[y][:, 128 * d : 128 * d + 128] for y in range(NY)], axis=1) for d in range(3)
    ]
    out_ref[...] = dot(jnp.concatenate(tall_parts, axis=0), lanes_ref[...]).astype(BF)


def first_act(
    pos_ref, lat_ref, sums_ref, vectors_ref, lanes_ref, groups_t_ref, squares_t_ref, stack, flat
):
    row, col = pos_ref[0] // COLS, pos_ref[0] % COLS
    mean_l, scale_l = merge(sums_ref[...], 320.0 * WG * NY * COLS, groups_t_ref[...], squares_t_ref[...])
    affine = exact(vectors_ref[...], lanes_ref[...])
    scale_l = scale_l * affine[0:1]
    shift_l = affine[1:2]
    has_w = (col > 0).astype(F32)
    has_e = (col < COLS - 1).astype(F32)
    has_n = (row > 0).astype(F32)
    has_s = (row < NZ - 1).astype(F32)
    flat[...] = jnp.zeros_like(flat)
    for t in range(NY):
        act = silu((lat_ref[t].astype(F32) - mean_l) * scale_l + shift_l)
        for r in range(-2, ROWS + 2):
            base = GUARD + PITCH * (r + 2)
            if 0 <= r < ROWS:
                cells = act[WIDE * r : WIDE * r + WIDE]
                left, right = act[320 + 2 * r : 322 + 2 * r] * has_w, act[336 + 2 * r : 338 + 2 * r] * has_e
            else:
                start, at, inside = (352, r + 2, has_n) if r < 0 else (440, r - ROWS, has_s)
                cells = act[start + WIDE * at : start + WIDE * at + WIDE] * inside
                left = act[start + 80 + 2 * at : start + 82 + 2 * at] * (inside * has_w)
                right = act[start + 84 + 2 * at : start + 86 + 2 * at] * (inside * has_e)
            flat[base : base + WIDE, :] = cells
            flat[base + WIDE : base + WIDE + 2, :] = right
            flat[base - 2 : base, :] = left
        for d in range(3):
            start = GUARD - LEAD + d - 1
            stack[t, :, CH * d : CH * d + CH] = flat[start : start + FIELD, :].astype(BF)


def first_conv(
    pos_ref, stack, own_ref, other_ref, vectors_ref, part_ref, part_t_ref, part_squares_ref, spread_ref,
    out_ref, sums_ref, packed, weights,
):
    core = pos_ref[0] % NC
    bias = exact(vectors_ref[...], chosen(pos_ref[1]))[2:3]
    for mine in range(NC):

        @pl.when(core == mine)
        def _():
            for x in range(NX):
                for g in range(7):
                    at = 48 * (NC * x + mine)
                    packed[g, at : at + 48, :] = own_ref[x, 48 * g : 48 * g + 48, :]
                    at = 48 * (NC * x + 1 - mine)
                    packed[g, at : at + 48, :] = other_ref[x, 48 * g : 48 * g + 48, :]

    for g in range(7):
        taps = dot(packed[g], spread_ref[...]).astype(BF)
        for tap in range(4 * g, min(4 * g + 4, 27)):
            down, right = CH * (tap % 3), 128 * (tap // 3)
            weights[down : down + CH, right : right + 128] = taps[:, 128 * (tap % 4) : 128 * (tap % 4) + 128]
    totals = [None] * NY
    for t in range(NY):
        for dt in range(3):
            to = t + 2 - dt
            if to >= NY:
                continue
            part = dot(stack[t], weights[:, CH * dt : CH * dt + CH])
            term = part[0:RING, 0:128]
            for dy in (1, 2):
                term = term + part[PITCH * dy : PITCH * dy + RING, 128 * dy : 128 * dy + 128]
            totals[to] = term if totals[to] is None else totals[to] + term
    at = lax.broadcasted_iota(jnp.int32, (RING, 1), 0) - (LEAD + PITCH)
    inside = ((at >= 0) & (at < PITCH * ROWS) & (at % PITCH < WIDE)).astype(F32)
    sums = None
    for t in range(NY):
        totals[t] = totals[t] + bias
        out_ref[t] = totals[t]
        line = jnp.sum(totals[t] * inside, axis=0, keepdims=True)
        sums = line if sums is None else sums + line
    mean = exact(tall(sums), part_ref[...]) * (1.0 / (320 * NY * WG))
    mean_l = exact(mean, part_t_ref[...])[0:1]
    sums = None
    for t in range(NY):
        off = (totals[t] - mean_l) * inside
        line = jnp.sum(off * off, axis=0, keepdims=True)
        sums = line if sums is None else sums + line
    squares = exact(tall(sums), part_squares_ref[...])
    sums_ref[...] = jnp.broadcast_to((mean + squares)[0:1], (SPACE, 128))


def assemble_second(pos_ref, own_ref, other_ref, weights):
    core = pos_ref[0] % NC
    for mine in range(NC):

        @pl.when(core == mine)
        def _():
            for x in range(NX):
                for d in range(3):
                    for k in range(9):
                        tap = 9 * (k // 3) + 3 * (k % 3) + d
                        source = 144 * d + 16 * k
                        at = 128 * tap + 16 * (NC * x + mine)
                        weights[at : at + 16, :] = own_ref[x, source : source + 16, :]
                        at = 128 * tap + 16 * (NC * x + 1 - mine)
                        weights[at : at + 16, :] = other_ref[x, source : source + 16, :]


def second_conv(
    pos_ref, field_ref, sums_ref, vectors_ref, weights, groups_t_ref, squares_t_ref, order_ref, out_ref, flat, stack
):
    row, col = pos_ref[0] // COLS, pos_ref[0] % COLS
    mean_l, scale_l = merge(sums_ref[...], 320.0 * NY * WG, groups_t_ref[...], squares_t_ref[...])
    affine = exact(vectors_ref[...], chosen(pos_ref[1]))
    scale_l = scale_l * affine[3:4]
    shift_l = affine[4:5]

    at = lax.broadcasted_iota(jnp.int32, (RING, 1), 0) - LEAD
    outside = (at < 0) & (row == 0) | (at < PITCH - 2) & (row == 0)
    outside = outside | (at >= PITCH * (ROWS + 1) - 1) & (row == NZ - 1)
    at = (at + PITCH) % PITCH
    outside = outside | (at == WIDE) & (col == COLS - 1) | (at == PITCH - 1) & (col == 0)
    keep = 1.0 - outside.astype(F32)
    for t in range(NY):
        act = silu((field_ref[t] - mean_l) * scale_l + shift_l) * keep
        flat[...] = dot(act.astype(BF), order_ref[...])
        for dy in range(3):
            for dx in range(3):
                start = LEAD + PITCH * dy + dx - 1
                lane = 128 * (3 * dy + dx)
                stack[t, :, lane : lane + 128] = flat[start : start + 384, :].astype(BF)
    for t in range(NY):
        total = None
        for dt in range(3):
            source = t - 2 + dt
            if source < 0:
                continue
            term = dot(stack[source], weights[1152 * dt : 1152 * dt + 1152, :])
            total = term if total is None else total + term
        for r in range(ROWS):
            out_ref[t, r] = total[PITCH * r : PITCH * r + WIDE].astype(BF)


def call(body, outs, scratch, smem, *args):
    return pl.pallas_call(
        body,
        out_shape=outs,
        in_specs=[SM] * smem + [VM] * (len(args) - smem),
        out_specs=jax.tree.map(lambda _: VM, outs),
        scratch_shapes=scratch,
        compiler_params=pltpu.CompilerParams(vmem_limit_bytes=56 * 1024 * 1024),
    )(*args)


def shape(dims, dtype):
    return jax.ShapeDtypeStruct(dims, dtype)


def by_group(kernel):
    taps = jnp.pad(kernel.reshape(27, 6, PART), ((0, 1), (0, 0), (0, 0))).reshape(7, 4, 6, PART)
    return jnp.transpose(taps, (0, 2, 1, 3)).reshape(42, CH)


def by_column(kernel):
    rows = jnp.transpose(kernel, (0, 1, 3, 2, 4)).reshape(54, 3, PART)
    return jnp.pad(rows, ((0, 10), (0, 0), (0, 32))).reshape(64, CH)


def shards(
    latents,
    gain_first,
    shift_first,
    kernel_first,
    bias_first,
    gain_second,
    shift_second,
    kernel_second,
    bias_second,
):
    space = lax.axis_index("space")
    frame = lax.axis_index("tm")
    pos = jnp.stack([space, frame]).astype(jnp.int32)
    vectors = jnp.stack(
        [gain_first, shift_first, bias_first, gain_second, shift_second, bias_second, bias_second, bias_second]
    )
    tile = latents[0, 0]
    flat_tile = tile.reshape(ROWS * WIDE, CH)

    swapped = lax.ppermute(by_column(kernel_second), BOTH, SWAP)
    placed, west, east, sums = call(
        measure_tile,
        (shape((320, CH), BF), shape((16, CH), BF), shape((16, CH), BF), shape((NY * COLS, 128), F32)),
        [],
        0,
        flat_tile,
        jnp.asarray(CHANNEL_LANES, BF),
        jnp.asarray(GROUPS_OF),
        jnp.asarray(GROUPS_OF.T),
        jnp.asarray(SQUARES_OF),
        jnp.asarray(EDGES, BF),
    )
    send = functools.partial(lax.ppermute, axis_name="space")
    from_west, from_east = send(east, perm=moved(0, 1)), send(west, perm=moved(0, -1))
    plane_sums = lax.all_to_all(sums, BOTH, 0, 0, tiled=True, axis_index_groups=PLANE)
    sums_rows = call(pool_plane, shape((8, CH), BF), [], 0, plane_sums)
    from_west, from_east, sums_rows, swapped, packed = lax.optimization_barrier(
        (from_west, from_east, sums_rows, swapped, by_group(kernel_first))
    )
    letter = jnp.concatenate([packed, sums_rows[0:6], swapped], axis=0)
    got = lax.all_to_all(
        jnp.broadcast_to(letter[None], (NZ, 112, CH)), "space", 0, 0, tiled=True, axis_index_groups=ALONG_Z
    )
    from_north = send(jnp.concatenate([placed[240:320], from_west[12:16], from_east[12:16]]), perm=moved(1, 0))
    from_south = send(jnp.concatenate([placed[0:80], from_west[0:4], from_east[0:4]]), perm=moved(-1, 0))
    parcel = jnp.concatenate([placed, from_west, from_east, from_north, from_south], axis=0)
    frames = lax.all_gather(parcel, "tm")
    ordered, all_sums = call(
        arrange_first,
        (shape((NX, 336, CH), BF), shape((8, 128), F32)),
        [],
        0,
        got,
        jnp.asarray(FIRST_ROWS, BF),
    )
    own = lax.all_to_all(ordered, "space", 0, 0, tiled=True, axis_index_groups=ALONG_X)
    stack = call(
        first_act,
        shape((NY, FIELD, 3 * CH), BF),
        [pltpu.VMEM((GUARD + (ROWS + 4) * PITCH + GUARD, CH), F32)],
        1,
        pos,
        frames,
        all_sums,
        vectors,
        jnp.asarray(CHANNEL_LANES),
        jnp.asarray(GROUPS_OF_LANES),
        jnp.asarray(SQUARES_OF_LANES),
    )
    got_second, _ = lax.optimization_barrier((got, stack))
    ordered_second = call(
        arrange_second,
        shape((432, CH), BF),
        [],
        0,
        got_second,
        jnp.asarray(SECOND_ROWS, BF),
        jnp.asarray(SECOND_LANES, BF),
    )
    own, stack, _ = lax.optimization_barrier((own, stack, ordered_second))
    other = lax.ppermute(own, "space", SIBLING)

    field, sums = call(
        first_conv,
        (shape((NY, RING, 128), F32), shape((SPACE, 128), F32)),
        [pltpu.VMEM((7, CH, CH), BF), pltpu.VMEM((3 * CH, 9 * 128), BF)],
        1,
        pos,
        stack,
        own,
        other,
        vectors,
        jnp.asarray(PART_GROUPS),
        jnp.asarray(PART_GROUPS.T),
        jnp.asarray(PART_SQUARES),
        jnp.asarray(SECOND_LANES.T, BF),
    )
    all_sums = lax.all_to_all(sums, "space", 0, 0, tiled=True)
    own_second = lax.all_gather(ordered_second, "space", axis_index_groups=ALONG_X)
    own_second, _ = lax.optimization_barrier((own_second, field))
    other_second = lax.ppermute(own_second, "space", SIBLING)
    weights_second = call(assemble_second, shape((27 * 128, CH), BF), [], 1, pos, own_second, other_second)
    partial = call(
        second_conv,
        shape((NY, ROWS, WIDE, CH), BF),
        [pltpu.VMEM((RING, 128), F32), pltpu.VMEM((NY, 384, 9 * 128), BF)],
        1,
        pos,
        field,
        all_sums,
        vectors,
        weights_second,
        jnp.asarray(PART_GROUPS.T),
        jnp.asarray(PART_SQUARES.T),
        jnp.asarray(PART_LANES, BF),
    )
    parts = lax.all_to_all(partial, "tm", 0, 0, tiled=True)
    second_out = jnp.sum(parts.astype(F32), axis=0) + bias_second
    return (tile.astype(F32) + second_out).astype(BF)[None, None]


def solution(mesh):
    placed = (
        P("tm", "space", None, None, None),
        P(),
        P(),
        P(None, None, None, "space", "tm"),
        P(),
        P(),
        P(),
        P(None, None, None, "space", "tm"),
        P(),
    )
    return jax.shard_map(
        shards,
        mesh=mesh,
        in_specs=placed,
        out_specs=P("tm", "space", None, None, None),
        check_vma=False,
    )
```

time: 202 us -> 175 us (0.87)
  starting transfers between devices: 56.8 us -> 32.7 us
  waiting for transfers between devices: 41.5 us -> 30.3 us
  Pallas kernels: 39.8 us -> 43.3 us
    ppermute x16 -> x4, starting transfers between devices: 36.1 us -> 7.77 us  [the longest x1 3.85 us: shards(): send(west, perm=moved(0, -1))]
    ppermute x16 -> x4, waiting for transfers between devices: 16.2 us -> 4.25 us  [the longest x1 2.45 us: shards(): send(jnp.concatenate([placed[0:80], from_west[0:4], from_east[0:4]]), per...]
    all_to_all x2, waiting for transfers between devices: 25.2 us -> 19.6 us  [the longest x1 16 us: shards(): lax.all_to_all(jnp.broadcast_to(letter[None], (NZ, 112, CH)), 'space', 0,...]
    pallas_call x7 -> x8, Pallas kernels: 38.4 us -> 43.3 us  [call(): pl.pallas_call(body, out_shape=outs, in_specs=[SM] * smem + [VM] * (len(a...]
    all_to_all x2, starting transfers between devices: 12.6 us -> 16.5 us  [the longest x1 11.3 us: shards(): lax.all_to_all(jnp.broadcast_to(letter[None], (NZ, 112, CH)), 'space', 0,...]
    all_to_all x1, waiting for transfers between devices: 0.01 us -> 3.77 us  [shards(): all_sums = lax.all_to_all(sums, 'space', 0, 0, tiled=True)]
    ppermute x1, waiting for transfers between devices: 0.01 us -> 2.63 us  [shards(): other = lax.ppermute(own, 'space', SIBLING)]
    unnamed x56 -> x38, local copies, waits for them, and re-layouts: 5.06 us -> 6.94 us
  transfers between devices with their start and end apart: 24 -> 12, of which waited for: 5 -> 6; matrix products, arithmetic and copies ran while one was open for 2% -> 3% of each run, Pallas kernels for 14% -> 12%
where the time goes in v3:
time: 175 us; the launch traced here: 173 us
  Pallas kernels  43.3 us (25%)
  blocking collectives  41.4 us (24%)
  starting transfers between devices  32.7 us (19%)
  waiting for transfers between devices  30.3 us (17%)
  between operations  13.7 us (8%)
  local copies, waits for them, and re-layouts  9.61 us (5%)
  other arithmetic  2.29 us (1%)
    pallas_call x8, Pallas kernels, call(): pl.pallas_call(body, out_shape=outs, in_specs=[SM] * smem + [VM] * (len(a...  43.3 us
    all_to_all x1, blocking collectives, shards(): lax.all_to_all(ordered, 'space', 0, 0, tiled=True, axis_index_groups=ALON...  23.1 us
    all_to_all x1, blocking collectives, shards(): parts = lax.all_to_all(partial, 'tm', 0, 0, tiled=True)  18.3 us
    all_to_all x1, waiting for transfers between devices, shards(): lax.all_to_all(jnp.broadcast_to(letter[None], (NZ, 112, CH)), 'space', 0,...  16 us
    all_to_all x1, starting transfers between devices, shards(): lax.all_to_all(jnp.broadcast_to(letter[None], (NZ, 112, CH)), 'space', 0,...  11.3 us
    all_to_all x1, starting transfers between devices, shards(): all_sums = lax.all_to_all(sums, 'space', 0, 0, tiled=True)  7.42 us
    unnamed x38, local copies, waits for them, and re-layouts  6.94 us
    all_to_all x1, starting transfers between devices, shards(): lax.all_to_all(sums, BOTH, 0, 0, tiled=True, axis_index_groups=PLANE)  5.22 us
  transfers between devices with their start and end apart: 12, of which 6 were waited for; matrix products, arithmetic and copies ran while one was open for 3% of the time, Pallas kernels for 12%

profile of v3, /device:TPU:32, one launch (start us, length us, event | category | flops | bytes accessed | tf_op | source)
XLA Modules:
  0.0 173.4 jit_solution(13966209165900295100)
XLA Ops:
  6.5 3.0 %shard_map.253 = (bf16[320,384]{1,0:T(8,128)(2,1)}, bf16[16,384]{1,0:T(8,128)(2,1)}, bf16[16,384]{1,0:T(8,128)(2,1)}, f32[32,128]{1,0:T(8,128)}) custom-call(bf16[320,384]{1,0:T(8,128)(2,1)} %bitcast.33, bf16[384,384]{1,0:T(8,128)(2,1)} %constant.48.clone.lanes_ref, f32[384,128]{1,0:T(8,128)} %constant.49.clone.groups_ref, ...), custom_call_target="tpu_custom_call" | custom-call | tf_op jit(solution)/shard_map/pallas_call | solution.py:304
  9.5 3.9 %collective-permute-start.1 = (bf16[16,384]{1,0:T(8,128)(2,1)}, bf16[16,384]{1,0:T(8,128)(2,1)S(1)}, u32[]{:S(2)}, u32[]{:S(2)}) collective-permute-start(bf16[16,384]{1,0:T(8,128)(2,1)} %get-tuple-element.23), channel_id=1, source_target_pairs={{0,63},{1,0},{2,1},{3,2},{4,3},{5,4},{6,5},{7,6},{8,7},{9,8},{10,9... | collective-permute-start | bytes 36872 | tf_op jit(solution)/shard_map/ppermute | solution.py:362
  13.4 5.2 %all-to-all-start = ((f32[32,1,128]{2,1,0:T(1,128)}), f32[32,1,128]{2,1,0:T(1,128)S(1)}, u32[]{:S(2)}, u32[]{:S(2)}) async-start(f32[32,1,128]{2,1,0:T(1,128)} %bitcast.44), calls=%async_computation | async-start | bytes 32768 | tf_op jit(solution)/shard_map/all_to_all | solution.py:363
  21.1 1.0 constant_dynamic-update-slice_fusion.4
  22.4 3.6 %all-to-all-done = f32[32,1,128]{2,1,0:T(1,128)S(1)} async-done(((f32[32,1,128]{2,1,0:T(1,128)}), f32[32,1,128]{2,1,0:T(1,128)S(1)}, u32[]{:S(2)}, u32[]{:S(2)}) %all-to-all-start) | async-done | bytes 16416 | tf_op jit(solution)/shard_map/all_to_all | solution.py:363
  26.6 1.4 shard_map.254
  28.0 3.8 %collective-permute-start.3 = (bf16[88,384]{1,0:T(8,128)(2,1)S(1)}, bf16[88,384]{1,0:T(8,128)(2,1)S(1)}, u32[]{:S(2)}, u32[]{:S(2)}) collective-permute-start(bf16[88,384]{1,0:T(8,128)(2,1)S(1)} %pad_maximum_fusion.1), channel_id=1, source_target_pairs={{0,8},{1,9},{2,10},{3,11},{4,12},{5,13},{6,14},{7,15},{8,16},{9,17... | collective-permute-start | bytes 202760 | tf_op jit(solution)/shard_map/ppermute | solution.py:372
  32.0 1.8 %collective-permute-done.3 = bf16[88,384]{1,0:T(8,128)(2,1)S(1)} collective-permute-done((bf16[88,384]{1,0:T(8,128)(2,1)S(1)}, bf16[88,384]{1,0:T(8,128)(2,1)S(1)}, u32[]{:S(2)}, u32[]{:S(2)}) %collective-permute-start.3) | collective-permute-done | bytes 67616 | tf_op jit(solution)/shard_map/ppermute | solution.py:372
  33.8 2.4 %collective-permute-done.4 = bf16[88,384]{1,0:T(8,128)(2,1)S(1)} collective-permute-done((bf16[88,384]{1,0:T(8,128)(2,1)S(1)}, bf16[88,384]{1,0:T(8,128)(2,1)S(1)}, u32[]{:S(2)}, u32[]{:S(2)}) %collective-permute-start.4) | collective-permute-done | bytes 67616 | tf_op jit(solution)/shard_map/ppermute | solution.py:373
  38.7 11.3 %all-to-all-start.1 = ((bf16[8,112,384]{2,1,0:T(8,128)(2,1)}), bf16[8,112,384]{2,1,0:T(8,128)(2,1)S(1)}, u32[]{:S(2)}, u32[]{:S(2)}) async-start(bf16[8,112,384]{2,1,0:T(8,128)(2,1)} %broadcast_in_dim.2), calls=%async_computation.1 | async-start | bytes 1376256 | tf_op jit(solution)/shard_map/all_to_all | solution.py:369
  51.4 16.0 %all-to-all-done.1.got_ref = bf16[8,112,384]{2,1,0:T(8,128)(2,1)S(1)} async-done(((bf16[8,112,384]{2,1,0:T(8,128)(2,1)}), bf16[8,112,384]{2,1,0:T(8,128)(2,1)S(1)}, u32[]{:S(2)}, u32[]{:S(2)}) %all-to-all-start.1) | async-done | bytes 688160 | tf_op jit(solution)/shard_map/all_to_all | solution.py:369
  68.4 2.5 %shard_map.255 = (bf16[4,336,384]{2,1,0:T(8,128)(2,1)}, f32[8,128]{1,0:T(8,128)}) custom-call(bf16[8,112,384]{2,1,0:T(8,128)(2,1)} %copy-done, bf16[336,384]{1,0:T(8,128)(2,1)} %constant.53.clone.rows_ref), custom_call_target="tpu_custom_call" | custom-call | tf_op jit(solution)/shard_map/pallas_call | solution.py:304
  70.9 7.8 %shard_map.256.stack = bf16[4,592,1152]{2,1,0:T(8,128)(2,1)} custom-call(s32[2]{0:T(128)} %pad_add_fusion.pos_ref, bf16[4,528,384]{2,1,0:T(8,128)(2,1)} %bitcast.30, f32[8,128]{1,0:T(8,128)} %get-tuple-element.32.sums_ref, f32[8,384]{1,0:T(8,128)} %stack.41.vectors_ref, f32[384,384]{1,0:T(8,128)} %constant.54.clone.lanes_ref, ...), custom_call_target="tpu_custom_call" | custom-call | tf_op jit(solution)/shard_map/pallas_call | solution.py:304
  78.7 2.6 %shard_map.257 = bf16[432,384]{1,0:T(8,128)(2,1)} custom-call(bf16[8,112,384]{2,1,0:T(8,128)(2,1)} %copy-done, bf16[144,128]{1,0:T(8,128)(2,1)} %constant.57.clone.rows_ref, bf16[512,384]{1,0:T(8,128)(2,1)} %constant.58.clone.lanes_ref), custom_call_target="tpu_custom_call" | custom-call | tf_op jit(solution)/shard_map/pallas_call | solution.py:304
  81.3 23.1 %all_to_all.37.own_ref = bf16[4,336,384]{2,1,0:T(8,128)(2,1)S(1)} all-to-all(bf16[4,336,384]{2,1,0:T(8,128)(2,1)S(1)} %copy-done.5), channel_id=1, replica_groups={{0,2,4,6},{1,3,5,7},{8,10,12,14},{9,11,13,15},{16,18,20,22},{17,19,21,2..., dimensions={0} | all-to-all | bytes 2064384 | tf_op jit(solution)/shard_map/all_to_all | solution.py:384
  104.4 2.6 %collective-permute-done.5.other_ref = bf16[4,336,384]{2,1,0:T(8,128)(2,1)S(1)} collective-permute-done((bf16[4,336,384]{2,1,0:T(8,128)(2,1)S(1)}, bf16[4,336,384]{2,1,0:T(8,128)(2,1)S(1)}, u32[]{:S(2)}, u32[]{:S(2)}) %collective-permute-start.5) | collective-permute-done | bytes 1032224 | tf_op jit(solution)/shard_map/ppermute | solution.py:409
  107.1 1.0 copy-done.4
  108.1 13.8 %shard_map.258 = (f32[4,496,128]{2,1,0:T(8,128)}, f32[64,128]{1,0:T(8,128)}) custom-call(s32[2]{0:T(128)} %pad_add_fusion.pos_ref, bf16[4,592,1152]{2,1,0:T(8,128)(2,1)} %shard_map.256.stack, bf16[4,336,384]{2,1,0:T(8,128)(2,1)} %copy-done.1, bf16[4,336,384]{2,1,0:T(8,128)(2,1)} %copy-done.4, f32[8,384]{1,0:T(8,128)} %stack.41.vectors_ref, ...), custom_call_target="tpu_custom_call" | custom-call | tf_op jit(solution)/shard_map/pallas_call | solution.py:304
  122.3 7.4 %all-to-all-start.3 = ((f32[64,1,128]{2,1,0:T(1,128)}), f32[64,1,128]{2,1,0:T(1,128)S(1)}, u32[]{:S(2)}, u32[]{:S(2)}) async-start(f32[64,1,128]{2,1,0:T(1,128)} %bitcast.42), calls=%async_computation.3 | async-start | bytes 65536 | tf_op jit(solution)/shard_map/all_to_all | solution.py:426
  129.7 1.1 copy-done.2
  130.8 3.7 %shard_map.259.weights = bf16[3456,384]{1,0:T(8,128)(2,1)} custom-call(s32[2]{0:T(128)} %pad_add_fusion.pos_ref, bf16[4,432,384]{2,1,0:T(8,128)(2,1)} %bitcast.32, bf16[4,432,384]{2,1,0:T(8,128)(2,1)} %copy-done.2), custom_call_target="tpu_custom_call" | custom-call | tf_op jit(solution)/shard_map/pallas_call | solution.py:304
  134.5 3.8 %all-to-all-done.3 = f32[64,1,128]{2,1,0:T(1,128)S(1)} async-done(((f32[64,1,128]{2,1,0:T(1,128)}), f32[64,1,128]{2,1,0:T(1,128)S(1)}, u32[]{:S(2)}, u32[]{:S(2)}) %all-to-all-start.3) | async-done | bytes 32800 | tf_op jit(solution)/shard_map/all_to_all | solution.py:426
  138.9 8.4 %shard_map.260 = bf16[4,8,40,384]{3,2,1,0:T(8,128)(2,1)} custom-call(s32[2]{0:T(128)} %pad_add_fusion.pos_ref, f32[4,496,128]{2,1,0:T(8,128)} %get-tuple-element.36.field_ref, f32[64,128]{1,0:T(8,128)} %bitcast.37, f32[8,384]{1,0:T(8,128)} %stack.41.vectors_ref, bf16[3456,384]{1,0:T(8,128)(2,1)} %shard_map.259.weights, ...), custom_call_target="tpu_custom_call" | custom-call | tf_op jit(solution)/shard_map/pallas_call | solution.py:304
  147.3 18.3 %all_to_all.38 = bf16[4,8,40,384]{3,2,1,0:T(8,128)(2,1)S(1)} all-to-all(bf16[4,8,40,384]{3,2,1,0:T(8,128)(2,1)} %shard_map.260), channel_id=1, replica_groups=mesh['tm'=4,'space'=64] {'tm'}, dimensions={0} | all-to-all | bytes 1966080 | tf_op jit(solution)/shard_map/all_to_all | solution.py:445
  (73 shorter events, 10.0 us)
Async XLA Ops:
  6.5 15.6 %copy-start.9 = (bf16[3,3,3,6,96]{4,3,2,1,0:T(8,128)(2,1)S(1)}, bf16[3,3,3,6,96]{4,3,2,1,0:T(8,128)(2,1)}, u32[]{:S(2)}) copy-start(bf16[3,3,3,6,96]{4,3,2,1,0:T(8,128)(2,1)} %param.30) | copy-start | bytes 93316
  9.5 18.4 %collective-permute-start = (bf16[16,384]{1,0:T(8,128)(2,1)}, bf16[16,384]{1,0:T(8,128)(2,1)S(1)}, u32[]{:S(2)}, u32[]{:S(2)}) collective-permute-start(bf16[16,384]{1,0:T(8,128)(2,1)} %get-tuple-element.22), channel_id=1, source_target_pairs={{0,1},{1,2},{2,3},{3,4},{4,5},{5,6},{6,7},{7,8},{8,9},{9,10},{10,1... | collective-permute-start | bytes 36872 | tf_op jit(solution)/shard_map/ppermute | solution.py:362
  9.5 18.4 %collective-permute-start.1 = (bf16[16,384]{1,0:T(8,128)(2,1)}, bf16[16,384]{1,0:T(8,128)(2,1)S(1)}, u32[]{:S(2)}, u32[]{:S(2)}) collective-permute-start(bf16[16,384]{1,0:T(8,128)(2,1)} %get-tuple-element.23), channel_id=1, source_target_pairs={{0,63},{1,0},{2,1},{3,2},{4,3},{5,4},{6,5},{7,6},{8,7},{9,8},{10,9... | collective-permute-start | bytes 36872 | tf_op jit(solution)/shard_map/ppermute | solution.py:362
  13.4 12.6 %all-to-all-start = ((f32[32,1,128]{2,1,0:T(1,128)}), f32[32,1,128]{2,1,0:T(1,128)S(1)}, u32[]{:S(2)}, u32[]{:S(2)}) async-start(f32[32,1,128]{2,1,0:T(1,128)} %bitcast.44), calls=%async_computation | async-start | bytes 32768 | tf_op jit(solution)/shard_map/all_to_all | solution.py:363
  18.6 52.3 %all-gather.5.cloned.1.call-start = ((), (), s32[]{:S(2)}) async-start(), calls=%async_computation.5 | async-start | bytes 2027520 | tf_op jit(solution)/shard_map/all_gather | solution.py:375
  19.6 8.4 %collective-permute-start.2 = (bf16[64,384]{1,0:T(8,128)(2,1)S(1)}, bf16[64,384]{1,0:T(8,128)(2,1)S(1)}, u32[]{:S(2)}, u32[]{:S(2)}) collective-permute-start(bf16[64,384]{1,0:T(8,128)(2,1)S(1)} %bitcast.41), channel_id=1, source_target_pairs={{0,0},{1,1},{2,2},{3,3},{4,4},{5,5},{6,6},{7,7},{8,8},{9,9},{10,10... | collective-permute-start | bytes 147464 | tf_op jit(solution)/shard_map/ppermute | solution.py:348
  22.1 27.9 %copy-start.11 = (f32[384]{0:T(512)S(1)}, f32[384]{0:T(512)}, u32[]{:S(2)}) copy-start(f32[384]{0:T(512)} %param.28) | copy-start | bytes 4612
  22.1 27.9 %copy-start.12 = (f32[384]{0:T(512)S(1)}, f32[384]{0:T(512)}, u32[]{:S(2)}) copy-start(f32[384]{0:T(512)} %param.29) | copy-start | bytes 4612
  22.1 27.9 %copy-start.13 = (f32[384]{0:T(512)S(1)}, f32[384]{0:T(512)}, u32[]{:S(2)}) copy-start(f32[384]{0:T(512)} %param.31) | copy-start | bytes 4612
  22.1 27.9 %copy-start.14 = (f32[384]{0:T(512)S(1)}, f32[384]{0:T(512)}, u32[]{:S(2)}) copy-start(f32[384]{0:T(512)} %param.32) | copy-start | bytes 4612
  22.1 27.9 %copy-start.15 = (f32[384]{0:T(512)S(1)}, f32[384]{0:T(512)}, u32[]{:S(2)}) copy-start(f32[384]{0:T(512)} %param.33) | copy-start | bytes 4612
  22.2 28.0 %copy-start.10 = (f32[384]{0:T(512)S(1)}, f32[384]{0:T(512)}, u32[]{:S(2)}) copy-start(f32[384]{0:T(512)} %param.35) | copy-start | bytes 4612
  28.0 5.8 %collective-permute-start.3 = (bf16[88,384]{1,0:T(8,128)(2,1)S(1)}, bf16[88,384]{1,0:T(8,128)(2,1)S(1)}, u32[]{:S(2)}, u32[]{:S(2)}) collective-permute-start(bf16[88,384]{1,0:T(8,128)(2,1)S(1)} %pad_maximum_fusion.1), channel_id=1, source_target_pairs={{0,8},{1,9},{2,10},{3,11},{4,12},{5,13},{6,14},{7,15},{8,16},{9,17... | collective-permute-start | bytes 202760 | tf_op jit(solution)/shard_map/ppermute | solution.py:372
  31.9 4.4 %collective-permute-start.4 = (bf16[88,384]{1,0:T(8,128)(2,1)S(1)}, bf16[88,384]{1,0:T(8,128)(2,1)S(1)}, u32[]{:S(2)}, u32[]{:S(2)}) collective-permute-start(bf16[88,384]{1,0:T(8,128)(2,1)S(1)} %pad_maximum_fusion.2), channel_id=1, source_target_pairs={{0,56},{1,57},{2,58},{3,59},{4,60},{5,61},{6,62},{7,63},{8,0},{9,1... | collective-permute-start | bytes 202760 | tf_op jit(solution)/shard_map/ppermute | solution.py:373
  38.7 28.7 %all-to-all-start.1 = ((bf16[8,112,384]{2,1,0:T(8,128)(2,1)}), bf16[8,112,384]{2,1,0:T(8,128)(2,1)S(1)}, u32[]{:S(2)}, u32[]{:S(2)}) async-start(bf16[8,112,384]{2,1,0:T(8,128)(2,1)} %broadcast_in_dim.2), calls=%async_computation.1 | async-start | bytes 1376256 | tf_op jit(solution)/shard_map/all_to_all | solution.py:369
  50.0 72.0 %all-gather.7.cloned.1.call-start = ((), (), s32[]{:S(2)}) async-start(), calls=%async_computation.6 | async-start | bytes 1658880 | tf_op jit(solution)/shard_map/all_gather | solution.py:427
  78.7 2.6 %copy-start.5 = (bf16[4,336,384]{2,1,0:T(8,128)(2,1)S(1)}, bf16[4,336,384]{2,1,0:T(8,128)(2,1)}, u32[]{:S(2)}) copy-start(bf16[4,336,384]{2,1,0:T(8,128)(2,1)} %get-tuple-element.28) | copy-start | bytes 3096580
  104.4 2.6 %copy-start.1 = (bf16[4,336,384]{2,1,0:T(8,128)(2,1)}, bf16[4,336,384]{2,1,0:T(8,128)(2,1)S(1)}, u32[]{:S(2)}) copy-start(bf16[4,336,384]{2,1,0:T(8,128)(2,1)S(1)} %all_to_all.37.own_ref) | copy-start | bytes 3096580
  104.4 2.6 %collective-permute-start.5 = (bf16[4,336,384]{2,1,0:T(8,128)(2,1)S(1)}, bf16[4,336,384]{2,1,0:T(8,128)(2,1)S(1)}, u32[]{:S(2)}, u32[]{:S(2)}) collective-permute-start(bf16[4,336,384]{2,1,0:T(8,128)(2,1)S(1)} %all_to_all.37.own_ref), channel_id=1, source_target_pairs={{0,1},{1,0},{2,3},{3,2},{4,5},{5,4},{6,7},{7,6},{8,9},{9,8},{10,11... | collective-permute-start | bytes 3096584 | tf_op jit(solution)/shard_map/ppermute | solution.py:409
  107.1 1.0 copy-start.4
  122.0 7.7 %collective-permute-start.6 = (bf16[4,432,384]{2,1,0:T(8,128)(2,1)}, bf16[4,432,384]{2,1,0:T(8,128)(2,1)S(1)}, u32[]{:S(2)}, u32[]{:S(2)}) collective-permute-start(bf16[4,432,384]{2,1,0:T(8,128)(2,1)} %bitcast.31), channel_id=1, source_target_pairs={{0,1},{1,0},{2,3},{3,2},{4,5},{5,4},{6,7},{7,6},{8,9},{9,8},{10,11... | collective-permute-start | bytes 3981320 | tf_op jit(solution)/shard_map/ppermute | solution.py:429
  122.3 16.0 %all-to-all-start.3 = ((f32[64,1,128]{2,1,0:T(1,128)}), f32[64,1,128]{2,1,0:T(1,128)S(1)}, u32[]{:S(2)}, u32[]{:S(2)}) async-start(f32[64,1,128]{2,1,0:T(1,128)} %bitcast.42), calls=%async_computation.3 | async-start | bytes 65536 | tf_op jit(solution)/shard_map/all_to_all | solution.py:426
  129.7 1.1 copy-start.2
  147.3 18.4 %copy-start.6 = (bf16[1,1,8,40,384]{4,3,2,1,0:T(8,128)(2,1)S(1)}, bf16[1,1,8,40,384]{4,3,2,1,0:T(8,128)(2,1)}, u32[]{:S(2)}) copy-start(bf16[1,1,8,40,384]{4,3,2,1,0:T(8,128)(2,1)} %param.27) | copy-start | bytes 737284
  (4 other events, 2.9 us)
Sparse Core Ops, SparseCore 0:
  37.2 32.8 all-gather.4
  81.4 28.7 all-gather.6

commit v4 on v3

--- a/solution.py
+++ b/solution.py
@@ -164,7 +164,7 @@
 
 
 def first_act(
-    pos_ref, lat_ref, sums_ref, vectors_ref, lanes_ref, groups_t_ref, squares_t_ref, stack, flat
+    pos_ref, lat0_ref, lat1_ref, lat2_ref, lat3_ref, sums_ref, vectors_ref, lanes_ref, groups_t_ref, squares_t_ref, stack, flat
 ):
     row, col = pos_ref[0] // COLS, pos_ref[0] % COLS
     mean_l, scale_l = merge(sums_ref[...], 320.0 * WG * NY * COLS, groups_t_ref[...], squares_t_ref[...])
@@ -176,8 +176,9 @@
     has_n = (row > 0).astype(F32)
     has_s = (row < NZ - 1).astype(F32)
     flat[...] = jnp.zeros_like(flat)
-    for t in range(NY):
-        act = silu((lat_ref[t].astype(F32) - mean_l) * scale_l + shift_l)
+    for back, lat_ref in enumerate((lat0_ref, lat1_ref, lat2_ref, lat3_ref)):
+        t = (pos_ref[1] + (NY - back)) % NY
+        act = silu((lat_ref[...].astype(F32) - mean_l) * scale_l + shift_l)
         for r in range(-2, ROWS + 2):
             base = GUARD + PITCH * (r + 2)
             if 0 <= r < ROWS:
@@ -220,11 +221,11 @@
             weights[down : down + CH, right : right + 128] = taps[:, 128 * (tap % 4) : 128 * (tap % 4) + 128]
     totals = [None] * NY
     for t in range(NY):
-        for dt in range(3):
+        first = max(0, t + 3 - NY)
+        product = dot(stack[t], weights[:, CH * first :])
+        for dt in range(first, 3):
             to = t + 2 - dt
-            if to >= NY:
-                continue
-            part = dot(stack[t], weights[:, CH * dt : CH * dt + CH])
+            part = product[:, CH * (dt - first) : CH * (dt - first) + CH]
             term = part[0:RING, 0:128]
             for dy in (1, 2):
                 term = term + part[PITCH * dy : PITCH * dy + RING, 128 * dy : 128 * dy + 128]
@@ -248,7 +249,10 @@
     sums_ref[...] = jnp.broadcast_to((mean + squares)[0:1], (SPACE, 128))
 
 
-def assemble_second(pos_ref, own_ref, other_ref, weights):
+def second_conv(
+    pos_ref, field_ref, sums_ref, vectors_ref, own_ref, other_ref, groups_t_ref, squares_t_ref, order_ref, out_ref,
+    weights, flat, stack,
+):
     core = pos_ref[0] % NC
     for mine in range(NC):
 
@@ -264,10 +268,6 @@
                         at = 128 * tap + 16 * (NC * x + 1 - mine)
                         weights[at : at + 16, :] = other_ref[x, source : source + 16, :]
 
-
-def second_conv(
-    pos_ref, field_ref, sums_ref, vectors_ref, weights, groups_t_ref, squares_t_ref, order_ref, out_ref, flat, stack
-):
     row, col = pos_ref[0] // COLS, pos_ref[0] % COLS
     mean_l, scale_l = merge(sums_ref[...], 320.0 * NY * WG, groups_t_ref[...], squares_t_ref[...])
     affine = exact(vectors_ref[...], chosen(pos_ref[1]))
@@ -300,7 +300,7 @@
             out_ref[t, r] = total[PITCH * r : PITCH * r + WIDE].astype(BF)
 
 
-def call(body, outs, scratch, smem, *args):
+def call(body, outs, scratch, smem, *args, flops=0):
     return pl.pallas_call(
         body,
         out_shape=outs,
@@ -308,6 +308,7 @@
         out_specs=jax.tree.map(lambda _: VM, outs),
         scratch_shapes=scratch,
         compiler_params=pltpu.CompilerParams(vmem_limit_bytes=56 * 1024 * 1024),
+        cost_estimate=pl.CostEstimate(flops=flops, bytes_accessed=0, transcendentals=0),
     )(*args)
 
 
@@ -362,17 +363,15 @@
     from_west, from_east = send(east, perm=moved(0, 1)), send(west, perm=moved(0, -1))
     plane_sums = lax.all_to_all(sums, BOTH, 0, 0, tiled=True, axis_index_groups=PLANE)
     sums_rows = call(pool_plane, shape((8, CH), BF), [], 0, plane_sums)
-    from_west, from_east, sums_rows, swapped, packed = lax.optimization_barrier(
-        (from_west, from_east, sums_rows, swapped, by_group(kernel_first))
-    )
-    letter = jnp.concatenate([packed, sums_rows[0:6], swapped], axis=0)
-    got = lax.all_to_all(
-        jnp.broadcast_to(letter[None], (NZ, 112, CH)), "space", 0, 0, tiled=True, axis_index_groups=ALONG_Z
-    )
     from_north = send(jnp.concatenate([placed[240:320], from_west[12:16], from_east[12:16]]), perm=moved(1, 0))
     from_south = send(jnp.concatenate([placed[0:80], from_west[0:4], from_east[0:4]]), perm=moved(-1, 0))
     parcel = jnp.concatenate([placed, from_west, from_east, from_north, from_south], axis=0)
-    frames = lax.all_gather(parcel, "tm")
+    sums_rows, swapped, packed = lax.optimization_barrier((sums_rows, swapped, by_group(kernel_first)))
+    letter = jnp.concatenate([packed, sums_rows[0:6], swapped], axis=0)
+    letters = jnp.broadcast_to(letter[None], (NZ, 112, CH))
+    letters, parcel = lax.optimization_barrier((letters, parcel))
+    got = lax.all_to_all(letters, "space", 0, 0, tiled=True, axis_index_groups=ALONG_Z)
+    later = [lax.ppermute(parcel, "tm", [(t, (t + k) % NY) for t in range(NY)]) for k in range(1, NY)]
     ordered, all_sums = call(
         arrange_first,
         (shape((NX, 336, CH), BF), shape((8, 128), F32)),
@@ -388,14 +387,16 @@
         [pltpu.VMEM((GUARD + (ROWS + 4) * PITCH + GUARD, CH), F32)],
         1,
         pos,
-        frames,
+        parcel,
+        *later,
         all_sums,
         vectors,
         jnp.asarray(CHANNEL_LANES),
         jnp.asarray(GROUPS_OF_LANES),
         jnp.asarray(SQUARES_OF_LANES),
-    )
-    got_second, _ = lax.optimization_barrier((got, stack))
+        flops=int(2e10),
+    )
+    got_second, _ = lax.optimization_barrier((got, ordered))
     ordered_second = call(
         arrange_second,
         shape((432, CH), BF),
@@ -427,17 +428,17 @@
     own_second = lax.all_gather(ordered_second, "space", axis_index_groups=ALONG_X)
     own_second, _ = lax.optimization_barrier((own_second, field))
     other_second = lax.ppermute(own_second, "space", SIBLING)
-    weights_second = call(assemble_second, shape((27 * 128, CH), BF), [], 1, pos, own_second, other_second)
     partial = call(
         second_conv,
         shape((NY, ROWS, WIDE, CH), BF),
-        [pltpu.VMEM((RING, 128), F32), pltpu.VMEM((NY, 384, 9 * 128), BF)],
+        [pltpu.VMEM((27 * 128, CH), BF), pltpu.VMEM((RING, 128), F32), pltpu.VMEM((NY, 384, 9 * 128), BF)],
         1,
         pos,
         field,
         all_sums,
         vectors,
-        weights_second,
+        own_second,
+        other_second,
         jnp.asarray(PART_GROUPS.T),
         jnp.asarray(PART_SQUARES.T),
         jnp.asarray(PART_LANES, BF),

time: 175 us -> 155 us (0.89)
  waiting for transfers between devices: 30.3 us -> 17.5 us
  blocking collectives: 41.4 us -> 35.9 us
  Pallas kernels: 43.3 us -> 38.8 us
  starting transfers between devices: 32.7 us -> 35.4 us
    all_to_all x2, waiting for transfers between devices: 19.8 us -> 13.3 us  [the longest x1 13.3 us: shards(): lax.all_to_all(letters, 'space', 0, 0, tiled=True, axis_index_groups=ALON...]
    all_to_all x1, blocking collectives: 23.1 us -> 17.5 us  [shards(): all_sums = lax.all_to_all(sums, 'space', 0, 0, tiled=True)]
    all_to_all x2, starting transfers between devices: 18.7 us -> 13.3 us  [the longest x1 9.03 us: shards(): lax.all_to_all(letters, 'space', 0, 0, tiled=True, axis_index_groups=ALON...]
    pallas_call x8 -> x7, Pallas kernels: 43.3 us -> 38.8 us  [call(): pl.pallas_call(body, out_shape=outs, in_specs=[SM] * smem + [VM] * (len(a...]
    ppermute x0 -> x3, starting transfers between devices: none -> 4.36 us  [shards(): lax.ppermute(parcel, 'tm', [(t, (t + k) % NY) for t in range(NY)])]
    all_to_all x1, waiting for transfers between devices: 3.59 us -> 0.01 us  [shards(): lax.all_to_all(sums, BOTH, 0, 0, tiled=True, axis_index_groups=PLANE)]
    ppermute x1, starting transfers between devices: 3.84 us -> 7.41 us  [shards(): send(jnp.concatenate([placed[240:320], from_west[12:16], from_east[12:16]...]
    ppermute x1, waiting for transfers between devices: 1.8 us -> 0.01 us  [shards(): send(jnp.concatenate([placed[240:320], from_west[12:16], from_east[12:16]...]
  transfers between devices with their start and end apart: 12 -> 14, of which waited for: 6 -> 3; matrix products, arithmetic and copies ran while one was open for 3% -> 3% of each run, Pallas kernels for 12% -> 18%
where the time goes in v4:
time: 155 us; the launch traced here: 153 us
  Pallas kernels  38.8 us (25%)
  blocking collectives  35.9 us (23%)
  starting transfers between devices  35.4 us (23%)
  waiting for transfers between devices  17.5 us (11%)
  between operations  13.8 us (9%)
  local copies, waits for them, and re-layouts  9.35 us (6%)
  other arithmetic  2.23 us (1%)
    pallas_call x7, Pallas kernels, call(): pl.pallas_call(body, out_shape=outs, in_specs=[SM] * smem + [VM] * (len(a...  38.8 us
    all_to_all x1, blocking collectives, shards(): parts = lax.all_to_all(partial, 'tm', 0, 0, tiled=True)  18.5 us
    all_to_all x1, blocking collectives, shards(): all_sums = lax.all_to_all(sums, 'space', 0, 0, tiled=True)  17.5 us
    all_to_all x1, waiting for transfers between devices, shards(): lax.all_to_all(letters, 'space', 0, 0, tiled=True, axis_index_groups=ALON...  13.3 us
    all_to_all x1, starting transfers between devices, shards(): lax.all_to_all(letters, 'space', 0, 0, tiled=True, axis_index_groups=ALON...  9.03 us
    ppermute x1, starting transfers between devices, shards(): send(jnp.concatenate([placed[240:320], from_west[12:16], from_east[12:16]...  7.41 us
    unnamed x40, local copies, waits for them, and re-layouts  6.57 us
    all_to_all x1, starting transfers between devices, shards(): lax.all_to_all(sums, BOTH, 0, 0, tiled=True, axis_index_groups=PLANE)  5.22 us
  transfers between devices with their start and end apart: 14, of which 3 were waited for; matrix products, arithmetic and copies ran while one was open for 3% of the time, Pallas kernels for 18%

profile of v4, /device:TPU:32, one launch (start us, length us, event | category | flops | bytes accessed | tf_op | source)
XLA Modules:
  0.0 153.0 jit_solution(12571313712124597635)
XLA Ops:
  6.5 3.0 %shard_map.253 = (bf16[320,384]{1,0:T(8,128)(2,1)}, bf16[16,384]{1,0:T(8,128)(2,1)}, bf16[16,384]{1,0:T(8,128)(2,1)}, f32[32,128]{1,0:T(8,128)}) custom-call(bf16[320,384]{1,0:T(8,128)(2,1)} %bitcast.31, bf16[384,384]{1,0:T(8,128)(2,1)} %constant.48.clone.lanes_ref, f32[384,128]{1,0:T(8,128)} %constant.49.clone.groups_ref, ...), custom_call_target="tpu_custom_call" | custom-call | tf_op jit(solution)/shard_map/pallas_call | solution.py:304
  9.5 3.9 %collective-permute-start.2 = (bf16[16,384]{1,0:T(8,128)(2,1)}, bf16[16,384]{1,0:T(8,128)(2,1)S(1)}, u32[]{:S(2)}, u32[]{:S(2)}) collective-permute-start(bf16[16,384]{1,0:T(8,128)(2,1)} %get-tuple-element.28), channel_id=1, source_target_pairs={{0,63},{1,0},{2,1},{3,2},{4,3},{5,4},{6,5},{7,6},{8,7},{9,8},{10,9... | collective-permute-start | bytes 36872 | tf_op jit(solution)/shard_map/ppermute | solution.py:363
  13.4 5.2 %all-to-all-start = ((f32[32,1,128]{2,1,0:T(1,128)}), f32[32,1,128]{2,1,0:T(1,128)S(1)}, u32[]{:S(2)}, u32[]{:S(2)}) async-start(f32[32,1,128]{2,1,0:T(1,128)} %bitcast.42), calls=%async_computation | async-start | bytes 32768 | tf_op jit(solution)/shard_map/all_to_all | solution.py:364
  20.2 0.9 fusion.2
  21.1 1.0 constant_dynamic-update-slice_fusion.4
  22.4 7.4 %collective-permute-start.3 = (bf16[88,384]{1,0:T(8,128)(2,1)S(1)}, bf16[88,384]{1,0:T(8,128)(2,1)S(1)}, u32[]{:S(2)}, u32[]{:S(2)}) collective-permute-start(bf16[88,384]{1,0:T(8,128)(2,1)S(1)} %pad_maximum_fusion.1), channel_id=1, source_target_pairs={{0,8},{1,9},{2,10},{3,11},{4,12},{5,13},{6,14},{7,15},{8,16},{9,17... | collective-permute-start | bytes 202760 | tf_op jit(solution)/shard_map/ppermute | solution.py:366
  30.6 1.4 shard_map.254
  32.7 1.5 collective-permute-done.4
  34.2 1.0 broadcast_in_dim.2
  35.3 9.0 %all-to-all-start.1 = ((bf16[8,112,384]{2,1,0:T(8,128)(2,1)}), bf16[8,112,384]{2,1,0:T(8,128)(2,1)S(1)}, u32[]{:S(2)}, u32[]{:S(2)}) async-start(bf16[8,112,384]{2,1,0:T(8,128)(2,1)} %broadcast_in_dim.2), calls=%async_computation.1 | async-start | bytes 1376256 | tf_op jit(solution)/shard_map/all_to_all | solution.py:373
  44.3 2.0 %collective-permute-start.6 = (bf16[528,384]{1,0:T(8,128)(2,1)S(1)}, bf16[528,384]{1,0:T(8,128)(2,1)S(1)}, u32[]{:S(2)}, u32[]{:S(2)}) collective-permute-start(bf16[528,384]{1,0:T(8,128)(2,1)S(1)} %constant_dynamic-update-slice_fusion.lat0_ref), channel_id=1, source_target_pairs={{0,128},{64,192},{128,0},{192,64},{1,129},{65,193},{129,1},{193,65... | collective-permute-start | bytes 1216520 | tf_op jit(solution)/shard_map/ppermute | solution.py:374
  46.3 2.4 %collective-permute-start.7 = (bf16[528,384]{1,0:T(8,128)(2,1)S(1)}, bf16[528,384]{1,0:T(8,128)(2,1)S(1)}, u32[]{:S(2)}, u32[]{:S(2)}) collective-permute-start(bf16[528,384]{1,0:T(8,128)(2,1)S(1)} %constant_dynamic-update-slice_fusion.lat0_ref), channel_id=1, source_target_pairs={{0,192},{64,0},{128,64},{192,128},{1,193},{65,1},{129,65},{193,129... | collective-permute-start | bytes 1216520 | tf_op jit(solution)/shard_map/ppermute | solution.py:374
  50.0 13.3 %all-to-all-done.1.got_ref = bf16[8,112,384]{2,1,0:T(8,128)(2,1)S(1)} async-done(((bf16[8,112,384]{2,1,0:T(8,128)(2,1)}), bf16[8,112,384]{2,1,0:T(8,128)(2,1)S(1)}, u32[]{:S(2)}, u32[]{:S(2)}) %all-to-all-start.1) | async-done | bytes 688160 | tf_op jit(solution)/shard_map/all_to_all | solution.py:373
  64.1 2.5 %shard_map.255 = (bf16[4,336,384]{2,1,0:T(8,128)(2,1)}, f32[8,128]{1,0:T(8,128)}) custom-call(bf16[8,112,384]{2,1,0:T(8,128)(2,1)} %copy-done, bf16[336,384]{1,0:T(8,128)(2,1)} %constant.53.clone.rows_ref), custom_call_target="tpu_custom_call" | custom-call | tf_op jit(solution)/shard_map/pallas_call | solution.py:304
  66.6 4.2 %all-to-all-start.2 = ((bf16[4,336,384]{2,1,0:T(8,128)(2,1)}), bf16[4,336,384]{2,1,0:T(8,128)(2,1)S(1)}, u32[]{:S(2)}, u32[]{:S(2)}) async-start(bf16[4,336,384]{2,1,0:T(8,128)(2,1)} %get-tuple-element.30), calls=%async_computation.2 | async-start | bytes 2064384 | tf_op jit(solution)/shard_map/all_to_all | solution.py:383
  70.9 2.5 %shard_map.257 = bf16[432,384]{1,0:T(8,128)(2,1)} custom-call(bf16[8,112,384]{2,1,0:T(8,128)(2,1)} %copy-done, bf16[144,128]{1,0:T(8,128)(2,1)} %constant.57.clone.rows_ref, bf16[512,384]{1,0:T(8,128)(2,1)} %constant.58.clone.lanes_ref), custom_call_target="tpu_custom_call" | custom-call | tf_op jit(solution)/shard_map/pallas_call | solution.py:304
  74.5 7.9 %shard_map.256.stack = bf16[4,592,1152]{2,1,0:T(8,128)(2,1)} custom-call(s32[2]{0:T(128)} %pad_add_fusion.pos_ref, bf16[528,384]{1,0:T(8,128)(2,1)} %copy-done.5, bf16[528,384]{1,0:T(8,128)(2,1)} %copy-done.14, bf16[528,384]{1,0:T(8,128)(2,1)} %copy-done.15, bf16[528,384]{1,0:T(8,128)(2,1)} %copy-done.16, f32[8,128]{1,0:T(8,128)} %get-tuple-element.32.sums_ref, ...), custom_call_target="tpu_custom_call" | custom-call | flops 20000000000 | tf_op jit(solution)/shard_map/pallas_call | solution.py:304
  82.6 2.6 %collective-permute-done.8.other_ref = bf16[4,336,384]{2,1,0:T(8,128)(2,1)S(1)} collective-permute-done((bf16[4,336,384]{2,1,0:T(8,128)(2,1)S(1)}, bf16[4,336,384]{2,1,0:T(8,128)(2,1)S(1)}, u32[]{:S(2)}, u32[]{:S(2)}) %collective-permute-start.8) | collective-permute-done | bytes 1032224 | tf_op jit(solution)/shard_map/ppermute | solution.py:410
  85.3 1.0 copy-done.3
  86.3 12.6 %shard_map.258 = (f32[4,496,128]{2,1,0:T(8,128)}, f32[64,128]{1,0:T(8,128)}) custom-call(s32[2]{0:T(128)} %pad_add_fusion.pos_ref, bf16[4,592,1152]{2,1,0:T(8,128)(2,1)} %shard_map.256.stack, bf16[4,336,384]{2,1,0:T(8,128)(2,1)} %copy-done.1, bf16[4,336,384]{2,1,0:T(8,128)(2,1)} %copy-done.3, f32[8,384]{1,0:T(8,128)} %stack.41.vectors_ref, ...), custom_call_target="tpu_custom_call" | custom-call | tf_op jit(solution)/shard_map/pallas_call | solution.py:304
  99.2 17.5 %all_to_all.37 = f32[64,1,128]{2,1,0:T(1,128)} all-to-all(f32[64,1,128]{2,1,0:T(1,128)} %bitcast.40), channel_id=1, replica_groups=mesh['tm'=4,'space'=64] {'space'}, dimensions={0} | all-to-all | bytes 65536 | tf_op jit(solution)/shard_map/all_to_all | solution.py:427
  116.7 1.1 copy-done.2
  117.8 8.9 %shard_map.259 = bf16[4,8,40,384]{3,2,1,0:T(8,128)(2,1)} custom-call(s32[2]{0:T(128)} %pad_add_fusion.pos_ref, f32[4,496,128]{2,1,0:T(8,128)} %get-tuple-element.36.field_ref, f32[64,128]{1,0:T(8,128)} %bitcast.35, f32[8,384]{1,0:T(8,128)} %stack.41.vectors_ref, bf16[4,432,384]{2,1,0:T(8,128)(2,1)} %bitcast.30, bf16[4,432,384]{2,1,0:T(8,128)(2,1)} %copy-done.2, ...), custom_call_target="tpu_custom_call" | custom-call | tf_op jit(solution)/shard_map/pallas_call | solution.py:304
  126.7 18.5 %all_to_all.38 = bf16[4,8,40,384]{3,2,1,0:T(8,128)(2,1)S(1)} all-to-all(bf16[4,8,40,384]{3,2,1,0:T(8,128)(2,1)} %shard_map.259), channel_id=1, replica_groups=mesh['tm'=4,'space'=64] {'tm'}, dimensions={0} | all-to-all | bytes 1966080 | tf_op jit(solution)/shard_map/all_to_all | solution.py:446
  (78 shorter events, 8.0 us)
Async XLA Ops:
  6.5 15.6 %copy-start.7 = (bf16[3,3,3,6,96]{4,3,2,1,0:T(8,128)(2,1)S(1)}, bf16[3,3,3,6,96]{4,3,2,1,0:T(8,128)(2,1)}, u32[]{:S(2)}) copy-start(bf16[3,3,3,6,96]{4,3,2,1,0:T(8,128)(2,1)} %param.30) | copy-start | bytes 93316
  9.5 12.8 %collective-permute-start.1 = (bf16[16,384]{1,0:T(8,128)(2,1)}, bf16[16,384]{1,0:T(8,128)(2,1)S(1)}, u32[]{:S(2)}, u32[]{:S(2)}) collective-permute-start(bf16[16,384]{1,0:T(8,128)(2,1)} %get-tuple-element.27), channel_id=1, source_target_pairs={{0,1},{1,2},{2,3},{3,4},{4,5},{5,6},{6,7},{7,8},{8,9},{9,10},{10,1... | collective-permute-start | bytes 36872 | tf_op jit(solution)/shard_map/ppermute | solution.py:363
  9.5 12.8 %collective-permute-start.2 = (bf16[16,384]{1,0:T(8,128)(2,1)}, bf16[16,384]{1,0:T(8,128)(2,1)S(1)}, u32[]{:S(2)}, u32[]{:S(2)}) collective-permute-start(bf16[16,384]{1,0:T(8,128)(2,1)} %get-tuple-element.28), channel_id=1, source_target_pairs={{0,63},{1,0},{2,1},{3,2},{4,3},{5,4},{6,5},{7,6},{8,7},{9,8},{10,9... | collective-permute-start | bytes 36872 | tf_op jit(solution)/shard_map/ppermute | solution.py:363
  13.4 16.6 %all-to-all-start = ((f32[32,1,128]{2,1,0:T(1,128)}), f32[32,1,128]{2,1,0:T(1,128)S(1)}, u32[]{:S(2)}, u32[]{:S(2)}) async-start(f32[32,1,128]{2,1,0:T(1,128)} %bitcast.42), calls=%async_computation | async-start | bytes 32768 | tf_op jit(solution)/shard_map/all_to_all | solution.py:364
  19.5 12.5 %collective-permute-start = (bf16[64,384]{1,0:T(8,128)(2,1)S(1)}, bf16[64,384]{1,0:T(8,128)(2,1)S(1)}, u32[]{:S(2)}, u32[]{:S(2)}) collective-permute-start(bf16[64,384]{1,0:T(8,128)(2,1)S(1)} %bitcast.39), channel_id=1, source_target_pairs={{0,0},{1,1},{2,2},{3,3},{4,4},{5,5},{6,6},{7,7},{8,8},{9,9},{10,10... | collective-permute-start | bytes 147464 | tf_op jit(solution)/shard_map/ppermute | solution.py:349
  21.1 27.6 %copy-start.9 = (f32[384]{0:T(512)S(1)}, f32[384]{0:T(512)}, u32[]{:S(2)}) copy-start(f32[384]{0:T(512)} %param.28) | copy-start | bytes 4612
  21.1 27.6 %copy-start.10 = (f32[384]{0:T(512)S(1)}, f32[384]{0:T(512)}, u32[]{:S(2)}) copy-start(f32[384]{0:T(512)} %param.29) | copy-start | bytes 4612
  21.1 27.6 %copy-start.11 = (f32[384]{0:T(512)S(1)}, f32[384]{0:T(512)}, u32[]{:S(2)}) copy-start(f32[384]{0:T(512)} %param.31) | copy-start | bytes 4612
  21.1 27.6 %copy-start.12 = (f32[384]{0:T(512)S(1)}, f32[384]{0:T(512)}, u32[]{:S(2)}) copy-start(f32[384]{0:T(512)} %param.32) | copy-start | bytes 4612
  21.1 27.6 %copy-start.13 = (f32[384]{0:T(512)S(1)}, f32[384]{0:T(512)}, u32[]{:S(2)}) copy-start(f32[384]{0:T(512)} %param.33) | copy-start | bytes 4612
  21.1 27.6 %copy-start.8 = (f32[384]{0:T(512)S(1)}, f32[384]{0:T(512)}, u32[]{:S(2)}) copy-start(f32[384]{0:T(512)} %param.35) | copy-start | bytes 4612
  22.4 10.3 %collective-permute-start.3 = (bf16[88,384]{1,0:T(8,128)(2,1)S(1)}, bf16[88,384]{1,0:T(8,128)(2,1)S(1)}, u32[]{:S(2)}, u32[]{:S(2)}) collective-permute-start(bf16[88,384]{1,0:T(8,128)(2,1)S(1)} %pad_maximum_fusion.1), channel_id=1, source_target_pairs={{0,8},{1,9},{2,10},{3,11},{4,12},{5,13},{6,14},{7,15},{8,16},{9,17... | collective-permute-start | bytes 202760 | tf_op jit(solution)/shard_map/ppermute | solution.py:366
  29.8 4.4 %collective-permute-start.4 = (bf16[88,384]{1,0:T(8,128)(2,1)S(1)}, bf16[88,384]{1,0:T(8,128)(2,1)S(1)}, u32[]{:S(2)}, u32[]{:S(2)}) collective-permute-start(bf16[88,384]{1,0:T(8,128)(2,1)S(1)} %pad_maximum_fusion.2), channel_id=1, source_target_pairs={{0,56},{1,57},{2,58},{3,59},{4,60},{5,61},{6,62},{7,63},{8,0},{9,1... | collective-permute-start | bytes 202760 | tf_op jit(solution)/shard_map/ppermute | solution.py:367
  34.2 32.4 %copy-start.5 = (bf16[528,384]{1,0:T(8,128)(2,1)}, bf16[528,384]{1,0:T(8,128)(2,1)S(1)}, u32[]{:S(2)}) copy-start(bf16[528,384]{1,0:T(8,128)(2,1)S(1)} %constant_dynamic-update-slice_fusion.lat0_ref) | copy-start | bytes 1216516
  35.3 28.0 %all-to-all-start.1 = ((bf16[8,112,384]{2,1,0:T(8,128)(2,1)}), bf16[8,112,384]{2,1,0:T(8,128)(2,1)S(1)}, u32[]{:S(2)}, u32[]{:S(2)}) async-start(bf16[8,112,384]{2,1,0:T(8,128)(2,1)} %broadcast_in_dim.2), calls=%async_computation.1 | async-start | bytes 1376256 | tf_op jit(solution)/shard_map/all_to_all | solution.py:373
  44.3 29.1 %collective-permute-start.5 = (bf16[528,384]{1,0:T(8,128)(2,1)S(1)}, bf16[528,384]{1,0:T(8,128)(2,1)S(1)}, u32[]{:S(2)}, u32[]{:S(2)}) collective-permute-start(bf16[528,384]{1,0:T(8,128)(2,1)S(1)} %constant_dynamic-update-slice_fusion.lat0_ref), channel_id=1, source_target_pairs={{0,64},{64,128},{128,192},{192,0},{1,65},{65,129},{129,193},{193,1... | collective-permute-start | bytes 1216520 | tf_op jit(solution)/shard_map/ppermute | solution.py:374
  44.3 29.1 %collective-permute-start.6 = (bf16[528,384]{1,0:T(8,128)(2,1)S(1)}, bf16[528,384]{1,0:T(8,128)(2,1)S(1)}, u32[]{:S(2)}, u32[]{:S(2)}) collective-permute-start(bf16[528,384]{1,0:T(8,128)(2,1)S(1)} %constant_dynamic-update-slice_fusion.lat0_ref), channel_id=1, source_target_pairs={{0,128},{64,192},{128,0},{192,64},{1,129},{65,193},{129,1},{193,65... | collective-permute-start | bytes 1216520 | tf_op jit(solution)/shard_map/ppermute | solution.py:374
  46.3 27.2 %collective-permute-start.7 = (bf16[528,384]{1,0:T(8,128)(2,1)S(1)}, bf16[528,384]{1,0:T(8,128)(2,1)S(1)}, u32[]{:S(2)}, u32[]{:S(2)}) collective-permute-start(bf16[528,384]{1,0:T(8,128)(2,1)S(1)} %constant_dynamic-update-slice_fusion.lat0_ref), channel_id=1, source_target_pairs={{0,192},{64,0},{128,64},{192,128},{1,193},{65,1},{129,65},{193,129... | collective-permute-start | bytes 1216520 | tf_op jit(solution)/shard_map/ppermute | solution.py:374
  66.6 15.7 %all-to-all-start.2 = ((bf16[4,336,384]{2,1,0:T(8,128)(2,1)}), bf16[4,336,384]{2,1,0:T(8,128)(2,1)S(1)}, u32[]{:S(2)}, u32[]{:S(2)}) async-start(bf16[4,336,384]{2,1,0:T(8,128)(2,1)} %get-tuple-element.30), calls=%async_computation.2 | async-start | bytes 2064384 | tf_op jit(solution)/shard_map/all_to_all | solution.py:383
  70.9 28.0 %all-gather.3.cloned.1.call-start = ((), (), s32[]{:S(2)}) async-start(), calls=%async_computation.5 | async-start | bytes 1658880 | tf_op jit(solution)/shard_map/all_gather | solution.py:428
  82.4 2.9 %copy-start.1 = (bf16[4,336,384]{2,1,0:T(8,128)(2,1)}, bf16[4,336,384]{2,1,0:T(8,128)(2,1)S(1)}, u32[]{:S(2)}) copy-start(bf16[4,336,384]{2,1,0:T(8,128)(2,1)S(1)} %all-to-all-done.2.own_ref) | copy-start | bytes 3096580
  82.4 2.9 %collective-permute-start.8 = (bf16[4,336,384]{2,1,0:T(8,128)(2,1)S(1)}, bf16[4,336,384]{2,1,0:T(8,128)(2,1)S(1)}, u32[]{:S(2)}, u32[]{:S(2)}) collective-permute-start(bf16[4,336,384]{2,1,0:T(8,128)(2,1)S(1)} %all-to-all-done.2.own_ref), channel_id=1, source_target_pairs={{0,1},{1,0},{2,3},{3,2},{4,5},{5,4},{6,7},{7,6},{8,9},{9,8},{10,11... | collective-permute-start | bytes 3096584 | tf_op jit(solution)/shard_map/ppermute | solution.py:410
  98.9 17.8 %collective-permute-start.9 = (bf16[4,432,384]{2,1,0:T(8,128)(2,1)}, bf16[4,432,384]{2,1,0:T(8,128)(2,1)S(1)}, u32[]{:S(2)}, u32[]{:S(2)}) collective-permute-start(bf16[4,432,384]{2,1,0:T(8,128)(2,1)} %bitcast.29), channel_id=1, source_target_pairs={{0,1},{1,0},{2,3},{3,2},{4,5},{5,4},{6,7},{7,6},{8,9},{9,8},{10,11... | collective-permute-start | bytes 3981320 | tf_op jit(solution)/shard_map/ppermute | solution.py:430
  126.7 18.6 %copy-start.4 = (bf16[1,1,8,40,384]{4,3,2,1,0:T(8,128)(2,1)S(1)}, bf16[1,1,8,40,384]{4,3,2,1,0:T(8,128)(2,1)}, u32[]{:S(2)}) copy-start(bf16[1,1,8,40,384]{4,3,2,1,0:T(8,128)(2,1)} %param.27) | copy-start | bytes 737284
  (7 other events, 6.4 us)
Sparse Core Ops, SparseCore 0:
  73.5 23.9 all-gather.2

commit v5 on v4

--- a/solution.py
+++ b/solution.py
@@ -13,6 +13,8 @@
 F32 = jnp.float32
 VM = pl.BlockSpec(memory_space=pltpu.VMEM)
 SM = pl.BlockSpec(memory_space=pltpu.SMEM)
+AT = pl.BlockSpec(memory_space=pl.ANY)
+HB = pl.BlockSpec(memory_space=pltpu.HBM)
 HIGH = lax.Precision.HIGHEST
 
 NZ, NX, NC, NY = 8, 4, 2, 4
@@ -160,15 +162,28 @@
     tall_parts = [
         jnp.concatenate([by_part[y][:, 128 * d : 128 * d + 128] for y in range(NY)], axis=1) for d in range(3)
     ]
-    out_ref[...] = dot(jnp.concatenate(tall_parts, axis=0), lanes_ref[...]).astype(BF)
+    rows = [tall_parts[d][16 * k : 16 * k + 16] for k in range(9) for d in range(3)]
+    out_ref[...] = dot(jnp.concatenate(rows, axis=0), lanes_ref[...]).astype(BF)
 
 
 def first_act(
-    pos_ref, lat0_ref, lat1_ref, lat2_ref, lat3_ref, sums_ref, vectors_ref, lanes_ref, groups_t_ref, squares_t_ref, stack, flat
+    pos_ref, lat0_ref, lat1_ref, lat2_ref, lat3_ref, sums_ref, vectors_ref, lanes_ref, groups_t_ref, squares_t_ref,
+    stack_ref, flat, lats, stack, in_sems, out_sems,
 ):
+    arrivals = [
+        pltpu.make_async_copy(lat_ref, lats.at[back], in_sems.at[back])
+        for back, lat_ref in enumerate((lat0_ref, lat1_ref, lat2_ref, lat3_ref))
+    ]
+    for arrival in arrivals:
+        arrival.start()
     row, col = pos_ref[0] // COLS, pos_ref[0] % COLS
     mean_l, scale_l = merge(sums_ref[...], 320.0 * WG * NY * COLS, groups_t_ref[...], squares_t_ref[...])
-    affine = exact(vectors_ref[...], lanes_ref[...])
+    vectors = vectors_ref[...]
+    high = vectors.astype(BF)
+    middle = (vectors - high.astype(F32)).astype(BF)
+    low = (vectors - high.astype(F32) - middle.astype(F32)).astype(BF)
+    lanes = lanes_ref[...]
+    affine = dot(high, lanes) + dot(middle, lanes) + dot(low, lanes)
     scale_l = scale_l * affine[0:1]
     shift_l = affine[1:2]
     has_w = (col > 0).astype(F32)
@@ -176,9 +191,11 @@
     has_n = (row > 0).astype(F32)
     has_s = (row < NZ - 1).astype(F32)
     flat[...] = jnp.zeros_like(flat)
-    for back, lat_ref in enumerate((lat0_ref, lat1_ref, lat2_ref, lat3_ref)):
+    leaving = []
+    for back in range(NY):
         t = (pos_ref[1] + (NY - back)) % NY
-        act = silu((lat_ref[...].astype(F32) - mean_l) * scale_l + shift_l)
+        arrivals[back].wait()
+        act = silu((lats[back].astype(F32) - mean_l) * scale_l + shift_l)
         for r in range(-2, ROWS + 2):
             base = GUARD + PITCH * (r + 2)
             if 0 <= r < ROWS:
@@ -194,34 +211,44 @@
             flat[base - 2 : base, :] = left
         for d in range(3):
             start = GUARD - LEAD + d - 1
-            stack[t, :, CH * d : CH * d + CH] = flat[start : start + FIELD, :].astype(BF)
+            stack[back, :, CH * d : CH * d + CH] = flat[start : start + FIELD, :].astype(BF)
+        leaving.append(pltpu.make_async_copy(stack.at[back], stack_ref.at[t], out_sems.at[back]))
+        leaving[back].start()
+    for leave in leaving:
+        leave.wait()
+
+
+def land(core, own_ref, other_ref, slots, sems):
+    copies = []
+    for x in range(NX):
+        at = NC * x
+        copies.append(pltpu.make_async_copy(own_ref.at[x], slots.at[:, at + core], sems.at[at]))
+        copies.append(pltpu.make_async_copy(other_ref.at[x], slots.at[:, at + 1 - core], sems.at[at + 1]))
+    for copy in copies:
+        copy.start()
+    return copies
 
 
 def first_conv(
-    pos_ref, stack, own_ref, other_ref, vectors_ref, part_ref, part_t_ref, part_squares_ref, spread_ref,
-    out_ref, sums_ref, packed, weights,
+    pos_ref, stack_ref, own_ref, other_ref, vectors_ref, part_ref, part_t_ref, part_squares_ref, spread_ref,
+    out_ref, sums_ref, packed, weights, stack, sems, stack_sems,
 ):
-    core = pos_ref[0] % NC
+    landing = land(pos_ref[0] % NC, own_ref, other_ref, packed, sems)
+    arrivals = [pltpu.make_async_copy(stack_ref.at[t], stack.at[t], stack_sems.at[t]) for t in range(NY)]
+    for arrival in arrivals:
+        arrival.start()
     bias = exact(vectors_ref[...], chosen(pos_ref[1]))[2:3]
-    for mine in range(NC):
-
-        @pl.when(core == mine)
-        def _():
-            for x in range(NX):
-                for g in range(7):
-                    at = 48 * (NC * x + mine)
-                    packed[g, at : at + 48, :] = own_ref[x, 48 * g : 48 * g + 48, :]
-                    at = 48 * (NC * x + 1 - mine)
-                    packed[g, at : at + 48, :] = other_ref[x, 48 * g : 48 * g + 48, :]
-
+    for copy in landing:
+        copy.wait()
     for g in range(7):
-        taps = dot(packed[g], spread_ref[...]).astype(BF)
+        taps = dot(packed[g].reshape(CH, CH), spread_ref[...]).astype(BF)
         for tap in range(4 * g, min(4 * g + 4, 27)):
             down, right = CH * (tap % 3), 128 * (tap // 3)
             weights[down : down + CH, right : right + 128] = taps[:, 128 * (tap % 4) : 128 * (tap % 4) + 128]
     totals = [None] * NY
     for t in range(NY):
         first = max(0, t + 3 - NY)
+        arrivals[t].wait()
         product = dot(stack[t], weights[:, CH * first :])
         for dt in range(first, 3):
             to = t + 2 - dt
@@ -250,24 +277,13 @@
 
 
 def second_conv(
-    pos_ref, field_ref, sums_ref, vectors_ref, own_ref, other_ref, groups_t_ref, squares_t_ref, order_ref, out_ref,
-    weights, flat, stack,
+    pos_ref, field_ref, own_ref, other_ref, sums_ref, vectors_ref, groups_t_ref, squares_t_ref, order_ref, out_ref,
+    weights, flat, stack, field, sems, field_sems,
 ):
-    core = pos_ref[0] % NC
-    for mine in range(NC):
-
-        @pl.when(core == mine)
-        def _():
-            for x in range(NX):
-                for d in range(3):
-                    for k in range(9):
-                        tap = 9 * (k // 3) + 3 * (k % 3) + d
-                        source = 144 * d + 16 * k
-                        at = 128 * tap + 16 * (NC * x + mine)
-                        weights[at : at + 16, :] = own_ref[x, source : source + 16, :]
-                        at = 128 * tap + 16 * (NC * x + 1 - mine)
-                        weights[at : at + 16, :] = other_ref[x, source : source + 16, :]
-
+    arrivals = [pltpu.make_async_copy(field_ref.at[t], field.at[t], field_sems.at[t]) for t in range(NY)]
+    for arrival in arrivals:
+        arrival.start()
+    landing = land(pos_ref[0] % NC, own_ref, other_ref, weights, sems)
     row, col = pos_ref[0] // COLS, pos_ref[0] % COLS
     mean_l, scale_l = merge(sums_ref[...], 320.0 * NY * WG, groups_t_ref[...], squares_t_ref[...])
     affine = exact(vectors_ref[...], chosen(pos_ref[1]))
@@ -281,33 +297,36 @@
     outside = outside | (at == WIDE) & (col == COLS - 1) | (at == PITCH - 1) & (col == 0)
     keep = 1.0 - outside.astype(F32)
     for t in range(NY):
-        act = silu((field_ref[t] - mean_l) * scale_l + shift_l) * keep
+        arrivals[t].wait()
+        act = silu((field[t] - mean_l) * scale_l + shift_l) * keep
         flat[...] = dot(act.astype(BF), order_ref[...])
         for dy in range(3):
             for dx in range(3):
                 start = LEAD + PITCH * dy + dx - 1
                 lane = 128 * (3 * dy + dx)
                 stack[t, :, lane : lane + 128] = flat[start : start + 384, :].astype(BF)
+    for copy in landing:
+        copy.wait()
     for t in range(NY):
         total = None
         for dt in range(3):
             source = t - 2 + dt
             if source < 0:
                 continue
-            term = dot(stack[source], weights[1152 * dt : 1152 * dt + 1152, :])
+            term = dot(stack[source], weights[9 * dt : 9 * dt + 9].reshape(1152, CH))
             total = term if total is None else total + term
         for r in range(ROWS):
             out_ref[t, r] = total[PITCH * r : PITCH * r + WIDE].astype(BF)
 
 
-def call(body, outs, scratch, smem, *args, flops=0):
+def call(body, outs, scratch, places, *args, flops=0, out_places=None, grant=50):
     return pl.pallas_call(
         body,
         out_shape=outs,
-        in_specs=[SM] * smem + [VM] * (len(args) - smem),
-        out_specs=jax.tree.map(lambda _: VM, outs),
+        in_specs=[*places, *[VM] * (len(args) - len(places))],
+        out_specs=jax.tree.map(lambda _: VM, outs) if out_places is None else out_places,
         scratch_shapes=scratch,
-        compiler_params=pltpu.CompilerParams(vmem_limit_bytes=56 * 1024 * 1024),
+        compiler_params=pltpu.CompilerParams(vmem_limit_bytes=grant * 1024 * 1024),
         cost_estimate=pl.CostEstimate(flops=flops, bytes_accessed=0, transcendentals=0),
     )(*args)
 
@@ -351,18 +370,19 @@
         measure_tile,
         (shape((320, CH), BF), shape((16, CH), BF), shape((16, CH), BF), shape((NY * COLS, 128), F32)),
         [],
-        0,
+        [],
         flat_tile,
         jnp.asarray(CHANNEL_LANES, BF),
         jnp.asarray(GROUPS_OF),
         jnp.asarray(GROUPS_OF.T),
         jnp.asarray(SQUARES_OF),
         jnp.asarray(EDGES, BF),
+        grant=60,
     )
     send = functools.partial(lax.ppermute, axis_name="space")
     from_west, from_east = send(east, perm=moved(0, 1)), send(west, perm=moved(0, -1))
     plane_sums = lax.all_to_all(sums, BOTH, 0, 0, tiled=True, axis_index_groups=PLANE)
-    sums_rows = call(pool_plane, shape((8, CH), BF), [], 0, plane_sums)
+    sums_rows = call(pool_plane, shape((8, CH), BF), [], [], plane_sums)
     from_north = send(jnp.concatenate([placed[240:320], from_west[12:16], from_east[12:16]]), perm=moved(1, 0))
     from_south = send(jnp.concatenate([placed[0:80], from_west[0:4], from_east[0:4]]), perm=moved(-1, 0))
     parcel = jnp.concatenate([placed, from_west, from_east, from_north, from_south], axis=0)
@@ -376,7 +396,7 @@
         arrange_first,
         (shape((NX, 336, CH), BF), shape((8, 128), F32)),
         [],
-        0,
+        [],
         got,
         jnp.asarray(FIRST_ROWS, BF),
     )
@@ -384,24 +404,31 @@
     stack = call(
         first_act,
         shape((NY, FIELD, 3 * CH), BF),
-        [pltpu.VMEM((GUARD + (ROWS + 4) * PITCH + GUARD, CH), F32)],
-        1,
+        [
+            pltpu.VMEM((GUARD + (ROWS + 4) * PITCH + GUARD, CH), F32),
+            pltpu.VMEM((NY, 528, CH), BF),
+            pltpu.VMEM((NY, FIELD, 3 * CH), BF),
+            pltpu.SemaphoreType.DMA((NY,)),
+            pltpu.SemaphoreType.DMA((NY,)),
+        ],
+        [SM, AT, AT, AT, AT],
         pos,
         parcel,
         *later,
         all_sums,
         vectors,
-        jnp.asarray(CHANNEL_LANES),
+        jnp.asarray(CHANNEL_LANES, BF),
         jnp.asarray(GROUPS_OF_LANES),
         jnp.asarray(SQUARES_OF_LANES),
         flops=int(2e10),
+        out_places=HB,
     )
     got_second, _ = lax.optimization_barrier((got, ordered))
     ordered_second = call(
         arrange_second,
         shape((432, CH), BF),
         [],
-        0,
+        [],
         got_second,
         jnp.asarray(SECOND_ROWS, BF),
         jnp.asarray(SECOND_LANES, BF),
@@ -412,12 +439,18 @@
     field, sums = call(
         first_conv,
         (shape((NY, RING, 128), F32), shape((SPACE, 128), F32)),
-        [pltpu.VMEM((7, CH, CH), BF), pltpu.VMEM((3 * CH, 9 * 128), BF)],
-        1,
+        [
+            pltpu.VMEM((7, COLS, 48, CH), BF),
+            pltpu.VMEM((3 * CH, 9 * 128), BF),
+            pltpu.VMEM((NY, FIELD, 3 * CH), BF),
+            pltpu.SemaphoreType.DMA((COLS,)),
+            pltpu.SemaphoreType.DMA((NY,)),
+        ],
+        [SM, HB, AT, AT],
         pos,
         stack,
-        own,
-        other,
+        own.reshape(NX, 7, 48, CH),
+        other.reshape(NX, 7, 48, CH),
         vectors,
         jnp.asarray(PART_GROUPS),
         jnp.asarray(PART_GROUPS.T),
@@ -431,17 +464,25 @@
     partial = call(
         second_conv,
         shape((NY, ROWS, WIDE, CH), BF),
-        [pltpu.VMEM((27 * 128, CH), BF), pltpu.VMEM((RING, 128), F32), pltpu.VMEM((NY, 384, 9 * 128), BF)],
-        1,
+        [
+            pltpu.VMEM((27, COLS, 16, CH), BF),
+            pltpu.VMEM((RING, 128), F32),
+            pltpu.VMEM((NY, 384, 9 * 128), BF),
+            pltpu.VMEM((NY, RING, 128), F32),
+            pltpu.SemaphoreType.DMA((COLS,)),
+            pltpu.SemaphoreType.DMA((NY,)),
+        ],
+        [SM, AT, HB, AT],
         pos,
         field,
+        own_second.reshape(NX, 27, 16, CH),
+        other_second.reshape(NX, 27, 16, CH),
         all_sums,
         vectors,
-        own_second,
-        other_second,
         jnp.asarray(PART_GROUPS.T),
         jnp.asarray(PART_SQUARES.T),
         jnp.asarray(PART_LANES, BF),
+        grant=46,
     )
     parts = lax.all_to_all(partial, "tm", 0, 0, tiled=True)
     second_out = jnp.sum(parts.astype(F32), axis=0) + bias_second

time: 155 us -> 151 us (0.974)
  waiting for transfers between devices: 17.5 us -> 25.3 us
  Pallas kernels: 38.8 us -> 31.2 us
  local copies, waits for them, and re-layouts: 9.35 us -> 6.3 us
    pallas_call x7, Pallas kernels: 38.8 us -> 31.2 us  [call(): pl.pallas_call(body, out_shape=outs, in_specs=[*places, *[VM] * (len(args...]
    all_to_all x1, waiting for transfers between devices: 0.01 us -> 2.82 us  [shards(): lax.all_to_all(ordered, 'space', 0, 0, tiled=True, axis_index_groups=ALON...]
    unnamed x40 -> x48, local copies, waits for them, and re-layouts: 6.57 us -> 4.24 us
    all_gather x1, waiting for transfers between devices: 0.01 us -> 2.18 us  [shards(): lax.all_gather(ordered_second, 'space', axis_index_groups=ALONG_X)]
    ppermute x1, waiting for transfers between devices: 0.01 us -> 1.65 us  [shards(): send(jnp.concatenate([placed[240:320], from_west[12:16], from_east[12:16]...]
  transfers between devices with their start and end apart: 14 -> 14, of which waited for: 3 -> 6; matrix products, arithmetic and copies ran while one was open for 3% -> 2% of each run, Pallas kernels for 18% -> 13%
where the time goes in v5:
time: 151 us; the launch traced here: 150 us
  blocking collectives  36.9 us (24%)
  starting transfers between devices  35.1 us (23%)
  Pallas kernels  31.2 us (21%)
  waiting for transfers between devices  25.3 us (17%)
  between operations  13.8 us (9%)
  local copies, waits for them, and re-layouts  6.3 us (4%)
    pallas_call x7, Pallas kernels, call(): pl.pallas_call(body, out_shape=outs, in_specs=[*places, *[VM] * (len(args...  31.2 us
    all_to_all x1, blocking collectives, shards(): parts = lax.all_to_all(partial, 'tm', 0, 0, tiled=True)  18.6 us
    all_to_all x1, blocking collectives, shards(): all_sums = lax.all_to_all(sums, 'space', 0, 0, tiled=True)  18.3 us
    all_to_all x1, waiting for transfers between devices, shards(): lax.all_to_all(letters, 'space', 0, 0, tiled=True, axis_index_groups=ALON...  13.6 us
    all_to_all x1, starting transfers between devices, shards(): lax.all_to_all(letters, 'space', 0, 0, tiled=True, axis_index_groups=ALON...  9.16 us
    ppermute x1, starting transfers between devices, shards(): send(jnp.concatenate([placed[240:320], from_west[12:16], from_east[12:16]...  7.41 us
    all_to_all x1, starting transfers between devices, shards(): lax.all_to_all(sums, BOTH, 0, 0, tiled=True, axis_index_groups=PLANE)  5.22 us
    all_to_all x1, starting transfers between devices, shards(): lax.all_to_all(ordered, 'space', 0, 0, tiled=True, axis_index_groups=ALON...  4.38 us
  transfers between devices with their start and end apart: 14, of which 6 were waited for; matrix products, arithmetic and copies ran while one was open for 2% of the time, Pallas kernels for 13%

profile of v5, /device:TPU:32, one launch (start us, length us, event | category | flops | bytes accessed | tf_op | source)
XLA Modules:
  0.0 149.7 jit_solution(9968738411059376177)
XLA Ops:
  6.5 3.0 %shard_map.253 = (bf16[320,384]{1,0:T(8,128)(2,1)}, bf16[16,384]{1,0:T(8,128)(2,1)}, bf16[16,384]{1,0:T(8,128)(2,1)}, f32[32,128]{1,0:T(8,128)}) custom-call(bf16[320,384]{1,0:T(8,128)(2,1)} %bitcast.42, bf16[384,384]{1,0:T(8,128)(2,1)} %constant.46.clone.lanes_ref, f32[384,128]{1,0:T(8,128)} %constant.47.clone.groups_ref, ...), custom_call_target="tpu_custom_call" | custom-call | tf_op jit(solution)/shard_map/pallas_call | solution.py:323
  9.5 3.9 %collective-permute-start.2 = (bf16[16,384]{1,0:T(8,128)(2,1)}, bf16[16,384]{1,0:T(8,128)(2,1)S(1)}, u32[]{:S(2)}, u32[]{:S(2)}) collective-permute-start(bf16[16,384]{1,0:T(8,128)(2,1)} %get-tuple-element.28), channel_id=1, source_target_pairs={{0,63},{1,0},{2,1},{3,2},{4,3},{5,4},{6,5},{7,6},{8,7},{9,8},{10,9... | collective-permute-start | bytes 36872 | tf_op jit(solution)/shard_map/ppermute | solution.py:383
  13.4 5.2 %all-to-all-start = ((f32[32,1,128]{2,1,0:T(1,128)}), f32[32,1,128]{2,1,0:T(1,128)S(1)}, u32[]{:S(2)}, u32[]{:S(2)}) async-start(f32[32,1,128]{2,1,0:T(1,128)} %bitcast.49), calls=%async_computation | async-start | bytes 32768 | tf_op jit(solution)/shard_map/all_to_all | solution.py:384
  21.2 1.0 constant_dynamic-update-slice_fusion.4
  22.5 7.4 %collective-permute-start.3 = (bf16[88,384]{1,0:T(8,128)(2,1)S(1)}, bf16[88,384]{1,0:T(8,128)(2,1)S(1)}, u32[]{:S(2)}, u32[]{:S(2)}) collective-permute-start(bf16[88,384]{1,0:T(8,128)(2,1)S(1)} %pad_maximum_fusion.1), channel_id=1, source_target_pairs={{0,8},{1,9},{2,10},{3,11},{4,12},{5,13},{6,14},{7,15},{8,16},{9,17... | collective-permute-start | bytes 202760 | tf_op jit(solution)/shard_map/ppermute | solution.py:386
  30.1 1.7 %collective-permute-done.3 = bf16[88,384]{1,0:T(8,128)(2,1)S(1)} collective-permute-done((bf16[88,384]{1,0:T(8,128)(2,1)S(1)}, bf16[88,384]{1,0:T(8,128)(2,1)S(1)}, u32[]{:S(2)}, u32[]{:S(2)}) %collective-permute-start.3) | collective-permute-done | bytes 67616 | tf_op jit(solution)/shard_map/ppermute | solution.py:386
  31.8 2.4 %collective-permute-done.4 = bf16[88,384]{1,0:T(8,128)(2,1)S(1)} collective-permute-done((bf16[88,384]{1,0:T(8,128)(2,1)S(1)}, bf16[88,384]{1,0:T(8,128)(2,1)S(1)}, u32[]{:S(2)}, u32[]{:S(2)}) %collective-permute-start.4) | collective-permute-done | bytes 67616 | tf_op jit(solution)/shard_map/ppermute | solution.py:387
  35.2 9.2 %all-to-all-start.1 = ((bf16[8,112,384]{2,1,0:T(8,128)(2,1)}), bf16[8,112,384]{2,1,0:T(8,128)(2,1)S(1)}, u32[]{:S(2)}, u32[]{:S(2)}) async-start(bf16[8,112,384]{2,1,0:T(8,128)(2,1)} %broadcast_in_dim.2), calls=%async_computation.1 | async-start | bytes 1376256 | tf_op jit(solution)/shard_map/all_to_all | solution.py:393
  44.3 2.0 %collective-permute-start.6 = (bf16[528,384]{1,0:T(8,128)(2,1)S(1)}, bf16[528,384]{1,0:T(8,128)(2,1)}, u32[]{:S(2)}, u32[]{:S(2)}) collective-permute-start(bf16[528,384]{1,0:T(8,128)(2,1)S(1)} %constant_dynamic-update-slice_fusion.lat0_ref), channel_id=1, source_target_pairs={{0,128},{64,192},{128,0},{192,64},{1,129},{65,193},{129,1},{193,65... | collective-permute-start | bytes 1216520 | tf_op jit(solution)/shard_map/ppermute | solution.py:394
  46.3 2.4 %collective-permute-start.7 = (bf16[528,384]{1,0:T(8,128)(2,1)S(1)}, bf16[528,384]{1,0:T(8,128)(2,1)}, u32[]{:S(2)}, u32[]{:S(2)}) collective-permute-start(bf16[528,384]{1,0:T(8,128)(2,1)S(1)} %constant_dynamic-update-slice_fusion.lat0_ref), channel_id=1, source_target_pairs={{0,192},{64,0},{128,64},{192,128},{1,193},{65,1},{129,65},{193,129... | collective-permute-start | bytes 1216520 | tf_op jit(solution)/shard_map/ppermute | solution.py:394
  48.9 13.6 %all-to-all-done.1.got_ref = bf16[8,112,384]{2,1,0:T(8,128)(2,1)S(1)} async-done(((bf16[8,112,384]{2,1,0:T(8,128)(2,1)}), bf16[8,112,384]{2,1,0:T(8,128)(2,1)S(1)}, u32[]{:S(2)}, u32[]{:S(2)}) %all-to-all-start.1) | async-done | bytes 688160 | tf_op jit(solution)/shard_map/all_to_all | solution.py:393
  62.5 1.4 shard_map.255
  63.8 4.4 %all-to-all-start.2 = ((bf16[4,336,384]{2,1,0:T(8,128)(2,1)}), bf16[4,336,384]{2,1,0:T(8,128)(2,1)S(1)}, u32[]{:S(2)}, u32[]{:S(2)}) async-start(bf16[4,336,384]{2,1,0:T(8,128)(2,1)} %get-tuple-element.30), calls=%async_computation.2 | async-start | bytes 2064384 | tf_op jit(solution)/shard_map/all_to_all | solution.py:403
  68.2 1.3 shard_map.257
  69.6 0.9 copy-done.12
  70.5 5.7 %shard_map.256.stack_ref = bf16[4,592,1152]{2,1,0:T(8,128)(2,1)} custom-call(s32[2]{0:T(128)S(1)} %pad_add_fusion.pos_ref, bf16[528,384]{1,0:T(8,128)(2,1)S(1)} %constant_dynamic-update-slice_fusion.lat0_ref, bf16[528,384]{1,0:T(8,128)(2,1)S(1)} %collective-permute-done.5.lat1_ref, bf16[528,384]{1,0:T(8,128)(2,1)} %collective-permute-done.6.lat2_ref, ...), custom_call_target="tpu_custom_call" | custom-call | flops 20000000000 | tf_op jit(solution)/shard_map/pallas_call | solution.py:323
  76.2 2.8 %all-to-all-done.2 = bf16[4,336,384]{2,1,0:T(8,128)(2,1)S(1)} async-done(((bf16[4,336,384]{2,1,0:T(8,128)(2,1)}), bf16[4,336,384]{2,1,0:T(8,128)(2,1)S(1)}, u32[]{:S(2)}, u32[]{:S(2)}) %all-to-all-start.2) | async-done | bytes 1032224 | tf_op jit(solution)/shard_map/all_to_all | solution.py:403
  79.0 2.6 %collective-permute-done.8 = bf16[4,336,384]{2,1,0:T(8,128)(2,1)S(1)} collective-permute-done((bf16[4,336,384]{2,1,0:T(8,128)(2,1)S(1)}, bf16[4,336,384]{2,1,0:T(8,128)(2,1)S(1)}, u32[]{:S(2)}, u32[]{:S(2)}) %collective-permute-start.8) | collective-permute-done | bytes 1032224 | tf_op jit(solution)/shard_map/ppermute | solution.py:437
  81.7 11.2 %shard_map.258 = (f32[4,496,128]{2,1,0:T(8,128)S(1)}, f32[64,128]{1,0:T(8,128)S(1)}) custom-call(s32[2]{0:T(128)S(1)} %pad_add_fusion.pos_ref, bf16[4,592,1152]{2,1,0:T(8,128)(2,1)} %shard_map.256.stack_ref, bf16[4,7,48,384]{3,2,1,0:T(8,128)(2,1)S(1)} %bitcast.33, bf16[4,7,48,384]{3,2,1,0:T(8,128)(2,1)S(1)} %bitcast.37, f32[8,384]{1,0:T(8,128)S(1)} %stack.41.vectors_ref, ...), custom_call_target="tpu_custom_call" | custom-call | tf_op jit(solution)/shard_map/pallas_call | solution.py:323
  92.9 2.2 %all-gather.3.cloned.1.call-done = bf16[1728,384]{1,0:T(8,128)(2,1)} async-done(((bf16[432,384]{1,0:T(8,128)(2,1)}), bf16[1728,384]{1,0:T(8,128)(2,1)}) %all-gather.3.cloned.1.call-update) | async-done | bytes 1327120 | tf_op jit(solution)/shard_map/all_gather | solution.py:461
  95.1 18.3 %all_to_all.37 = f32[64,1,128]{2,1,0:T(1,128)S(1)} all-to-all(f32[64,1,128]{2,1,0:T(1,128)S(1)} %bitcast.40), channel_id=1, replica_groups=mesh['tm'=4,'space'=64] {'space'}, dimensions={0} | all-to-all | bytes 65536 | tf_op jit(solution)/shard_map/all_to_all | solution.py:460
  113.5 1.3 copy-done
  114.8 8.6 %shard_map.259 = bf16[4,8,40,384]{3,2,1,0:T(8,128)(2,1)S(1)} custom-call(s32[2]{0:T(128)S(1)} %pad_add_fusion.pos_ref, f32[4,496,128]{2,1,0:T(8,128)S(1)} %get-tuple-element.36.field_ref, bf16[4,27,16,384]{3,2,1,0:T(8,128)(2,1)S(1)} %bitcast.35, bf16[4,27,16,384]{3,2,1,0:T(8,128)(2,1)S(1)} %bitcast.36, f32[64,128]{1,0:T(8,128)S(1)} %bitcast.38, ...), custom_call_target="tpu_custom_call" | custom-call | tf_op jit(solution)/shard_map/pallas_call | solution.py:323
  123.4 18.6 %all_to_all.38 = bf16[4,8,40,384]{3,2,1,0:T(8,128)(2,1)S(1)} all-to-all(bf16[4,8,40,384]{3,2,1,0:T(8,128)(2,1)S(1)} %shard_map.259), channel_id=1, replica_groups=mesh['tm'=4,'space'=64] {'tm'}, dimensions={0} | all-to-all | bytes 1966080 | tf_op jit(solution)/shard_map/all_to_all | solution.py:487
  (86 shorter events, 5.0 us)
Async XLA Ops:
  9.5 12.9 %collective-permute-start.1 = (bf16[16,384]{1,0:T(8,128)(2,1)}, bf16[16,384]{1,0:T(8,128)(2,1)S(1)}, u32[]{:S(2)}, u32[]{:S(2)}) collective-permute-start(bf16[16,384]{1,0:T(8,128)(2,1)} %get-tuple-element.27), channel_id=1, source_target_pairs={{0,1},{1,2},{2,3},{3,4},{4,5},{5,6},{6,7},{7,8},{8,9},{9,10},{10,1... | collective-permute-start | bytes 36872 | tf_op jit(solution)/shard_map/ppermute | solution.py:383
  9.5 12.9 %collective-permute-start.2 = (bf16[16,384]{1,0:T(8,128)(2,1)}, bf16[16,384]{1,0:T(8,128)(2,1)S(1)}, u32[]{:S(2)}, u32[]{:S(2)}) collective-permute-start(bf16[16,384]{1,0:T(8,128)(2,1)} %get-tuple-element.28), channel_id=1, source_target_pairs={{0,63},{1,0},{2,1},{3,2},{4,3},{5,4},{6,5},{7,6},{8,7},{9,8},{10,9... | collective-permute-start | bytes 36872 | tf_op jit(solution)/shard_map/ppermute | solution.py:383
  13.4 16.6 %all-to-all-start = ((f32[32,1,128]{2,1,0:T(1,128)}), f32[32,1,128]{2,1,0:T(1,128)S(1)}, u32[]{:S(2)}, u32[]{:S(2)}) async-start(f32[32,1,128]{2,1,0:T(1,128)} %bitcast.49), calls=%async_computation | async-start | bytes 32768 | tf_op jit(solution)/shard_map/all_to_all | solution.py:384
  19.5 10.6 %collective-permute-start = (bf16[64,384]{1,0:T(8,128)(2,1)S(1)}, bf16[64,384]{1,0:T(8,128)(2,1)S(1)}, u32[]{:S(2)}, u32[]{:S(2)}) collective-permute-start(bf16[64,384]{1,0:T(8,128)(2,1)S(1)} %bitcast.48), channel_id=1, source_target_pairs={{0,0},{1,1},{2,2},{3,3},{4,4},{5,5},{6,6},{7,7},{8,8},{9,9},{10,10... | collective-permute-start | bytes 147464 | tf_op jit(solution)/shard_map/ppermute | solution.py:368
  21.1 27.6 %copy-start.16 = (f32[384]{0:T(512)S(1)}, f32[384]{0:T(512)}, u32[]{:S(2)}) copy-start(f32[384]{0:T(512)} %param.28) | copy-start | bytes 4612
  21.1 27.6 %copy-start.17 = (f32[384]{0:T(512)S(1)}, f32[384]{0:T(512)}, u32[]{:S(2)}) copy-start(f32[384]{0:T(512)} %param.29) | copy-start | bytes 4612
  21.1 27.6 %copy-start.19 = (f32[384]{0:T(512)S(1)}, f32[384]{0:T(512)}, u32[]{:S(2)}) copy-start(f32[384]{0:T(512)} %param.32) | copy-start | bytes 4612
  21.1 27.6 %copy-start.20 = (f32[384]{0:T(512)S(1)}, f32[384]{0:T(512)}, u32[]{:S(2)}) copy-start(f32[384]{0:T(512)} %param.33) | copy-start | bytes 4612
  21.1 27.6 %copy-start.15 = (f32[384]{0:T(512)S(1)}, f32[384]{0:T(512)}, u32[]{:S(2)}) copy-start(f32[384]{0:T(512)} %param.35) | copy-start | bytes 4612
  21.1 41.3 %copy-start.5 = (bf16[336,384]{1,0:T(8,128)(2,1)S(1)}, bf16[336,384]{1,0:T(8,128)(2,1)}, u32[]{:S(2)}) copy-start(bf16[336,384]{1,0:T(8,128)(2,1)} %constant.51.clone.rows_ref) | copy-start | bytes 774148
  22.5 9.3 %collective-permute-start.3 = (bf16[88,384]{1,0:T(8,128)(2,1)S(1)}, bf16[88,384]{1,0:T(8,128)(2,1)S(1)}, u32[]{:S(2)}, u32[]{:S(2)}) collective-permute-start(bf16[88,384]{1,0:T(8,128)(2,1)S(1)} %pad_maximum_fusion.1), channel_id=1, source_target_pairs={{0,8},{1,9},{2,10},{3,11},{4,12},{5,13},{6,14},{7,15},{8,16},{9,17... | collective-permute-start | bytes 202760 | tf_op jit(solution)/shard_map/ppermute | solution.py:386
  29.9 4.4 %collective-permute-start.4 = (bf16[88,384]{1,0:T(8,128)(2,1)S(1)}, bf16[88,384]{1,0:T(8,128)(2,1)S(1)}, u32[]{:S(2)}, u32[]{:S(2)}) collective-permute-start(bf16[88,384]{1,0:T(8,128)(2,1)S(1)} %pad_maximum_fusion.2), channel_id=1, source_target_pairs={{0,56},{1,57},{2,58},{3,59},{4,60},{5,61},{6,62},{7,63},{8,0},{9,1... | collective-permute-start | bytes 202760 | tf_op jit(solution)/shard_map/ppermute | solution.py:387
  35.2 33.1 %copy-start.2 = (bf16[512,384]{1,0:T(8,128)(2,1)S(1)}, bf16[512,384]{1,0:T(8,128)(2,1)}, u32[]{:S(2)}) copy-start(bf16[512,384]{1,0:T(8,128)(2,1)} %constant.55.clone.lanes_ref) | copy-start | bytes 1179652
  35.2 33.1 %copy-start.9 = (bf16[144,128]{1,0:T(8,128)(2,1)S(1)}, bf16[144,128]{1,0:T(8,128)(2,1)}, u32[]{:S(2)}) copy-start(bf16[144,128]{1,0:T(8,128)(2,1)} %constant.54.clone.rows_ref) | copy-start | bytes 110596
  35.2 27.3 %all-to-all-start.1 = ((bf16[8,112,384]{2,1,0:T(8,128)(2,1)}), bf16[8,112,384]{2,1,0:T(8,128)(2,1)S(1)}, u32[]{:S(2)}, u32[]{:S(2)}) async-start(bf16[8,112,384]{2,1,0:T(8,128)(2,1)} %broadcast_in_dim.2), calls=%async_computation.1 | async-start | bytes 1376256 | tf_op jit(solution)/shard_map/all_to_all | solution.py:393
  44.3 25.2 %collective-permute-start.5 = (bf16[528,384]{1,0:T(8,128)(2,1)S(1)}, bf16[528,384]{1,0:T(8,128)(2,1)S(1)}, u32[]{:S(2)}, u32[]{:S(2)}) collective-permute-start(bf16[528,384]{1,0:T(8,128)(2,1)S(1)} %constant_dynamic-update-slice_fusion.lat0_ref), channel_id=1, source_target_pairs={{0,64},{64,128},{128,192},{192,0},{1,65},{65,129},{129,193},{193,1... | collective-permute-start | bytes 1216520 | tf_op jit(solution)/shard_map/ppermute | solution.py:394
  44.3 25.2 %collective-permute-start.6 = (bf16[528,384]{1,0:T(8,128)(2,1)S(1)}, bf16[528,384]{1,0:T(8,128)(2,1)}, u32[]{:S(2)}, u32[]{:S(2)}) collective-permute-start(bf16[528,384]{1,0:T(8,128)(2,1)S(1)} %constant_dynamic-update-slice_fusion.lat0_ref), channel_id=1, source_target_pairs={{0,128},{64,192},{128,0},{192,64},{1,129},{65,193},{129,1},{193,65... | collective-permute-start | bytes 1216520 | tf_op jit(solution)/shard_map/ppermute | solution.py:394
  46.3 23.3 %collective-permute-start.7 = (bf16[528,384]{1,0:T(8,128)(2,1)S(1)}, bf16[528,384]{1,0:T(8,128)(2,1)}, u32[]{:S(2)}, u32[]{:S(2)}) collective-permute-start(bf16[528,384]{1,0:T(8,128)(2,1)S(1)} %constant_dynamic-update-slice_fusion.lat0_ref), channel_id=1, source_target_pairs={{0,192},{64,0},{128,64},{192,128},{1,193},{65,1},{129,65},{193,129... | collective-permute-start | bytes 1216520 | tf_op jit(solution)/shard_map/ppermute | solution.py:394
  63.8 15.2 %all-to-all-start.2 = ((bf16[4,336,384]{2,1,0:T(8,128)(2,1)}), bf16[4,336,384]{2,1,0:T(8,128)(2,1)S(1)}, u32[]{:S(2)}, u32[]{:S(2)}) async-start(bf16[4,336,384]{2,1,0:T(8,128)(2,1)} %get-tuple-element.30), calls=%async_computation.2 | async-start | bytes 2064384 | tf_op jit(solution)/shard_map/all_to_all | solution.py:403
  68.2 26.9 %all-gather.3.cloned.1.call-start = ((), (), s32[]{:S(2)}) async-start(), calls=%async_computation.5 | async-start | bytes 1658880 | tf_op jit(solution)/shard_map/all_gather | solution.py:461
  79.0 2.6 %collective-permute-start.8 = (bf16[4,336,384]{2,1,0:T(8,128)(2,1)S(1)}, bf16[4,336,384]{2,1,0:T(8,128)(2,1)S(1)}, u32[]{:S(2)}, u32[]{:S(2)}) collective-permute-start(bf16[4,336,384]{2,1,0:T(8,128)(2,1)S(1)} %all-to-all-done.2), channel_id=1, source_target_pairs={{0,1},{1,0},{2,3},{3,2},{4,5},{5,4},{6,7},{7,6},{8,9},{9,8},{10,11... | collective-permute-start | bytes 3096584 | tf_op jit(solution)/shard_map/ppermute | solution.py:437
  81.7 31.8 %copy-start.6 = (f32[128,128]{1,0:T(8,128)S(1)}, f32[128,128]{1,0:T(8,128)}, u32[]{:S(2)}) copy-start(f32[128,128]{1,0:T(8,128)} %constant.60.clone.squares_t_ref) | copy-start | bytes 196612
  81.7 31.7 %copy-start.10 = (bf16[128,128]{1,0:T(8,128)(2,1)S(1)}, bf16[128,128]{1,0:T(8,128)(2,1)}, u32[]{:S(2)}) copy-start(bf16[128,128]{1,0:T(8,128)(2,1)} %constant.61.clone.order_ref) | copy-start | bytes 98308
  95.1 18.3 %collective-permute-start.9 = (bf16[4,432,384]{2,1,0:T(8,128)(2,1)}, bf16[4,432,384]{2,1,0:T(8,128)(2,1)S(1)}, u32[]{:S(2)}, u32[]{:S(2)}) collective-permute-start(bf16[4,432,384]{2,1,0:T(8,128)(2,1)} %bitcast.34), channel_id=1, source_target_pairs={{0,1},{1,0},{2,3},{3,2},{4,5},{5,4},{6,7},{7,6},{8,9},{9,8},{10,11... | collective-permute-start | bytes 3981320 | tf_op jit(solution)/shard_map/ppermute | solution.py:463
  (11 other events, 120.3 us)
Sparse Core Ops, SparseCore 0:
  70.8 24.2 all-gather.2

commit v6 on v5

--- a/solution.py
+++ b/solution.py
@@ -71,7 +71,7 @@
     336, 384, [(48 * g + 6 * z + i, 48 * z + 6 * g + i) for g in range(7) for z in range(8) for i in range(6)]
 )
 SECOND_ROWS = one_hot(
-    144, 128, [(16 * k + 6 * h + i, 64 * h + 6 * k + i) for k in range(9) for h in range(2) for i in range(6)]
+    112, 96, [(16 * g + 6 * h + i, 48 * h + 6 * g + i) for g in range(7) for h in range(2) for i in range(6)]
 )
 SECOND_LANES = one_hot(512, CH, [(128 * y + o, PART * y + o) for y in range(4) for o in range(PART)])
 PART_LANES = one_hot(
@@ -154,16 +154,17 @@
     sums_ref[...] = jnp.concatenate([b[42:43] + b[43:44] + b[44:45] for b in wide], axis=0)
 
 
-def arrange_second(got_ref, rows_ref, lanes_ref, out_ref):
-    by_part = []
+def arrange_second(got_ref, rows_ref, out_ref):
+    parts = []
     for y in range(NY):
-        pair = jnp.concatenate([got_ref[2 * y + h, 48:112, :] for h in range(2)], axis=0)
-        by_part.append(dot(rows_ref[...], pair).astype(BF))
-    tall_parts = [
-        jnp.concatenate([by_part[y][:, 128 * d : 128 * d + 128] for y in range(NY)], axis=1) for d in range(3)
-    ]
-    rows = [tall_parts[d][16 * k : 16 * k + 16] for k in range(9) for d in range(3)]
-    out_ref[...] = dot(jnp.concatenate(rows, axis=0), lanes_ref[...]).astype(BF)
+        pair = jnp.concatenate([got_ref[2 * y + h, 48:96, :] for h in range(2)], axis=0)
+        parts.append(dot(rows_ref[...], pair))
+    for k in range(4):
+        whole = jnp.concatenate([part[:, PART * k : PART * k + PART] for part in parts], axis=1).astype(BF)
+        for g in range(7):
+            tap = 4 * g + k
+            if tap < 27:
+                out_ref[16 * tap : 16 * tap + 16, :] = whole[16 * g : 16 * g + 16]
 
 
 def first_act(
@@ -340,11 +341,6 @@
     return jnp.transpose(taps, (0, 2, 1, 3)).reshape(42, CH)
 
 
-def by_column(kernel):
-    rows = jnp.transpose(kernel, (0, 1, 3, 2, 4)).reshape(54, 3, PART)
-    return jnp.pad(rows, ((0, 10), (0, 0), (0, 32))).reshape(64, CH)
-
-
 def shards(
     latents,
     gain_first,
@@ -365,7 +361,7 @@
     tile = latents[0, 0]
     flat_tile = tile.reshape(ROWS * WIDE, CH)
 
-    swapped = lax.ppermute(by_column(kernel_second), BOTH, SWAP)
+    swapped = lax.ppermute(jnp.pad(by_group(kernel_second), ((0, 6), (0, 0))), BOTH, SWAP)
     placed, west, east, sums = call(
         measure_tile,
         (shape((320, CH), BF), shape((16, CH), BF), shape((16, CH), BF), shape((NY * COLS, 128), F32)),
@@ -388,7 +384,7 @@
     parcel = jnp.concatenate([placed, from_west, from_east, from_north, from_south], axis=0)
     sums_rows, swapped, packed = lax.optimization_barrier((sums_rows, swapped, by_group(kernel_first)))
     letter = jnp.concatenate([packed, sums_rows[0:6], swapped], axis=0)
-    letters = jnp.broadcast_to(letter[None], (NZ, 112, CH))
+    letters = jnp.broadcast_to(letter[None], (NZ, 96, CH))
     letters, parcel = lax.optimization_barrier((letters, parcel))
     got = lax.all_to_all(letters, "space", 0, 0, tiled=True, axis_index_groups=ALONG_Z)
     later = [lax.ppermute(parcel, "tm", [(t, (t + k) % NY) for t in range(NY)]) for k in range(1, NY)]
@@ -400,6 +396,16 @@
         got,
         jnp.asarray(FIRST_ROWS, BF),
     )
+    got_second, _ = lax.optimization_barrier((got, ordered))
+    ordered_second = call(
+        arrange_second,
+        shape((432, CH), BF),
+        [],
+        [],
+        got_second,
+        jnp.asarray(SECOND_ROWS, BF),
+    )
+    ordered, ordered_second = lax.optimization_barrier((ordered, ordered_second))
     own = lax.all_to_all(ordered, "space", 0, 0, tiled=True, axis_index_groups=ALONG_X)
     stack = call(
         first_act,
@@ -423,17 +429,7 @@
         flops=int(2e10),
         out_places=HB,
     )
-    got_second, _ = lax.optimization_barrier((got, ordered))
-    ordered_second = call(
-        arrange_second,
-        shape((432, CH), BF),
-        [],
-        [],
-        got_second,
-        jnp.asarray(SECOND_ROWS, BF),
-        jnp.asarray(SECOND_LANES, BF),
-    )
-    own, stack, _ = lax.optimization_barrier((own, stack, ordered_second))
+    own, stack = lax.optimization_barrier((own, stack))
     other = lax.ppermute(own, "space", SIBLING)
 
     field, sums = call(

time: 151 us -> 150 us (level)
  waiting for transfers between devices: 25.3 us -> 22.5 us
  local copies, waits for them, and re-layouts: 6.3 us -> 8.01 us
    all_to_all x1, waiting for transfers between devices: 13.6 us -> 11.5 us  [shards(): lax.all_to_all(letters, 'space', 0, 0, tiled=True, axis_index_groups=ALON...]
where the time goes in v6:
time: 150 us; the launch traced here: 148 us
  blocking collectives  36.9 us (25%)
  starting transfers between devices  34.9 us (23%)
  Pallas kernels  31.2 us (21%)
  waiting for transfers between devices  22.5 us (15%)
  between operations  13.8 us (9%)
  local copies, waits for them, and re-layouts  8.01 us (5%)
    pallas_call x7, Pallas kernels, call(): pl.pallas_call(body, out_shape=outs, in_specs=[*places, *[VM] * (len(args...  31.2 us
    all_to_all x1, blocking collectives, shards(): parts = lax.all_to_all(partial, 'tm', 0, 0, tiled=True)  18.6 us
    all_to_all x1, blocking collectives, shards(): all_sums = lax.all_to_all(sums, 'space', 0, 0, tiled=True)  18.3 us
    all_to_all x1, waiting for transfers between devices, shards(): lax.all_to_all(letters, 'space', 0, 0, tiled=True, axis_index_groups=ALON...  11.5 us
    all_to_all x1, starting transfers between devices, shards(): lax.all_to_all(letters, 'space', 0, 0, tiled=True, axis_index_groups=ALON...  9.03 us
    ppermute x1, starting transfers between devices, shards(): send(jnp.concatenate([placed[240:320], from_west[12:16], from_east[12:16]...  7.41 us
    all_to_all x1, starting transfers between devices, shards(): lax.all_to_all(sums, BOTH, 0, 0, tiled=True, axis_index_groups=PLANE)  5.22 us
    unnamed x48, local copies, waits for them, and re-layouts  5.08 us
  transfers between devices with their start and end apart: 14, of which 6 were waited for; matrix products, arithmetic and copies ran while one was open for 2% of the time, Pallas kernels for 13%

profile of v6, /device:TPU:32, one launch (start us, length us, event | category | flops | bytes accessed | tf_op | source)
XLA Modules:
  0.0 148.4 jit_solution(13363627331945571137)
XLA Ops:
  6.5 3.0 %shard_map.244 = (bf16[320,384]{1,0:T(8,128)(2,1)}, bf16[16,384]{1,0:T(8,128)(2,1)}, bf16[16,384]{1,0:T(8,128)(2,1)}, f32[32,128]{1,0:T(8,128)}) custom-call(bf16[320,384]{1,0:T(8,128)(2,1)} %bitcast.42, bf16[384,384]{1,0:T(8,128)(2,1)} %constant.44.clone.lanes_ref, f32[384,128]{1,0:T(8,128)} %constant.45.clone.groups_ref, ...), custom_call_target="tpu_custom_call" | custom-call | tf_op jit(solution)/shard_map/pallas_call | solution.py:324
  9.5 3.9 %collective-permute-start.2 = (bf16[16,384]{1,0:T(8,128)(2,1)}, bf16[16,384]{1,0:T(8,128)(2,1)S(1)}, u32[]{:S(2)}, u32[]{:S(2)}) collective-permute-start(bf16[16,384]{1,0:T(8,128)(2,1)} %get-tuple-element.30), channel_id=1, source_target_pairs={{0,63},{1,0},{2,1},{3,2},{4,3},{5,4},{6,5},{7,6},{8,7},{9,8},{10,9... | collective-permute-start | bytes 36872 | tf_op jit(solution)/shard_map/ppermute | solution.py:379
  13.4 5.2 %all-to-all-start = ((f32[32,1,128]{2,1,0:T(1,128)}), f32[32,1,128]{2,1,0:T(1,128)S(1)}, u32[]{:S(2)}, u32[]{:S(2)}) async-start(f32[32,1,128]{2,1,0:T(1,128)} %bitcast.49), calls=%async_computation | async-start | bytes 32768 | tf_op jit(solution)/shard_map/all_to_all | solution.py:380
  21.2 1.0 constant_dynamic-update-slice_fusion.4
  22.5 7.4 %collective-permute-start.3 = (bf16[88,384]{1,0:T(8,128)(2,1)S(1)}, bf16[88,384]{1,0:T(8,128)(2,1)S(1)}, u32[]{:S(2)}, u32[]{:S(2)}) collective-permute-start(bf16[88,384]{1,0:T(8,128)(2,1)S(1)} %pad_maximum_fusion.1), channel_id=1, source_target_pairs={{0,8},{1,9},{2,10},{3,11},{4,12},{5,13},{6,14},{7,15},{8,16},{9,17... | collective-permute-start | bytes 202760 | tf_op jit(solution)/shard_map/ppermute | solution.py:382
  30.1 1.7 %collective-permute-done.3 = bf16[88,384]{1,0:T(8,128)(2,1)S(1)} collective-permute-done((bf16[88,384]{1,0:T(8,128)(2,1)S(1)}, bf16[88,384]{1,0:T(8,128)(2,1)S(1)}, u32[]{:S(2)}, u32[]{:S(2)}) %collective-permute-start.3) | collective-permute-done | bytes 67616 | tf_op jit(solution)/shard_map/ppermute | solution.py:382
  31.8 2.4 %collective-permute-done.4 = bf16[88,384]{1,0:T(8,128)(2,1)S(1)} collective-permute-done((bf16[88,384]{1,0:T(8,128)(2,1)S(1)}, bf16[88,384]{1,0:T(8,128)(2,1)S(1)}, u32[]{:S(2)}, u32[]{:S(2)}) %collective-permute-start.4) | collective-permute-done | bytes 67616 | tf_op jit(solution)/shard_map/ppermute | solution.py:383
  35.1 9.0 %all-to-all-start.1 = ((bf16[8,96,384]{2,1,0:T(8,128)(2,1)}), bf16[8,96,384]{2,1,0:T(8,128)(2,1)S(1)}, u32[]{:S(2)}, u32[]{:S(2)}) async-start(bf16[8,96,384]{2,1,0:T(8,128)(2,1)} %broadcast_in_dim.2), calls=%async_computation.1 | async-start | bytes 1179648 | tf_op jit(solution)/shard_map/all_to_all | solution.py:389
  44.2 2.0 %collective-permute-start.6 = (bf16[528,384]{1,0:T(8,128)(2,1)S(1)}, bf16[528,384]{1,0:T(8,128)(2,1)S(1)}, u32[]{:S(2)}, u32[]{:S(2)}) collective-permute-start(bf16[528,384]{1,0:T(8,128)(2,1)S(1)} %constant_dynamic-update-slice_fusion.lat0_ref), channel_id=1, source_target_pairs={{0,128},{64,192},{128,0},{192,64},{1,129},{65,193},{129,1},{193,65... | collective-permute-start | bytes 1216520 | tf_op jit(solution)/shard_map/ppermute | solution.py:390
  46.1 2.4 %collective-permute-start.7 = (bf16[528,384]{1,0:T(8,128)(2,1)S(1)}, bf16[528,384]{1,0:T(8,128)(2,1)}, u32[]{:S(2)}, u32[]{:S(2)}) collective-permute-start(bf16[528,384]{1,0:T(8,128)(2,1)S(1)} %constant_dynamic-update-slice_fusion.lat0_ref), channel_id=1, source_target_pairs={{0,192},{64,0},{128,64},{192,128},{1,193},{65,1},{129,65},{193,129... | collective-permute-start | bytes 1216520 | tf_op jit(solution)/shard_map/ppermute | solution.py:390
  48.7 11.5 %all-to-all-done.1.got_ref = bf16[8,96,384]{2,1,0:T(8,128)(2,1)S(1)} async-done(((bf16[8,96,384]{2,1,0:T(8,128)(2,1)}), bf16[8,96,384]{2,1,0:T(8,128)(2,1)S(1)}, u32[]{:S(2)}, u32[]{:S(2)}) %all-to-all-start.1) | async-done | bytes 589856 | tf_op jit(solution)/shard_map/all_to_all | solution.py:389
  60.2 1.3 shard_map.246
  61.6 1.1 shard_map.247
  62.7 4.2 %all-to-all-start.2 = ((bf16[4,336,384]{2,1,0:T(8,128)(2,1)}), bf16[4,336,384]{2,1,0:T(8,128)(2,1)S(1)}, u32[]{:S(2)}, u32[]{:S(2)}) async-start(bf16[4,336,384]{2,1,0:T(8,128)(2,1)} %get-tuple-element.34), calls=%async_computation.2 | async-start | bytes 2064384 | tf_op jit(solution)/shard_map/all_to_all | solution.py:409
  68.4 1.0 copy-done.11
  70.4 5.9 %shard_map.248.stack_ref = bf16[4,592,1152]{2,1,0:T(8,128)(2,1)} custom-call(s32[2]{0:T(128)S(1)} %pad_add_fusion.pos_ref, bf16[528,384]{1,0:T(8,128)(2,1)S(1)} %constant_dynamic-update-slice_fusion.lat0_ref, bf16[528,384]{1,0:T(8,128)(2,1)S(1)} %collective-permute-done.5.lat1_ref, bf16[528,384]{1,0:T(8,128)(2,1)S(1)} %copy-done.11, ...), custom_call_target="tpu_custom_call" | custom-call | flops 20000000000 | tf_op jit(solution)/shard_map/pallas_call | solution.py:324
  76.2 1.5 %all-to-all-done.2 = bf16[4,336,384]{2,1,0:T(8,128)(2,1)S(1)} async-done(((bf16[4,336,384]{2,1,0:T(8,128)(2,1)}), bf16[4,336,384]{2,1,0:T(8,128)(2,1)S(1)}, u32[]{:S(2)}, u32[]{:S(2)}) %all-to-all-start.2) | async-done | bytes 1032224 | tf_op jit(solution)/shard_map/all_to_all | solution.py:409
  77.7 2.6 %collective-permute-done.8 = bf16[4,336,384]{2,1,0:T(8,128)(2,1)S(1)} collective-permute-done((bf16[4,336,384]{2,1,0:T(8,128)(2,1)S(1)}, bf16[4,336,384]{2,1,0:T(8,128)(2,1)S(1)}, u32[]{:S(2)}, u32[]{:S(2)}) %collective-permute-start.8) | collective-permute-done | bytes 1032224 | tf_op jit(solution)/shard_map/ppermute | solution.py:433
  80.4 11.2 %shard_map.249 = (f32[4,496,128]{2,1,0:T(8,128)S(1)}, f32[64,128]{1,0:T(8,128)S(1)}) custom-call(s32[2]{0:T(128)S(1)} %pad_add_fusion.pos_ref, bf16[4,592,1152]{2,1,0:T(8,128)(2,1)} %shard_map.248.stack_ref, bf16[4,7,48,384]{3,2,1,0:T(8,128)(2,1)S(1)} %bitcast.33, bf16[4,7,48,384]{3,2,1,0:T(8,128)(2,1)S(1)} %bitcast.37, f32[8,384]{1,0:T(8,128)S(1)} %stack.41.vectors_ref, ...), custom_call_target="tpu_custom_call" | custom-call | tf_op jit(solution)/shard_map/pallas_call | solution.py:324
  91.7 2.1 %all-gather.3.cloned.1.call-done = bf16[1728,384]{1,0:T(8,128)(2,1)} async-done(((bf16[432,384]{1,0:T(8,128)(2,1)}), bf16[1728,384]{1,0:T(8,128)(2,1)}) %all-gather.3.cloned.1.call-update) | async-done | bytes 1327120 | tf_op jit(solution)/shard_map/all_gather | solution.py:457
  93.8 18.3 %all_to_all.37 = f32[64,1,128]{2,1,0:T(1,128)S(1)} all-to-all(f32[64,1,128]{2,1,0:T(1,128)S(1)} %bitcast.40), channel_id=1, replica_groups=mesh['tm'=4,'space'=64] {'space'}, dimensions={0} | all-to-all | bytes 65536 | tf_op jit(solution)/shard_map/all_to_all | solution.py:456
  112.1 1.3 copy-done
  113.4 8.6 %shard_map.250 = bf16[4,8,40,384]{3,2,1,0:T(8,128)(2,1)S(1)} custom-call(s32[2]{0:T(128)S(1)} %pad_add_fusion.pos_ref, f32[4,496,128]{2,1,0:T(8,128)S(1)} %get-tuple-element.39.field_ref, bf16[4,27,16,384]{3,2,1,0:T(8,128)(2,1)S(1)} %bitcast.35, bf16[4,27,16,384]{3,2,1,0:T(8,128)(2,1)S(1)} %bitcast.36, f32[64,128]{1,0:T(8,128)S(1)} %bitcast.38, ...), custom_call_target="tpu_custom_call" | custom-call | tf_op jit(solution)/shard_map/pallas_call | solution.py:324
  122.0 18.6 %all_to_all.38 = bf16[4,8,40,384]{3,2,1,0:T(8,128)(2,1)S(1)} all-to-all(bf16[4,8,40,384]{3,2,1,0:T(8,128)(2,1)S(1)} %shard_map.250), channel_id=1, replica_groups=mesh['tm'=4,'space'=64] {'tm'}, dimensions={0} | all-to-all | bytes 1966080 | tf_op jit(solution)/shard_map/all_to_all | solution.py:483
  (87 shorter events, 7.3 us)
Async XLA Ops:
  9.5 12.9 %collective-permute-start.1 = (bf16[16,384]{1,0:T(8,128)(2,1)}, bf16[16,384]{1,0:T(8,128)(2,1)S(1)}, u32[]{:S(2)}, u32[]{:S(2)}) collective-permute-start(bf16[16,384]{1,0:T(8,128)(2,1)} %get-tuple-element.29), channel_id=1, source_target_pairs={{0,1},{1,2},{2,3},{3,4},{4,5},{5,6},{6,7},{7,8},{8,9},{9,10},{10,1... | collective-permute-start | bytes 36872 | tf_op jit(solution)/shard_map/ppermute | solution.py:379
  9.5 12.9 %collective-permute-start.2 = (bf16[16,384]{1,0:T(8,128)(2,1)}, bf16[16,384]{1,0:T(8,128)(2,1)S(1)}, u32[]{:S(2)}, u32[]{:S(2)}) collective-permute-start(bf16[16,384]{1,0:T(8,128)(2,1)} %get-tuple-element.30), channel_id=1, source_target_pairs={{0,63},{1,0},{2,1},{3,2},{4,3},{5,4},{6,5},{7,6},{8,7},{9,8},{10,9... | collective-permute-start | bytes 36872 | tf_op jit(solution)/shard_map/ppermute | solution.py:379
  13.4 16.6 %all-to-all-start = ((f32[32,1,128]{2,1,0:T(1,128)}), f32[32,1,128]{2,1,0:T(1,128)S(1)}, u32[]{:S(2)}, u32[]{:S(2)}) async-start(f32[32,1,128]{2,1,0:T(1,128)} %bitcast.49), calls=%async_computation | async-start | bytes 32768 | tf_op jit(solution)/shard_map/all_to_all | solution.py:380
  19.5 29.1 %copy-start.17 = (f32[384]{0:T(512)S(1)}, f32[384]{0:T(512)}, u32[]{:S(2)}) copy-start(f32[384]{0:T(512)} %param.27) | copy-start | bytes 4612
  19.5 29.1 %copy-start.18 = (f32[384]{0:T(512)S(1)}, f32[384]{0:T(512)}, u32[]{:S(2)}) copy-start(f32[384]{0:T(512)} %param.28) | copy-start | bytes 4612
  19.5 29.1 %copy-start.19 = (f32[384]{0:T(512)S(1)}, f32[384]{0:T(512)}, u32[]{:S(2)}) copy-start(f32[384]{0:T(512)} %param.30) | copy-start | bytes 4612
  19.5 29.1 %copy-start.20 = (f32[384]{0:T(512)S(1)}, f32[384]{0:T(512)}, u32[]{:S(2)}) copy-start(f32[384]{0:T(512)} %param.31) | copy-start | bytes 4612
  19.5 29.1 %copy-start.21 = (f32[384]{0:T(512)S(1)}, f32[384]{0:T(512)}, u32[]{:S(2)}) copy-start(f32[384]{0:T(512)} %param.32) | copy-start | bytes 4612
  19.5 29.1 %copy-start.16 = (f32[384]{0:T(512)S(1)}, f32[384]{0:T(512)}, u32[]{:S(2)}) copy-start(f32[384]{0:T(512)} %param.34) | copy-start | bytes 4612
  19.6 40.7 %copy-start.4 = (bf16[336,384]{1,0:T(8,128)(2,1)S(1)}, bf16[336,384]{1,0:T(8,128)(2,1)}, u32[]{:S(2)}) copy-start(bf16[336,384]{1,0:T(8,128)(2,1)} %constant.49.clone.rows_ref) | copy-start | bytes 774148
  19.7 10.4 %collective-permute-start = (bf16[48,384]{1,0:T(8,128)(2,1)S(1)}, bf16[48,384]{1,0:T(8,128)(2,1)S(1)}, u32[]{:S(2)}, u32[]{:S(2)}) collective-permute-start(bf16[48,384]{1,0:T(8,128)(2,1)S(1)} %pad.12), channel_id=1, source_target_pairs={{0,0},{1,1},{2,2},{3,3},{4,4},{5,5},{6,6},{7,7},{8,8},{9,9},{10,10... | collective-permute-start | bytes 110600 | tf_op jit(solution)/shard_map/ppermute | solution.py:364
  22.2 39.4 %copy-start.9 = (bf16[112,96]{1,0:T(8,128)(2,1)S(1)}, bf16[112,96]{1,0:T(8,128)(2,1)}, u32[]{:S(2)}) copy-start(bf16[112,96]{1,0:T(8,128)(2,1)} %constant.50.clone.rows_ref) | copy-start | bytes 64516
  22.5 9.3 %collective-permute-start.3 = (bf16[88,384]{1,0:T(8,128)(2,1)S(1)}, bf16[88,384]{1,0:T(8,128)(2,1)S(1)}, u32[]{:S(2)}, u32[]{:S(2)}) collective-permute-start(bf16[88,384]{1,0:T(8,128)(2,1)S(1)} %pad_maximum_fusion.1), channel_id=1, source_target_pairs={{0,8},{1,9},{2,10},{3,11},{4,12},{5,13},{6,14},{7,15},{8,16},{9,17... | collective-permute-start | bytes 202760 | tf_op jit(solution)/shard_map/ppermute | solution.py:382
  29.9 4.4 %collective-permute-start.4 = (bf16[88,384]{1,0:T(8,128)(2,1)S(1)}, bf16[88,384]{1,0:T(8,128)(2,1)S(1)}, u32[]{:S(2)}, u32[]{:S(2)}) collective-permute-start(bf16[88,384]{1,0:T(8,128)(2,1)S(1)} %pad_maximum_fusion.2), channel_id=1, source_target_pairs={{0,56},{1,57},{2,58},{3,59},{4,60},{5,61},{6,62},{7,63},{8,0},{9,1... | collective-permute-start | bytes 202760 | tf_op jit(solution)/shard_map/ppermute | solution.py:383
  35.1 25.1 %all-to-all-start.1 = ((bf16[8,96,384]{2,1,0:T(8,128)(2,1)}), bf16[8,96,384]{2,1,0:T(8,128)(2,1)S(1)}, u32[]{:S(2)}, u32[]{:S(2)}) async-start(bf16[8,96,384]{2,1,0:T(8,128)(2,1)} %broadcast_in_dim.2), calls=%async_computation.1 | async-start | bytes 1179648 | tf_op jit(solution)/shard_map/all_to_all | solution.py:389
  44.2 23.5 %collective-permute-start.5 = (bf16[528,384]{1,0:T(8,128)(2,1)S(1)}, bf16[528,384]{1,0:T(8,128)(2,1)S(1)}, u32[]{:S(2)}, u32[]{:S(2)}) collective-permute-start(bf16[528,384]{1,0:T(8,128)(2,1)S(1)} %constant_dynamic-update-slice_fusion.lat0_ref), channel_id=1, source_target_pairs={{0,64},{64,128},{128,192},{192,0},{1,65},{65,129},{129,193},{193,1... | collective-permute-start | bytes 1216520 | tf_op jit(solution)/shard_map/ppermute | solution.py:390
  44.2 23.5 %collective-permute-start.6 = (bf16[528,384]{1,0:T(8,128)(2,1)S(1)}, bf16[528,384]{1,0:T(8,128)(2,1)S(1)}, u32[]{:S(2)}, u32[]{:S(2)}) collective-permute-start(bf16[528,384]{1,0:T(8,128)(2,1)S(1)} %constant_dynamic-update-slice_fusion.lat0_ref), channel_id=1, source_target_pairs={{0,128},{64,192},{128,0},{192,64},{1,129},{65,193},{129,1},{193,65... | collective-permute-start | bytes 1216520 | tf_op jit(solution)/shard_map/ppermute | solution.py:390
  46.1 22.3 %collective-permute-start.7 = (bf16[528,384]{1,0:T(8,128)(2,1)S(1)}, bf16[528,384]{1,0:T(8,128)(2,1)}, u32[]{:S(2)}, u32[]{:S(2)}) collective-permute-start(bf16[528,384]{1,0:T(8,128)(2,1)S(1)} %constant_dynamic-update-slice_fusion.lat0_ref), channel_id=1, source_target_pairs={{0,192},{64,0},{128,64},{192,128},{1,193},{65,1},{129,65},{193,129... | collective-permute-start | bytes 1216520 | tf_op jit(solution)/shard_map/ppermute | solution.py:390
  62.7 15.1 %all-to-all-start.2 = ((bf16[4,336,384]{2,1,0:T(8,128)(2,1)}), bf16[4,336,384]{2,1,0:T(8,128)(2,1)S(1)}, u32[]{:S(2)}, u32[]{:S(2)}) async-start(bf16[4,336,384]{2,1,0:T(8,128)(2,1)} %get-tuple-element.34), calls=%async_computation.2 | async-start | bytes 2064384 | tf_op jit(solution)/shard_map/all_to_all | solution.py:409
  66.9 26.9 %all-gather.3.cloned.1.call-start = ((), (), s32[]{:S(2)}) async-start(), calls=%async_computation.5 | async-start | bytes 1658880 | tf_op jit(solution)/shard_map/all_gather | solution.py:457
  77.7 2.6 %collective-permute-start.8 = (bf16[4,336,384]{2,1,0:T(8,128)(2,1)S(1)}, bf16[4,336,384]{2,1,0:T(8,128)(2,1)S(1)}, u32[]{:S(2)}, u32[]{:S(2)}) collective-permute-start(bf16[4,336,384]{2,1,0:T(8,128)(2,1)S(1)} %all-to-all-done.2), channel_id=1, source_target_pairs={{0,1},{1,0},{2,3},{3,2},{4,5},{5,4},{6,7},{7,6},{8,9},{9,8},{10,11... | collective-permute-start | bytes 3096584 | tf_op jit(solution)/shard_map/ppermute | solution.py:433
  80.4 31.7 %copy-start.5 = (f32[128,128]{1,0:T(8,128)S(1)}, f32[128,128]{1,0:T(8,128)}, u32[]{:S(2)}) copy-start(f32[128,128]{1,0:T(8,128)} %constant.57.clone.squares_t_ref) | copy-start | bytes 196612
  80.4 31.7 %copy-start.8 = (bf16[128,128]{1,0:T(8,128)(2,1)S(1)}, bf16[128,128]{1,0:T(8,128)(2,1)}, u32[]{:S(2)}) copy-start(bf16[128,128]{1,0:T(8,128)(2,1)} %constant.58.clone.order_ref) | copy-start | bytes 98308
  93.8 18.3 %collective-permute-start.9 = (bf16[4,432,384]{2,1,0:T(8,128)(2,1)}, bf16[4,432,384]{2,1,0:T(8,128)(2,1)S(1)}, u32[]{:S(2)}, u32[]{:S(2)}) collective-permute-start(bf16[4,432,384]{2,1,0:T(8,128)(2,1)} %bitcast.34), channel_id=1, source_target_pairs={{0,1},{1,0},{2,3},{3,2},{4,5},{5,4},{6,7},{7,6},{8,9},{9,8},{10,11... | collective-permute-start | bytes 3981320 | tf_op jit(solution)/shard_map/ppermute | solution.py:459
  (12 other events, 117.9 us)
Sparse Core Ops, SparseCore 0:
  69.6 24.1 all-gather.2

commit v7 on v6

--- a/solution.py
+++ b/solution.py
@@ -428,6 +428,7 @@
         jnp.asarray(SQUARES_OF_LANES),
         flops=int(2e10),
         out_places=HB,
+        grant=48,
     )
     own, stack = lax.optimization_barrier((own, stack))
     other = lax.ppermute(own, "space", SIBLING)
@@ -455,7 +456,7 @@
     )
     all_sums = lax.all_to_all(sums, "space", 0, 0, tiled=True)
     own_second = lax.all_gather(ordered_second, "space", axis_index_groups=ALONG_X)
-    own_second, _ = lax.optimization_barrier((own_second, field))
+    own_second, _ = lax.optimization_barrier((own_second, all_sums))
     other_second = lax.ppermute(own_second, "space", SIBLING)
     partial = call(
         second_conv,

time: 150 us -> 148 us (0.987)
  blocking collectives: 36.9 us -> 33.7 us
  waiting for transfers between devices: 22.5 us -> 24.6 us
    ppermute x1, waiting for transfers between devices: 0.01 us -> 3.27 us  [shards(): other_second = lax.ppermute(own_second, 'space', SIBLING)]
    all_to_all x1, blocking collectives: 18.3 us -> 15.8 us  [shards(): all_sums = lax.all_to_all(sums, 'space', 0, 0, tiled=True)]
    all_gather x1, waiting for transfers between devices: 2.12 us -> 0.01 us  [shards(): lax.all_gather(ordered_second, 'space', axis_index_groups=ALONG_X)]
where the time goes in v7:
time: 148 us; the launch traced here: 146 us
  starting transfers between devices  34.9 us (24%)
  blocking collectives  33.7 us (23%)
  Pallas kernels  31.2 us (21%)
  waiting for transfers between devices  24.6 us (17%)
  between operations  13.8 us (9%)
  local copies, waits for them, and re-layouts  7.09 us (5%)
    pallas_call x7, Pallas kernels, call(): pl.pallas_call(body, out_shape=outs, in_specs=[*places, *[VM] * (len(args...  31.2 us
    all_to_all x1, blocking collectives, shards(): parts = lax.all_to_all(partial, 'tm', 0, 0, tiled=True)  17.9 us
    all_to_all x1, blocking collectives, shards(): all_sums = lax.all_to_all(sums, 'space', 0, 0, tiled=True)  15.8 us
    all_to_all x1, waiting for transfers between devices, shards(): lax.all_to_all(letters, 'space', 0, 0, tiled=True, axis_index_groups=ALON...  11.5 us
    all_to_all x1, starting transfers between devices, shards(): lax.all_to_all(letters, 'space', 0, 0, tiled=True, axis_index_groups=ALON...  9.03 us
    ppermute x1, starting transfers between devices, shards(): send(jnp.concatenate([placed[240:320], from_west[12:16], from_east[12:16]...  7.41 us
    all_to_all x1, starting transfers between devices, shards(): lax.all_to_all(sums, BOTH, 0, 0, tiled=True, axis_index_groups=PLANE)  5.22 us
    ppermute x3, starting transfers between devices, shards(): lax.ppermute(parcel, 'tm', [(t, (t + k) % NY) for t in range(NY)])  4.36 us
  transfers between devices with their start and end apart: 14, of which 6 were waited for; matrix products, arithmetic and copies ran while one was open for 2% of the time, Pallas kernels for 13%

profile of v7, /device:TPU:32, one launch (start us, length us, event | category | flops | bytes accessed | tf_op | source)
XLA Modules:
  0.0 146.4 jit_solution(3297489366410535053)
XLA Ops:
  6.5 3.0 %shard_map.244 = (bf16[320,384]{1,0:T(8,128)(2,1)}, bf16[16,384]{1,0:T(8,128)(2,1)}, bf16[16,384]{1,0:T(8,128)(2,1)}, f32[32,128]{1,0:T(8,128)}) custom-call(bf16[320,384]{1,0:T(8,128)(2,1)} %bitcast.42, bf16[384,384]{1,0:T(8,128)(2,1)} %constant.44.clone.lanes_ref, f32[384,128]{1,0:T(8,128)} %constant.45.clone.groups_ref, ...), custom_call_target="tpu_custom_call" | custom-call | tf_op jit(solution)/shard_map/pallas_call | solution.py:324
  9.5 3.9 %collective-permute-start.2 = (bf16[16,384]{1,0:T(8,128)(2,1)}, bf16[16,384]{1,0:T(8,128)(2,1)S(1)}, u32[]{:S(2)}, u32[]{:S(2)}) collective-permute-start(bf16[16,384]{1,0:T(8,128)(2,1)} %get-tuple-element.30), channel_id=1, source_target_pairs={{0,63},{1,0},{2,1},{3,2},{4,3},{5,4},{6,5},{7,6},{8,7},{9,8},{10,9... | collective-permute-start | bytes 36872 | tf_op jit(solution)/shard_map/ppermute | solution.py:379
  13.4 5.2 %all-to-all-start = ((f32[32,1,128]{2,1,0:T(1,128)}), f32[32,1,128]{2,1,0:T(1,128)S(1)}, u32[]{:S(2)}, u32[]{:S(2)}) async-start(f32[32,1,128]{2,1,0:T(1,128)} %bitcast.49), calls=%async_computation | async-start | bytes 32768 | tf_op jit(solution)/shard_map/all_to_all | solution.py:380
  21.2 1.0 constant_dynamic-update-slice_fusion.4
  22.5 7.4 %collective-permute-start.3 = (bf16[88,384]{1,0:T(8,128)(2,1)S(1)}, bf16[88,384]{1,0:T(8,128)(2,1)S(1)}, u32[]{:S(2)}, u32[]{:S(2)}) collective-permute-start(bf16[88,384]{1,0:T(8,128)(2,1)S(1)} %pad_maximum_fusion.1), channel_id=1, source_target_pairs={{0,8},{1,9},{2,10},{3,11},{4,12},{5,13},{6,14},{7,15},{8,16},{9,17... | collective-permute-start | bytes 202760 | tf_op jit(solution)/shard_map/ppermute | solution.py:382
  30.1 1.7 %collective-permute-done.3 = bf16[88,384]{1,0:T(8,128)(2,1)S(1)} collective-permute-done((bf16[88,384]{1,0:T(8,128)(2,1)S(1)}, bf16[88,384]{1,0:T(8,128)(2,1)S(1)}, u32[]{:S(2)}, u32[]{:S(2)}) %collective-permute-start.3) | collective-permute-done | bytes 67616 | tf_op jit(solution)/shard_map/ppermute | solution.py:382
  31.8 2.4 %collective-permute-done.4 = bf16[88,384]{1,0:T(8,128)(2,1)S(1)} collective-permute-done((bf16[88,384]{1,0:T(8,128)(2,1)S(1)}, bf16[88,384]{1,0:T(8,128)(2,1)S(1)}, u32[]{:S(2)}, u32[]{:S(2)}) %collective-permute-start.4) | collective-permute-done | bytes 67616 | tf_op jit(solution)/shard_map/ppermute | solution.py:383
  35.1 9.0 %all-to-all-start.1 = ((bf16[8,96,384]{2,1,0:T(8,128)(2,1)}), bf16[8,96,384]{2,1,0:T(8,128)(2,1)S(1)}, u32[]{:S(2)}, u32[]{:S(2)}) async-start(bf16[8,96,384]{2,1,0:T(8,128)(2,1)} %broadcast_in_dim.2), calls=%async_computation.1 | async-start | bytes 1179648 | tf_op jit(solution)/shard_map/all_to_all | solution.py:389
  44.2 2.0 %collective-permute-start.6 = (bf16[528,384]{1,0:T(8,128)(2,1)S(1)}, bf16[528,384]{1,0:T(8,128)(2,1)S(1)}, u32[]{:S(2)}, u32[]{:S(2)}) collective-permute-start(bf16[528,384]{1,0:T(8,128)(2,1)S(1)} %constant_dynamic-update-slice_fusion.lat0_ref), channel_id=1, source_target_pairs={{0,128},{64,192},{128,0},{192,64},{1,129},{65,193},{129,1},{193,65... | collective-permute-start | bytes 1216520 | tf_op jit(solution)/shard_map/ppermute | solution.py:390
  46.1 2.4 %collective-permute-start.7 = (bf16[528,384]{1,0:T(8,128)(2,1)S(1)}, bf16[528,384]{1,0:T(8,128)(2,1)}, u32[]{:S(2)}, u32[]{:S(2)}) collective-permute-start(bf16[528,384]{1,0:T(8,128)(2,1)S(1)} %constant_dynamic-update-slice_fusion.lat0_ref), channel_id=1, source_target_pairs={{0,192},{64,0},{128,64},{192,128},{1,193},{65,1},{129,65},{193,129... | collective-permute-start | bytes 1216520 | tf_op jit(solution)/shard_map/ppermute | solution.py:390
  48.8 11.5 %all-to-all-done.1.got_ref = bf16[8,96,384]{2,1,0:T(8,128)(2,1)S(1)} async-done(((bf16[8,96,384]{2,1,0:T(8,128)(2,1)}), bf16[8,96,384]{2,1,0:T(8,128)(2,1)S(1)}, u32[]{:S(2)}, u32[]{:S(2)}) %all-to-all-start.1) | async-done | bytes 589856 | tf_op jit(solution)/shard_map/all_to_all | solution.py:389
  60.2 1.3 shard_map.246
  61.6 1.1 shard_map.247
  62.7 4.2 %all-to-all-start.2 = ((bf16[4,336,384]{2,1,0:T(8,128)(2,1)}), bf16[4,336,384]{2,1,0:T(8,128)(2,1)S(1)}, u32[]{:S(2)}, u32[]{:S(2)}) async-start(bf16[4,336,384]{2,1,0:T(8,128)(2,1)} %get-tuple-element.34), calls=%async_computation.2 | async-start | bytes 2064384 | tf_op jit(solution)/shard_map/all_to_all | solution.py:409
  68.5 1.0 copy-done.11
  69.5 5.9 %shard_map.248.stack_ref = bf16[4,592,1152]{2,1,0:T(8,128)(2,1)} custom-call(s32[2]{0:T(128)S(1)} %pad_add_fusion.pos_ref, bf16[528,384]{1,0:T(8,128)(2,1)S(1)} %constant_dynamic-update-slice_fusion.lat0_ref, bf16[528,384]{1,0:T(8,128)(2,1)S(1)} %collective-permute-done.5.lat1_ref, bf16[528,384]{1,0:T(8,128)(2,1)S(1)} %copy-done.11, ...), custom_call_target="tpu_custom_call" | custom-call | flops 20000000000 | tf_op jit(solution)/shard_map/pallas_call | solution.py:324
  75.3 2.4 %all-to-all-done.2 = bf16[4,336,384]{2,1,0:T(8,128)(2,1)S(1)} async-done(((bf16[4,336,384]{2,1,0:T(8,128)(2,1)}), bf16[4,336,384]{2,1,0:T(8,128)(2,1)S(1)}, u32[]{:S(2)}, u32[]{:S(2)}) %all-to-all-start.2) | async-done | bytes 1032224 | tf_op jit(solution)/shard_map/all_to_all | solution.py:409
  77.7 2.6 %collective-permute-done.8 = bf16[4,336,384]{2,1,0:T(8,128)(2,1)S(1)} collective-permute-done((bf16[4,336,384]{2,1,0:T(8,128)(2,1)S(1)}, bf16[4,336,384]{2,1,0:T(8,128)(2,1)S(1)}, u32[]{:S(2)}, u32[]{:S(2)}) %collective-permute-start.8) | collective-permute-done | bytes 1032224 | tf_op jit(solution)/shard_map/ppermute | solution.py:434
  80.4 11.2 %shard_map.249 = (f32[4,496,128]{2,1,0:T(8,128)S(1)}, f32[64,128]{1,0:T(8,128)S(1)}) custom-call(s32[2]{0:T(128)S(1)} %pad_add_fusion.pos_ref, bf16[4,592,1152]{2,1,0:T(8,128)(2,1)} %shard_map.248.stack_ref, bf16[4,7,48,384]{3,2,1,0:T(8,128)(2,1)S(1)} %bitcast.33, bf16[4,7,48,384]{3,2,1,0:T(8,128)(2,1)S(1)} %bitcast.37, f32[8,384]{1,0:T(8,128)S(1)} %stack.41.vectors_ref, ...), custom_call_target="tpu_custom_call" | custom-call | tf_op jit(solution)/shard_map/pallas_call | solution.py:324
  91.7 15.8 %all_to_all.37 = f32[64,1,128]{2,1,0:T(1,128)S(1)} all-to-all(f32[64,1,128]{2,1,0:T(1,128)S(1)} %bitcast.40), channel_id=1, replica_groups=mesh['tm'=4,'space'=64] {'space'}, dimensions={0} | all-to-all | bytes 65536 | tf_op jit(solution)/shard_map/all_to_all | solution.py:457
  107.5 3.3 %collective-permute-done.9 = bf16[4,432,384]{2,1,0:T(8,128)(2,1)S(1)} collective-permute-done((bf16[4,432,384]{2,1,0:T(8,128)(2,1)}, bf16[4,432,384]{2,1,0:T(8,128)(2,1)S(1)}, u32[]{:S(2)}, u32[]{:S(2)}) %collective-permute-start.9) | collective-permute-done | bytes 1327136 | tf_op jit(solution)/shard_map/ppermute | solution.py:460
  110.8 1.3 copy-done
  112.1 8.6 %shard_map.250 = bf16[4,8,40,384]{3,2,1,0:T(8,128)(2,1)S(1)} custom-call(s32[2]{0:T(128)S(1)} %pad_add_fusion.pos_ref, f32[4,496,128]{2,1,0:T(8,128)S(1)} %get-tuple-element.39.field_ref, bf16[4,27,16,384]{3,2,1,0:T(8,128)(2,1)S(1)} %bitcast.35, bf16[4,27,16,384]{3,2,1,0:T(8,128)(2,1)S(1)} %bitcast.36, f32[64,128]{1,0:T(8,128)S(1)} %bitcast.38, ...), custom_call_target="tpu_custom_call" | custom-call | tf_op jit(solution)/shard_map/pallas_call | solution.py:324
  120.7 17.9 %all_to_all.38 = bf16[4,8,40,384]{3,2,1,0:T(8,128)(2,1)S(1)} all-to-all(bf16[4,8,40,384]{3,2,1,0:T(8,128)(2,1)S(1)} %shard_map.250), channel_id=1, replica_groups=mesh['tm'=4,'space'=64] {'tm'}, dimensions={0} | all-to-all | bytes 1966080 | tf_op jit(solution)/shard_map/all_to_all | solution.py:484
  (87 shorter events, 6.4 us)
Async XLA Ops:
  9.5 12.9 %collective-permute-start.1 = (bf16[16,384]{1,0:T(8,128)(2,1)}, bf16[16,384]{1,0:T(8,128)(2,1)S(1)}, u32[]{:S(2)}, u32[]{:S(2)}) collective-permute-start(bf16[16,384]{1,0:T(8,128)(2,1)} %get-tuple-element.29), channel_id=1, source_target_pairs={{0,1},{1,2},{2,3},{3,4},{4,5},{5,6},{6,7},{7,8},{8,9},{9,10},{10,1... | collective-permute-start | bytes 36872 | tf_op jit(solution)/shard_map/ppermute | solution.py:379
  9.5 12.9 %collective-permute-start.2 = (bf16[16,384]{1,0:T(8,128)(2,1)}, bf16[16,384]{1,0:T(8,128)(2,1)S(1)}, u32[]{:S(2)}, u32[]{:S(2)}) collective-permute-start(bf16[16,384]{1,0:T(8,128)(2,1)} %get-tuple-element.30), channel_id=1, source_target_pairs={{0,63},{1,0},{2,1},{3,2},{4,3},{5,4},{6,5},{7,6},{8,7},{9,8},{10,9... | collective-permute-start | bytes 36872 | tf_op jit(solution)/shard_map/ppermute | solution.py:379
  13.4 16.6 %all-to-all-start = ((f32[32,1,128]{2,1,0:T(1,128)}), f32[32,1,128]{2,1,0:T(1,128)S(1)}, u32[]{:S(2)}, u32[]{:S(2)}) async-start(f32[32,1,128]{2,1,0:T(1,128)} %bitcast.49), calls=%async_computation | async-start | bytes 32768 | tf_op jit(solution)/shard_map/all_to_all | solution.py:380
  19.5 29.1 %copy-start.17 = (f32[384]{0:T(512)S(1)}, f32[384]{0:T(512)}, u32[]{:S(2)}) copy-start(f32[384]{0:T(512)} %param.27) | copy-start | bytes 4612
  19.5 29.1 %copy-start.18 = (f32[384]{0:T(512)S(1)}, f32[384]{0:T(512)}, u32[]{:S(2)}) copy-start(f32[384]{0:T(512)} %param.28) | copy-start | bytes 4612
  19.5 29.1 %copy-start.19 = (f32[384]{0:T(512)S(1)}, f32[384]{0:T(512)}, u32[]{:S(2)}) copy-start(f32[384]{0:T(512)} %param.30) | copy-start | bytes 4612
  19.5 29.1 %copy-start.20 = (f32[384]{0:T(512)S(1)}, f32[384]{0:T(512)}, u32[]{:S(2)}) copy-start(f32[384]{0:T(512)} %param.31) | copy-start | bytes 4612
  19.5 29.1 %copy-start.21 = (f32[384]{0:T(512)S(1)}, f32[384]{0:T(512)}, u32[]{:S(2)}) copy-start(f32[384]{0:T(512)} %param.32) | copy-start | bytes 4612
  19.5 29.1 %copy-start.16 = (f32[384]{0:T(512)S(1)}, f32[384]{0:T(512)}, u32[]{:S(2)}) copy-start(f32[384]{0:T(512)} %param.34) | copy-start | bytes 4612
  19.6 40.7 %copy-start.4 = (bf16[336,384]{1,0:T(8,128)(2,1)S(1)}, bf16[336,384]{1,0:T(8,128)(2,1)}, u32[]{:S(2)}) copy-start(bf16[336,384]{1,0:T(8,128)(2,1)} %constant.49.clone.rows_ref) | copy-start | bytes 774148
  19.7 10.4 %collective-permute-start = (bf16[48,384]{1,0:T(8,128)(2,1)S(1)}, bf16[48,384]{1,0:T(8,128)(2,1)S(1)}, u32[]{:S(2)}, u32[]{:S(2)}) collective-permute-start(bf16[48,384]{1,0:T(8,128)(2,1)S(1)} %pad.12), channel_id=1, source_target_pairs={{0,0},{1,1},{2,2},{3,3},{4,4},{5,5},{6,6},{7,7},{8,8},{9,9},{10,10... | collective-permute-start | bytes 110600 | tf_op jit(solution)/shard_map/ppermute | solution.py:364
  22.2 39.4 %copy-start.9 = (bf16[112,96]{1,0:T(8,128)(2,1)S(1)}, bf16[112,96]{1,0:T(8,128)(2,1)}, u32[]{:S(2)}) copy-start(bf16[112,96]{1,0:T(8,128)(2,1)} %constant.50.clone.rows_ref) | copy-start | bytes 64516
  22.5 9.3 %collective-permute-start.3 = (bf16[88,384]{1,0:T(8,128)(2,1)S(1)}, bf16[88,384]{1,0:T(8,128)(2,1)S(1)}, u32[]{:S(2)}, u32[]{:S(2)}) collective-permute-start(bf16[88,384]{1,0:T(8,128)(2,1)S(1)} %pad_maximum_fusion.1), channel_id=1, source_target_pairs={{0,8},{1,9},{2,10},{3,11},{4,12},{5,13},{6,14},{7,15},{8,16},{9,17... | collective-permute-start | bytes 202760 | tf_op jit(solution)/shard_map/ppermute | solution.py:382
  29.9 4.4 %collective-permute-start.4 = (bf16[88,384]{1,0:T(8,128)(2,1)S(1)}, bf16[88,384]{1,0:T(8,128)(2,1)S(1)}, u32[]{:S(2)}, u32[]{:S(2)}) collective-permute-start(bf16[88,384]{1,0:T(8,128)(2,1)S(1)} %pad_maximum_fusion.2), channel_id=1, source_target_pairs={{0,56},{1,57},{2,58},{3,59},{4,60},{5,61},{6,62},{7,63},{8,0},{9,1... | collective-permute-start | bytes 202760 | tf_op jit(solution)/shard_map/ppermute | solution.py:383
  35.1 25.1 %all-to-all-start.1 = ((bf16[8,96,384]{2,1,0:T(8,128)(2,1)}), bf16[8,96,384]{2,1,0:T(8,128)(2,1)S(1)}, u32[]{:S(2)}, u32[]{:S(2)}) async-start(bf16[8,96,384]{2,1,0:T(8,128)(2,1)} %broadcast_in_dim.2), calls=%async_computation.1 | async-start | bytes 1179648 | tf_op jit(solution)/shard_map/all_to_all | solution.py:389
  44.2 23.5 %collective-permute-start.5 = (bf16[528,384]{1,0:T(8,128)(2,1)S(1)}, bf16[528,384]{1,0:T(8,128)(2,1)S(1)}, u32[]{:S(2)}, u32[]{:S(2)}) collective-permute-start(bf16[528,384]{1,0:T(8,128)(2,1)S(1)} %constant_dynamic-update-slice_fusion.lat0_ref), channel_id=1, source_target_pairs={{0,64},{64,128},{128,192},{192,0},{1,65},{65,129},{129,193},{193,1... | collective-permute-start | bytes 1216520 | tf_op jit(solution)/shard_map/ppermute | solution.py:390
  44.2 23.5 %collective-permute-start.6 = (bf16[528,384]{1,0:T(8,128)(2,1)S(1)}, bf16[528,384]{1,0:T(8,128)(2,1)S(1)}, u32[]{:S(2)}, u32[]{:S(2)}) collective-permute-start(bf16[528,384]{1,0:T(8,128)(2,1)S(1)} %constant_dynamic-update-slice_fusion.lat0_ref), channel_id=1, source_target_pairs={{0,128},{64,192},{128,0},{192,64},{1,129},{65,193},{129,1},{193,65... | collective-permute-start | bytes 1216520 | tf_op jit(solution)/shard_map/ppermute | solution.py:390
  46.1 22.3 %collective-permute-start.7 = (bf16[528,384]{1,0:T(8,128)(2,1)S(1)}, bf16[528,384]{1,0:T(8,128)(2,1)}, u32[]{:S(2)}, u32[]{:S(2)}) collective-permute-start(bf16[528,384]{1,0:T(8,128)(2,1)S(1)} %constant_dynamic-update-slice_fusion.lat0_ref), channel_id=1, source_target_pairs={{0,192},{64,0},{128,64},{192,128},{1,193},{65,1},{129,65},{193,129... | collective-permute-start | bytes 1216520 | tf_op jit(solution)/shard_map/ppermute | solution.py:390
  62.7 15.1 %all-to-all-start.2 = ((bf16[4,336,384]{2,1,0:T(8,128)(2,1)}), bf16[4,336,384]{2,1,0:T(8,128)(2,1)S(1)}, u32[]{:S(2)}, u32[]{:S(2)}) async-start(bf16[4,336,384]{2,1,0:T(8,128)(2,1)} %get-tuple-element.34), calls=%async_computation.2 | async-start | bytes 2064384 | tf_op jit(solution)/shard_map/all_to_all | solution.py:409
  66.9 40.5 %all-gather.3.cloned.1.call-start = ((), (), s32[]{:S(2)}) async-start(), calls=%async_computation.5 | async-start | bytes 1658880 | tf_op jit(solution)/shard_map/all_gather | solution.py:458
  77.7 2.6 %collective-permute-start.8 = (bf16[4,336,384]{2,1,0:T(8,128)(2,1)S(1)}, bf16[4,336,384]{2,1,0:T(8,128)(2,1)S(1)}, u32[]{:S(2)}, u32[]{:S(2)}) collective-permute-start(bf16[4,336,384]{2,1,0:T(8,128)(2,1)S(1)} %all-to-all-done.2), channel_id=1, source_target_pairs={{0,1},{1,0},{2,3},{3,2},{4,5},{5,4},{6,7},{7,6},{8,9},{9,8},{10,11... | collective-permute-start | bytes 3096584 | tf_op jit(solution)/shard_map/ppermute | solution.py:434
  80.4 30.4 %copy-start.5 = (f32[128,128]{1,0:T(8,128)S(1)}, f32[128,128]{1,0:T(8,128)}, u32[]{:S(2)}) copy-start(f32[128,128]{1,0:T(8,128)} %constant.57.clone.squares_t_ref) | copy-start | bytes 196612
  80.4 30.3 %copy-start.8 = (bf16[128,128]{1,0:T(8,128)(2,1)S(1)}, bf16[128,128]{1,0:T(8,128)(2,1)}, u32[]{:S(2)}) copy-start(bf16[128,128]{1,0:T(8,128)(2,1)} %constant.58.clone.order_ref) | copy-start | bytes 98308
  107.5 3.3 %collective-permute-start.9 = (bf16[4,432,384]{2,1,0:T(8,128)(2,1)}, bf16[4,432,384]{2,1,0:T(8,128)(2,1)S(1)}, u32[]{:S(2)}, u32[]{:S(2)}) collective-permute-start(bf16[4,432,384]{2,1,0:T(8,128)(2,1)} %bitcast.34), channel_id=1, source_target_pairs={{0,1},{1,0},{2,3},{3,2},{4,5},{5,4},{6,7},{7,6},{8,9},{9,8},{10,11... | collective-permute-start | bytes 3981320 | tf_op jit(solution)/shard_map/ppermute | solution.py:460
  (12 other events, 139.6 us)
Sparse Core Ops, SparseCore 0:
  69.6 24.1 all-gather.2

commit v8 on v7

--- a/solution.py
+++ b/solution.py
@@ -122,11 +122,14 @@
 
 def measure_tile(
     tile_ref, lanes_ref, groups_ref, groups_t_ref, squares_ref, edges_ref,
-    placed_ref, west_ref, east_ref, sums_ref,
+    parcel_ref, north_ref, south_ref, west_ref, east_ref, sums_ref,
 ):
     tile = tile_ref[...]
     placed = dot(tile, lanes_ref[...]).astype(BF)
-    placed_ref[...] = placed
+    parcel_ref[0:320, :] = placed
+    parcel_ref[320:528, :] = jnp.zeros((208, CH), BF)
+    north_ref[...] = placed[0:80]
+    south_ref[...] = placed[240:320]
     edges = dot(edges_ref[...], placed).astype(BF)
     west_ref[...] = edges[0:16]
     east_ref[...] = edges[16:32]
@@ -362,9 +365,16 @@
     flat_tile = tile.reshape(ROWS * WIDE, CH)
 
     swapped = lax.ppermute(jnp.pad(by_group(kernel_second), ((0, 6), (0, 0))), BOTH, SWAP)
-    placed, west, east, sums = call(
+    parcel, north, south, west, east, sums = call(
         measure_tile,
-        (shape((320, CH), BF), shape((16, CH), BF), shape((16, CH), BF), shape((NY * COLS, 128), F32)),
+        (
+            shape((528, CH), BF),
+            shape((80, CH), BF),
+            shape((80, CH), BF),
+            shape((16, CH), BF),
+            shape((16, CH), BF),
+            shape((NY * COLS, 128), F32),
+        ),
         [],
         [],
         flat_tile,
@@ -379,9 +389,10 @@
     from_west, from_east = send(east, perm=moved(0, 1)), send(west, perm=moved(0, -1))
     plane_sums = lax.all_to_all(sums, BOTH, 0, 0, tiled=True, axis_index_groups=PLANE)
     sums_rows = call(pool_plane, shape((8, CH), BF), [], [], plane_sums)
-    from_north = send(jnp.concatenate([placed[240:320], from_west[12:16], from_east[12:16]]), perm=moved(1, 0))
-    from_south = send(jnp.concatenate([placed[0:80], from_west[0:4], from_east[0:4]]), perm=moved(-1, 0))
-    parcel = jnp.concatenate([placed, from_west, from_east, from_north, from_south], axis=0)
+    from_north = send(jnp.concatenate([south, from_west[12:16], from_east[12:16]]), perm=moved(1, 0))
+    from_south = send(jnp.concatenate([north, from_west[0:4], from_east[0:4]]), perm=moved(-1, 0))
+    for halo, row in ((from_west, 320), (from_east, 336), (from_north, 352), (from_south, 440)):
+        parcel = lax.dynamic_update_slice(parcel, halo, (row, 0))
     sums_rows, swapped, packed = lax.optimization_barrier((sums_rows, swapped, by_group(kernel_first)))
     letter = jnp.concatenate([packed, sums_rows[0:6], swapped], axis=0)
     letters = jnp.broadcast_to(letter[None], (NZ, 96, CH))
@@ -428,7 +439,7 @@
         jnp.asarray(SQUARES_OF_LANES),
         flops=int(2e10),
         out_places=HB,
-        grant=48,
+        grant=60,
     )
     own, stack = lax.optimization_barrier((own, stack))
     other = lax.ppermute(own, "space", SIBLING)

time: 148 us -> 150 us (1.014)
  waiting for transfers between devices: 24.6 us -> 22 us
  other arithmetic: 1.01 us -> 3.22 us
  local copies, waits for them, and re-layouts: 7.09 us -> 8.89 us
    dynamic_update_slice x0 -> x4, local copies, waits for them, and re-layouts: none -> 2.46 us  [shards(): parcel = lax.dynamic_update_slice(parcel, halo, (row, 0))]
    ppermute x2, waiting for transfers between devices: 4.09 us -> 2.3 us  [the longest x1 2.3 us: shards(): send(jnp.concatenate([north, from_west[0:4], from_east[0:4]]), perm=moved...]
    concatenate x2, other arithmetic: 0.03 us -> 1.68 us  [the longest x1 0.84 us: shards(): jnp.concatenate([south, from_west[12:16], from_east[12:16]])]
    unnamed x48 -> x44, local copies, waits for them, and re-layouts: 4.16 us -> 2.98 us
  transfers between devices with their start and end apart: 14 -> 14, of which waited for: 6 -> 5; matrix products, arithmetic and copies ran while one was open for 2% -> 5% of each run, Pallas kernels for 13% -> 14%
where the time goes in v8:
time: 150 us; the launch traced here: 148 us
  starting transfers between devices  34.9 us (23%)
  blocking collectives  33.7 us (22%)
  Pallas kernels  31.8 us (21%)
  waiting for transfers between devices  22 us (15%)
  between operations  13.8 us (9%)
  local copies, waits for them, and re-layouts  8.89 us (6%)
  other arithmetic  3.22 us (2%)
    pallas_call x7, Pallas kernels, call(): pl.pallas_call(body, out_shape=outs, in_specs=[*places, *[VM] * (len(args...  31.8 us
    all_to_all x1, blocking collectives, shards(): parts = lax.all_to_all(partial, 'tm', 0, 0, tiled=True)  17.9 us
    all_to_all x1, blocking collectives, shards(): all_sums = lax.all_to_all(sums, 'space', 0, 0, tiled=True)  15.7 us
    all_to_all x1, waiting for transfers between devices, shards(): lax.all_to_all(letters, 'space', 0, 0, tiled=True, axis_index_groups=ALON...  10.4 us
    all_to_all x1, starting transfers between devices, shards(): lax.all_to_all(letters, 'space', 0, 0, tiled=True, axis_index_groups=ALON...  9.03 us
    ppermute x1, starting transfers between devices, shards(): send(jnp.concatenate([south, from_west[12:16], from_east[12:16]]), perm=m...  7.49 us
    all_to_all x1, starting transfers between devices, shards(): lax.all_to_all(sums, BOTH, 0, 0, tiled=True, axis_index_groups=PLANE)  5.21 us
    ppermute x3, starting transfers between devices, shards(): lax.ppermute(parcel, 'tm', [(t, (t + k) % NY) for t in range(NY)])  4.27 us
  transfers between devices with their start and end apart: 14, of which 5 were waited for; matrix products, arithmetic and copies ran while one was open for 5% of the time, Pallas kernels for 14%

profile of v8, /device:TPU:32, one launch (start us, length us, event | category | flops | bytes accessed | tf_op | source)
XLA Modules:
  0.0 148.2 jit_solution(15884811760293688607)
XLA Ops:
  6.5 3.0 %shard_map.244 = (bf16[528,384]{1,0:T(8,128)(2,1)}, bf16[80,384]{1,0:T(8,128)(2,1)}, bf16[80,384]{1,0:T(8,128)(2,1)}, bf16[16,384]{1,0:T(8,128)(2,1)}, bf16[16,384]{1,0:T(8,128)(2,1)}, /*index=5*/f32[32,128]{1,0:T(8,128)}) custom-call(bf16[320,384]{1,0:T(8,128)(2,1)} %bitcast.42, bf16[384,384]{1,0:T(8,128)(2,1)} %constant.53.clone.lanes_ref, ...), custom_call_target="tpu_custom_call" | custom-call | tf_op jit(solution)/shard_map/pallas_call | solution.py:327
  9.7 3.8 %collective-permute-start.2 = (bf16[16,384]{1,0:T(8,128)(2,1)}, bf16[16,384]{1,0:T(8,128)(2,1)S(1)}, u32[]{:S(2)}, u32[]{:S(2)}) collective-permute-start(bf16[16,384]{1,0:T(8,128)(2,1)} %get-tuple-element.32), channel_id=1, source_target_pairs={{0,63},{1,0},{2,1},{3,2},{4,3},{5,4},{6,5},{7,6},{8,7},{9,8},{10,9... | collective-permute-start | bytes 36872 | tf_op jit(solution)/shard_map/ppermute | solution.py:389
  13.5 5.2 %all-to-all-start = ((f32[32,1,128]{2,1,0:T(1,128)}), f32[32,1,128]{2,1,0:T(1,128)S(1)}, u32[]{:S(2)}, u32[]{:S(2)}) async-start(f32[32,1,128]{2,1,0:T(1,128)} %bitcast.49), calls=%async_computation | async-start | bytes 32768 | tf_op jit(solution)/shard_map/all_to_all | solution.py:390
  21.4 0.8 pad_maximum_fusion.1
  22.3 7.5 %collective-permute-start.3 = (bf16[88,384]{1,0:T(8,128)(2,1)S(1)}, bf16[88,384]{1,0:T(8,128)(2,1)S(1)}, u32[]{:S(2)}, u32[]{:S(2)}) collective-permute-start(bf16[88,384]{1,0:T(8,128)(2,1)S(1)} %pad_maximum_fusion.1), channel_id=1, source_target_pairs={{0,8},{1,9},{2,10},{3,11},{4,12},{5,13},{6,14},{7,15},{8,16},{9,17... | collective-permute-start | bytes 202760 | tf_op jit(solution)/shard_map/ppermute | solution.py:392
  29.8 0.8 pad_maximum_fusion.2
  32.7 2.3 %collective-permute-done.4 = bf16[88,384]{1,0:T(8,128)(2,1)S(1)} collective-permute-done((bf16[88,384]{1,0:T(8,128)(2,1)S(1)}, bf16[88,384]{1,0:T(8,128)(2,1)S(1)}, u32[]{:S(2)}, u32[]{:S(2)}) %collective-permute-start.4) | collective-permute-done | bytes 67616 | tf_op jit(solution)/shard_map/ppermute | solution.py:393
  35.6 0.9 broadcast_in_dim.2
  36.5 9.0 %all-to-all-start.1 = ((bf16[8,96,384]{2,1,0:T(8,128)(2,1)}), bf16[8,96,384]{2,1,0:T(8,128)(2,1)S(1)}, u32[]{:S(2)}, u32[]{:S(2)}) async-start(bf16[8,96,384]{2,1,0:T(8,128)(2,1)} %broadcast_in_dim.2), calls=%async_computation.1 | async-start | bytes 1179648 | tf_op jit(solution)/shard_map/all_to_all | solution.py:400
  45.5 1.9 %collective-permute-start.6 = (bf16[528,384]{1,0:T(8,128)(2,1)}, bf16[528,384]{1,0:T(8,128)(2,1)S(1)}, u32[]{:S(2)}, u32[]{:S(2)}) collective-permute-start(bf16[528,384]{1,0:T(8,128)(2,1)} %constant_dynamic-update-slice_fusion.lat0_ref), channel_id=1, source_target_pairs={{0,128},{64,192},{128,0},{192,64},{1,129},{65,193},{129,1},{193,65... | collective-permute-start | bytes 1216520 | tf_op jit(solution)/shard_map/ppermute | solution.py:401
  47.4 2.4 %collective-permute-start.7 = (bf16[528,384]{1,0:T(8,128)(2,1)}, bf16[528,384]{1,0:T(8,128)(2,1)S(1)}, u32[]{:S(2)}, u32[]{:S(2)}) collective-permute-start(bf16[528,384]{1,0:T(8,128)(2,1)} %constant_dynamic-update-slice_fusion.lat0_ref), channel_id=1, source_target_pairs={{0,192},{64,0},{128,64},{192,128},{1,193},{65,1},{129,65},{193,129... | collective-permute-start | bytes 1216520 | tf_op jit(solution)/shard_map/ppermute | solution.py:401
  51.1 10.4 %all-to-all-done.1.got_ref = bf16[8,96,384]{2,1,0:T(8,128)(2,1)S(1)} async-done(((bf16[8,96,384]{2,1,0:T(8,128)(2,1)}), bf16[8,96,384]{2,1,0:T(8,128)(2,1)S(1)}, u32[]{:S(2)}, u32[]{:S(2)}) %all-to-all-start.1) | async-done | bytes 589856 | tf_op jit(solution)/shard_map/all_to_all | solution.py:400
  61.6 1.4 shard_map.246
  63.5 1.1 shard_map.247
  64.6 4.2 %all-to-all-start.2 = ((bf16[4,336,384]{2,1,0:T(8,128)(2,1)}), bf16[4,336,384]{2,1,0:T(8,128)(2,1)S(1)}, u32[]{:S(2)}, u32[]{:S(2)}) async-start(bf16[4,336,384]{2,1,0:T(8,128)(2,1)} %get-tuple-element.38), calls=%async_computation.2 | async-start | bytes 2064384 | tf_op jit(solution)/shard_map/all_to_all | solution.py:420
  70.6 6.4 %shard_map.248.stack_ref = bf16[4,592,1152]{2,1,0:T(8,128)(2,1)} custom-call(s32[2]{0:T(128)} %pad_add_fusion.pos_ref, bf16[528,384]{1,0:T(8,128)(2,1)} %constant_dynamic-update-slice_fusion.lat0_ref, bf16[528,384]{1,0:T(8,128)(2,1)} %copy-done.19, bf16[528,384]{1,0:T(8,128)(2,1)} %copy-done.20, bf16[528,384]{1,0:T(8,128)(2,1)} %copy-done.21, ...), custom_call_target="tpu_custom_call" | custom-call | flops 20000000000 | tf_op jit(solution)/shard_map/pallas_call | solution.py:327
  77.1 2.6 %all-to-all-done.2 = bf16[4,336,384]{2,1,0:T(8,128)(2,1)S(1)} async-done(((bf16[4,336,384]{2,1,0:T(8,128)(2,1)}), bf16[4,336,384]{2,1,0:T(8,128)(2,1)S(1)}, u32[]{:S(2)}, u32[]{:S(2)}) %all-to-all-start.2) | async-done | bytes 1032224 | tf_op jit(solution)/shard_map/all_to_all | solution.py:420
  79.6 2.6 %collective-permute-done.8 = bf16[4,336,384]{2,1,0:T(8,128)(2,1)S(1)} collective-permute-done((bf16[4,336,384]{2,1,0:T(8,128)(2,1)S(1)}, bf16[4,336,384]{2,1,0:T(8,128)(2,1)S(1)}, u32[]{:S(2)}, u32[]{:S(2)}) %collective-permute-start.8) | collective-permute-done | bytes 1032224 | tf_op jit(solution)/shard_map/ppermute | solution.py:445
  82.3 11.3 %shard_map.249 = (f32[4,496,128]{2,1,0:T(8,128)S(1)}, f32[64,128]{1,0:T(8,128)S(1)}) custom-call(s32[2]{0:T(128)S(1)} %copy-done.10, bf16[4,592,1152]{2,1,0:T(8,128)(2,1)} %shard_map.248.stack_ref, bf16[4,7,48,384]{3,2,1,0:T(8,128)(2,1)S(1)} %bitcast.33, bf16[4,7,48,384]{3,2,1,0:T(8,128)(2,1)S(1)} %bitcast.37, f32[8,384]{1,0:T(8,128)S(1)} %copy-done.4, ...), custom_call_target="tpu_custom_call" | custom-call | tf_op jit(solution)/shard_map/pallas_call | solution.py:327
  93.6 15.7 %all_to_all.37 = f32[64,1,128]{2,1,0:T(1,128)S(1)} all-to-all(f32[64,1,128]{2,1,0:T(1,128)S(1)} %bitcast.40), channel_id=1, replica_groups=mesh['tm'=4,'space'=64] {'space'}, dimensions={0} | all-to-all | bytes 65536 | tf_op jit(solution)/shard_map/all_to_all | solution.py:468
  109.3 3.3 %collective-permute-done.9 = bf16[4,432,384]{2,1,0:T(8,128)(2,1)S(1)} collective-permute-done((bf16[4,432,384]{2,1,0:T(8,128)(2,1)}, bf16[4,432,384]{2,1,0:T(8,128)(2,1)S(1)}, u32[]{:S(2)}, u32[]{:S(2)}) %collective-permute-start.9) | collective-permute-done | bytes 1327136 | tf_op jit(solution)/shard_map/ppermute | solution.py:471
  112.6 1.3 copy-done
  113.9 8.6 %shard_map.250 = bf16[4,8,40,384]{3,2,1,0:T(8,128)(2,1)S(1)} custom-call(s32[2]{0:T(128)S(1)} %copy-done.10, f32[4,496,128]{2,1,0:T(8,128)S(1)} %get-tuple-element.43.field_ref, bf16[4,27,16,384]{3,2,1,0:T(8,128)(2,1)S(1)} %bitcast.35, bf16[4,27,16,384]{3,2,1,0:T(8,128)(2,1)S(1)} %bitcast.36, f32[64,128]{1,0:T(8,128)S(1)} %bitcast.38, ...), custom_call_target="tpu_custom_call" | custom-call | tf_op jit(solution)/shard_map/pallas_call | solution.py:327
  122.5 17.9 %all_to_all.38 = bf16[4,8,40,384]{3,2,1,0:T(8,128)(2,1)S(1)} all-to-all(bf16[4,8,40,384]{3,2,1,0:T(8,128)(2,1)S(1)} %shard_map.250), channel_id=1, replica_groups=mesh['tm'=4,'space'=64] {'tm'}, dimensions={0} | all-to-all | bytes 1966080 | tf_op jit(solution)/shard_map/all_to_all | solution.py:495
  (85 shorter events, 9.9 us)
Async XLA Ops:
  9.5 40.3 %copy-start.14 = (f32[384]{0:T(512)S(1)}, f32[384]{0:T(512)}, u32[]{:S(2)}) copy-start(f32[384]{0:T(512)} %param.27) | copy-start | bytes 4612
  9.5 40.3 %copy-start.15 = (f32[384]{0:T(512)S(1)}, f32[384]{0:T(512)}, u32[]{:S(2)}) copy-start(f32[384]{0:T(512)} %param.28) | copy-start | bytes 4612
  9.5 40.3 %copy-start.16 = (f32[384]{0:T(512)S(1)}, f32[384]{0:T(512)}, u32[]{:S(2)}) copy-start(f32[384]{0:T(512)} %param.30) | copy-start | bytes 4612
  9.5 40.3 %copy-start.17 = (f32[384]{0:T(512)S(1)}, f32[384]{0:T(512)}, u32[]{:S(2)}) copy-start(f32[384]{0:T(512)} %param.31) | copy-start | bytes 4612
  9.5 40.3 %copy-start.18 = (f32[384]{0:T(512)S(1)}, f32[384]{0:T(512)}, u32[]{:S(2)}) copy-start(f32[384]{0:T(512)} %param.32) | copy-start | bytes 4612
  9.6 40.3 %copy-start.13 = (f32[384]{0:T(512)S(1)}, f32[384]{0:T(512)}, u32[]{:S(2)}) copy-start(f32[384]{0:T(512)} %param.34) | copy-start | bytes 4612
  9.6 52.0 %copy-start.3 = (bf16[336,384]{1,0:T(8,128)(2,1)S(1)}, bf16[336,384]{1,0:T(8,128)(2,1)}, u32[]{:S(2)}) copy-start(bf16[336,384]{1,0:T(8,128)(2,1)} %constant.58.clone.rows_ref) | copy-start | bytes 774148
  9.6 11.8 %collective-permute-start.1 = (bf16[16,384]{1,0:T(8,128)(2,1)}, bf16[16,384]{1,0:T(8,128)(2,1)S(1)}, u32[]{:S(2)}, u32[]{:S(2)}) collective-permute-start(bf16[16,384]{1,0:T(8,128)(2,1)} %get-tuple-element.31), channel_id=1, source_target_pairs={{0,1},{1,2},{2,3},{3,4},{4,5},{5,6},{6,7},{7,8},{8,9},{9,10},{10,1... | collective-permute-start | bytes 36872 | tf_op jit(solution)/shard_map/ppermute | solution.py:389
  9.7 11.7 %collective-permute-start.2 = (bf16[16,384]{1,0:T(8,128)(2,1)}, bf16[16,384]{1,0:T(8,128)(2,1)S(1)}, u32[]{:S(2)}, u32[]{:S(2)}) collective-permute-start(bf16[16,384]{1,0:T(8,128)(2,1)} %get-tuple-element.32), channel_id=1, source_target_pairs={{0,63},{1,0},{2,1},{3,2},{4,3},{5,4},{6,5},{7,6},{8,7},{9,8},{10,9... | collective-permute-start | bytes 36872 | tf_op jit(solution)/shard_map/ppermute | solution.py:389
  13.5 18.4 %all-to-all-start = ((f32[32,1,128]{2,1,0:T(1,128)}), f32[32,1,128]{2,1,0:T(1,128)S(1)}, u32[]{:S(2)}, u32[]{:S(2)}) async-start(f32[32,1,128]{2,1,0:T(1,128)} %bitcast.49), calls=%async_computation | async-start | bytes 32768 | tf_op jit(solution)/shard_map/all_to_all | solution.py:390
  19.7 43.8 %copy-start.9 = (bf16[112,96]{1,0:T(8,128)(2,1)S(1)}, bf16[112,96]{1,0:T(8,128)(2,1)}, u32[]{:S(2)}) copy-start(bf16[112,96]{1,0:T(8,128)(2,1)} %constant.59.clone.rows_ref) | copy-start | bytes 64516
  19.7 12.3 %collective-permute-start = (bf16[48,384]{1,0:T(8,128)(2,1)S(1)}, bf16[48,384]{1,0:T(8,128)(2,1)S(1)}, u32[]{:S(2)}, u32[]{:S(2)}) collective-permute-start(bf16[48,384]{1,0:T(8,128)(2,1)S(1)} %pad.12), channel_id=1, source_target_pairs={{0,0},{1,1},{2,2},{3,3},{4,4},{5,5},{6,6},{7,7},{8,8},{9,9},{10,10... | collective-permute-start | bytes 110600 | tf_op jit(solution)/shard_map/ppermute | solution.py:367
  22.3 9.8 %collective-permute-start.3 = (bf16[88,384]{1,0:T(8,128)(2,1)S(1)}, bf16[88,384]{1,0:T(8,128)(2,1)S(1)}, u32[]{:S(2)}, u32[]{:S(2)}) collective-permute-start(bf16[88,384]{1,0:T(8,128)(2,1)S(1)} %pad_maximum_fusion.1), channel_id=1, source_target_pairs={{0,8},{1,9},{2,10},{3,11},{4,12},{5,13},{6,14},{7,15},{8,16},{9,17... | collective-permute-start | bytes 202760 | tf_op jit(solution)/shard_map/ppermute | solution.py:392
  30.6 4.4 %collective-permute-start.4 = (bf16[88,384]{1,0:T(8,128)(2,1)S(1)}, bf16[88,384]{1,0:T(8,128)(2,1)S(1)}, u32[]{:S(2)}, u32[]{:S(2)}) collective-permute-start(bf16[88,384]{1,0:T(8,128)(2,1)S(1)} %pad_maximum_fusion.2), channel_id=1, source_target_pairs={{0,56},{1,57},{2,58},{3,59},{4,60},{5,61},{6,62},{7,63},{8,0},{9,1... | collective-permute-start | bytes 202760 | tf_op jit(solution)/shard_map/ppermute | solution.py:393
  36.5 25.1 %all-to-all-start.1 = ((bf16[8,96,384]{2,1,0:T(8,128)(2,1)}), bf16[8,96,384]{2,1,0:T(8,128)(2,1)S(1)}, u32[]{:S(2)}, u32[]{:S(2)}) async-start(bf16[8,96,384]{2,1,0:T(8,128)(2,1)} %broadcast_in_dim.2), calls=%async_computation.1 | async-start | bytes 1179648 | tf_op jit(solution)/shard_map/all_to_all | solution.py:400
  45.5 24.1 %collective-permute-start.5 = (bf16[528,384]{1,0:T(8,128)(2,1)}, bf16[528,384]{1,0:T(8,128)(2,1)S(1)}, u32[]{:S(2)}, u32[]{:S(2)}) collective-permute-start(bf16[528,384]{1,0:T(8,128)(2,1)} %constant_dynamic-update-slice_fusion.lat0_ref), channel_id=1, source_target_pairs={{0,64},{64,128},{128,192},{192,0},{1,65},{65,129},{129,193},{193,1... | collective-permute-start | bytes 1216520 | tf_op jit(solution)/shard_map/ppermute | solution.py:401
  45.5 24.1 %collective-permute-start.6 = (bf16[528,384]{1,0:T(8,128)(2,1)}, bf16[528,384]{1,0:T(8,128)(2,1)S(1)}, u32[]{:S(2)}, u32[]{:S(2)}) collective-permute-start(bf16[528,384]{1,0:T(8,128)(2,1)} %constant_dynamic-update-slice_fusion.lat0_ref), channel_id=1, source_target_pairs={{0,128},{64,192},{128,0},{192,64},{1,129},{65,193},{129,1},{193,65... | collective-permute-start | bytes 1216520 | tf_op jit(solution)/shard_map/ppermute | solution.py:401
  47.4 22.2 %collective-permute-start.7 = (bf16[528,384]{1,0:T(8,128)(2,1)}, bf16[528,384]{1,0:T(8,128)(2,1)S(1)}, u32[]{:S(2)}, u32[]{:S(2)}) collective-permute-start(bf16[528,384]{1,0:T(8,128)(2,1)} %constant_dynamic-update-slice_fusion.lat0_ref), channel_id=1, source_target_pairs={{0,192},{64,0},{128,64},{192,128},{1,193},{65,1},{129,65},{193,129... | collective-permute-start | bytes 1216520 | tf_op jit(solution)/shard_map/ppermute | solution.py:401
  64.6 15.1 %all-to-all-start.2 = ((bf16[4,336,384]{2,1,0:T(8,128)(2,1)}), bf16[4,336,384]{2,1,0:T(8,128)(2,1)S(1)}, u32[]{:S(2)}, u32[]{:S(2)}) async-start(bf16[4,336,384]{2,1,0:T(8,128)(2,1)} %get-tuple-element.38), calls=%async_computation.2 | async-start | bytes 2064384 | tf_op jit(solution)/shard_map/all_to_all | solution.py:420
  68.8 40.5 %all-gather.3.cloned.1.call-start = ((), (), s32[]{:S(2)}) async-start(), calls=%async_computation.5 | async-start | bytes 1658880 | tf_op jit(solution)/shard_map/all_gather | solution.py:469
  79.6 2.6 %collective-permute-start.8 = (bf16[4,336,384]{2,1,0:T(8,128)(2,1)S(1)}, bf16[4,336,384]{2,1,0:T(8,128)(2,1)S(1)}, u32[]{:S(2)}, u32[]{:S(2)}) collective-permute-start(bf16[4,336,384]{2,1,0:T(8,128)(2,1)S(1)} %all-to-all-done.2), channel_id=1, source_target_pairs={{0,1},{1,0},{2,3},{3,2},{4,5},{5,4},{6,7},{7,6},{8,9},{9,8},{10,11... | collective-permute-start | bytes 3096584 | tf_op jit(solution)/shard_map/ppermute | solution.py:445
  82.3 30.3 %copy-start.5 = (f32[128,128]{1,0:T(8,128)S(1)}, f32[128,128]{1,0:T(8,128)}, u32[]{:S(2)}) copy-start(f32[128,128]{1,0:T(8,128)} %constant.66.clone.squares_t_ref) | copy-start | bytes 196612
  82.3 30.3 %copy-start.8 = (bf16[128,128]{1,0:T(8,128)(2,1)S(1)}, bf16[128,128]{1,0:T(8,128)(2,1)}, u32[]{:S(2)}) copy-start(bf16[128,128]{1,0:T(8,128)(2,1)} %constant.67.clone.order_ref) | copy-start | bytes 98308
  109.3 3.3 %collective-permute-start.9 = (bf16[4,432,384]{2,1,0:T(8,128)(2,1)}, bf16[4,432,384]{2,1,0:T(8,128)(2,1)S(1)}, u32[]{:S(2)}, u32[]{:S(2)}) collective-permute-start(bf16[4,432,384]{2,1,0:T(8,128)(2,1)} %bitcast.34), channel_id=1, source_target_pairs={{0,1},{1,0},{2,3},{3,2},{4,5},{5,4},{6,7},{7,6},{8,9},{9,8},{10,11... | collective-permute-start | bytes 3981320 | tf_op jit(solution)/shard_map/ppermute | solution.py:471
  (12 other events, 92.8 us)
Sparse Core Ops, SparseCore 0:
  71.5 24.0 all-gather.2

commit v9 on v7

--- a/solution.py
+++ b/solution.py
@@ -428,7 +428,7 @@
         jnp.asarray(SQUARES_OF_LANES),
         flops=int(2e10),
         out_places=HB,
-        grant=48,
+        grant=60,
     )
     own, stack = lax.optimization_barrier((own, stack))
     other = lax.ppermute(own, "space", SIBLING)

time: 148 us -> 149 us (level)
    unnamed x48 -> x52, local copies, waits for them, and re-layouts: 4.16 us -> 4.02 us
  transfers between devices with their start and end apart: 14 -> 14, of which waited for: 6 -> 6; matrix products, arithmetic and copies ran while one was open for 2% -> 3% of each run, Pallas kernels for 13% -> 14%
where the time goes in v9:
time: 149 us; the launch traced here: 147 us
  starting transfers between devices  34.9 us (23%)
  blocking collectives  33.7 us (23%)
  Pallas kernels  31.8 us (21%)
  waiting for transfers between devices  23.7 us (16%)
  between operations  13.8 us (9%)
  local copies, waits for them, and re-layouts  7.62 us (5%)
  other arithmetic  1.55 us (1%)
    pallas_call x7, Pallas kernels, call(): pl.pallas_call(body, out_shape=outs, in_specs=[*places, *[VM] * (len(args...  31.8 us
    all_to_all x1, blocking collectives, shards(): parts = lax.all_to_all(partial, 'tm', 0, 0, tiled=True)  17.9 us
    all_to_all x1, blocking collectives, shards(): all_sums = lax.all_to_all(sums, 'space', 0, 0, tiled=True)  15.8 us
    all_to_all x1, waiting for transfers between devices, shards(): lax.all_to_all(letters, 'space', 0, 0, tiled=True, axis_index_groups=ALON...  10.4 us
    all_to_all x1, starting transfers between devices, shards(): lax.all_to_all(letters, 'space', 0, 0, tiled=True, axis_index_groups=ALON...  9.03 us
    ppermute x1, starting transfers between devices, shards(): send(jnp.concatenate([placed[240:320], from_west[12:16], from_east[12:16]...  7.41 us
    all_to_all x1, starting transfers between devices, shards(): lax.all_to_all(sums, BOTH, 0, 0, tiled=True, axis_index_groups=PLANE)  5.22 us
    ppermute x3, starting transfers between devices, shards(): lax.ppermute(parcel, 'tm', [(t, (t + k) % NY) for t in range(NY)])  4.36 us
  transfers between devices with their start and end apart: 14, of which 6 were waited for; matrix products, arithmetic and copies ran while one was open for 3% of the time, Pallas kernels for 14%

profile of v9, /device:TPU:32, one launch (start us, length us, event | category | flops | bytes accessed | tf_op | source)
XLA Modules:
  0.0 147.1 jit_solution(10014166659354425916)
XLA Ops:
  6.5 3.0 %shard_map.244 = (bf16[320,384]{1,0:T(8,128)(2,1)}, bf16[16,384]{1,0:T(8,128)(2,1)}, bf16[16,384]{1,0:T(8,128)(2,1)}, f32[32,128]{1,0:T(8,128)}) custom-call(bf16[320,384]{1,0:T(8,128)(2,1)} %bitcast.42, bf16[384,384]{1,0:T(8,128)(2,1)} %constant.44.clone.lanes_ref, f32[384,128]{1,0:T(8,128)} %constant.45.clone.groups_ref, ...), custom_call_target="tpu_custom_call" | custom-call | tf_op jit(solution)/shard_map/pallas_call | solution.py:324
  9.5 3.9 %collective-permute-start.2 = (bf16[16,384]{1,0:T(8,128)(2,1)}, bf16[16,384]{1,0:T(8,128)(2,1)S(1)}, u32[]{:S(2)}, u32[]{:S(2)}) collective-permute-start(bf16[16,384]{1,0:T(8,128)(2,1)} %get-tuple-element.30), channel_id=1, source_target_pairs={{0,63},{1,0},{2,1},{3,2},{4,3},{5,4},{6,5},{7,6},{8,7},{9,8},{10,9... | collective-permute-start | bytes 36872 | tf_op jit(solution)/shard_map/ppermute | solution.py:379
  13.4 5.2 %all-to-all-start = ((f32[32,1,128]{2,1,0:T(1,128)}), f32[32,1,128]{2,1,0:T(1,128)S(1)}, u32[]{:S(2)}, u32[]{:S(2)}) async-start(f32[32,1,128]{2,1,0:T(1,128)} %bitcast.49), calls=%async_computation | async-start | bytes 32768 | tf_op jit(solution)/shard_map/all_to_all | solution.py:380
  21.2 1.0 constant_dynamic-update-slice_fusion.4
  22.5 7.4 %collective-permute-start.3 = (bf16[88,384]{1,0:T(8,128)(2,1)S(1)}, bf16[88,384]{1,0:T(8,128)(2,1)S(1)}, u32[]{:S(2)}, u32[]{:S(2)}) collective-permute-start(bf16[88,384]{1,0:T(8,128)(2,1)S(1)} %pad_maximum_fusion.1), channel_id=1, source_target_pairs={{0,8},{1,9},{2,10},{3,11},{4,12},{5,13},{6,14},{7,15},{8,16},{9,17... | collective-permute-start | bytes 202760 | tf_op jit(solution)/shard_map/ppermute | solution.py:382
  30.1 1.7 %collective-permute-done.3 = bf16[88,384]{1,0:T(8,128)(2,1)S(1)} collective-permute-done((bf16[88,384]{1,0:T(8,128)(2,1)S(1)}, bf16[88,384]{1,0:T(8,128)(2,1)S(1)}, u32[]{:S(2)}, u32[]{:S(2)}) %collective-permute-start.3) | collective-permute-done | bytes 67616 | tf_op jit(solution)/shard_map/ppermute | solution.py:382
  31.8 2.4 %collective-permute-done.4 = bf16[88,384]{1,0:T(8,128)(2,1)S(1)} collective-permute-done((bf16[88,384]{1,0:T(8,128)(2,1)S(1)}, bf16[88,384]{1,0:T(8,128)(2,1)S(1)}, u32[]{:S(2)}, u32[]{:S(2)}) %collective-permute-start.4) | collective-permute-done | bytes 67616 | tf_op jit(solution)/shard_map/ppermute | solution.py:383
  34.3 1.0 broadcast_in_dim.2
  35.2 9.0 %all-to-all-start.1 = ((bf16[8,96,384]{2,1,0:T(8,128)(2,1)}), bf16[8,96,384]{2,1,0:T(8,128)(2,1)S(1)}, u32[]{:S(2)}, u32[]{:S(2)}) async-start(bf16[8,96,384]{2,1,0:T(8,128)(2,1)} %broadcast_in_dim.2), calls=%async_computation.1 | async-start | bytes 1179648 | tf_op jit(solution)/shard_map/all_to_all | solution.py:389
  44.3 2.0 %collective-permute-start.6 = (bf16[528,384]{1,0:T(8,128)(2,1)S(1)}, bf16[528,384]{1,0:T(8,128)(2,1)S(1)}, u32[]{:S(2)}, u32[]{:S(2)}) collective-permute-start(bf16[528,384]{1,0:T(8,128)(2,1)S(1)} %constant_dynamic-update-slice_fusion.lat0_ref), channel_id=1, source_target_pairs={{0,128},{64,192},{128,0},{192,64},{1,129},{65,193},{129,1},{193,65... | collective-permute-start | bytes 1216520 | tf_op jit(solution)/shard_map/ppermute | solution.py:390
  46.2 2.4 %collective-permute-start.7 = (bf16[528,384]{1,0:T(8,128)(2,1)S(1)}, bf16[528,384]{1,0:T(8,128)(2,1)S(1)}, u32[]{:S(2)}, u32[]{:S(2)}) collective-permute-start(bf16[528,384]{1,0:T(8,128)(2,1)S(1)} %constant_dynamic-update-slice_fusion.lat0_ref), channel_id=1, source_target_pairs={{0,192},{64,0},{128,64},{192,128},{1,193},{65,1},{129,65},{193,129... | collective-permute-start | bytes 1216520 | tf_op jit(solution)/shard_map/ppermute | solution.py:390
  49.9 10.4 %all-to-all-done.1.got_ref = bf16[8,96,384]{2,1,0:T(8,128)(2,1)S(1)} async-done(((bf16[8,96,384]{2,1,0:T(8,128)(2,1)}), bf16[8,96,384]{2,1,0:T(8,128)(2,1)S(1)}, u32[]{:S(2)}, u32[]{:S(2)}) %all-to-all-start.1) | async-done | bytes 589856 | tf_op jit(solution)/shard_map/all_to_all | solution.py:389
  60.3 1.4 shard_map.246
  62.3 1.1 shard_map.247
  63.3 4.2 %all-to-all-start.2 = ((bf16[4,336,384]{2,1,0:T(8,128)(2,1)}), bf16[4,336,384]{2,1,0:T(8,128)(2,1)S(1)}, u32[]{:S(2)}, u32[]{:S(2)}) async-start(bf16[4,336,384]{2,1,0:T(8,128)(2,1)} %get-tuple-element.34), calls=%async_computation.2 | async-start | bytes 2064384 | tf_op jit(solution)/shard_map/all_to_all | solution.py:409
  69.4 6.4 %shard_map.248.stack_ref = bf16[4,592,1152]{2,1,0:T(8,128)(2,1)} custom-call(s32[2]{0:T(128)} %pad_add_fusion.pos_ref, bf16[528,384]{1,0:T(8,128)(2,1)} %copy-done.13, bf16[528,384]{1,0:T(8,128)(2,1)} %copy-done.21, bf16[528,384]{1,0:T(8,128)(2,1)} %copy-done.22, bf16[528,384]{1,0:T(8,128)(2,1)} %copy-done.23, f32[8,128]{1,0:T(8,128)} %copy-done.11, ...), custom_call_target="tpu_custom_call" | custom-call | flops 20000000000 | tf_op jit(solution)/shard_map/pallas_call | solution.py:324
  75.8 2.6 %all-to-all-done.2 = bf16[4,336,384]{2,1,0:T(8,128)(2,1)S(1)} async-done(((bf16[4,336,384]{2,1,0:T(8,128)(2,1)}), bf16[4,336,384]{2,1,0:T(8,128)(2,1)S(1)}, u32[]{:S(2)}, u32[]{:S(2)}) %all-to-all-start.2) | async-done | bytes 1032224 | tf_op jit(solution)/shard_map/all_to_all | solution.py:409
  78.4 2.6 %collective-permute-done.8 = bf16[4,336,384]{2,1,0:T(8,128)(2,1)S(1)} collective-permute-done((bf16[4,336,384]{2,1,0:T(8,128)(2,1)S(1)}, bf16[4,336,384]{2,1,0:T(8,128)(2,1)S(1)}, u32[]{:S(2)}, u32[]{:S(2)}) %collective-permute-start.8) | collective-permute-done | bytes 1032224 | tf_op jit(solution)/shard_map/ppermute | solution.py:434
  81.1 11.3 %shard_map.249 = (f32[4,496,128]{2,1,0:T(8,128)S(1)}, f32[64,128]{1,0:T(8,128)S(1)}) custom-call(s32[2]{0:T(128)S(1)} %copy-done.10, bf16[4,592,1152]{2,1,0:T(8,128)(2,1)} %shard_map.248.stack_ref, bf16[4,7,48,384]{3,2,1,0:T(8,128)(2,1)S(1)} %bitcast.33, bf16[4,7,48,384]{3,2,1,0:T(8,128)(2,1)S(1)} %bitcast.37, f32[8,384]{1,0:T(8,128)S(1)} %copy-done.4, ...), custom_call_target="tpu_custom_call" | custom-call | tf_op jit(solution)/shard_map/pallas_call | solution.py:324
  92.4 15.8 %all_to_all.37 = f32[64,1,128]{2,1,0:T(1,128)S(1)} all-to-all(f32[64,1,128]{2,1,0:T(1,128)S(1)} %bitcast.40), channel_id=1, replica_groups=mesh['tm'=4,'space'=64] {'space'}, dimensions={0} | all-to-all | bytes 65536 | tf_op jit(solution)/shard_map/all_to_all | solution.py:457
  108.2 3.3 %collective-permute-done.9 = bf16[4,432,384]{2,1,0:T(8,128)(2,1)S(1)} collective-permute-done((bf16[4,432,384]{2,1,0:T(8,128)(2,1)}, bf16[4,432,384]{2,1,0:T(8,128)(2,1)S(1)}, u32[]{:S(2)}, u32[]{:S(2)}) %collective-permute-start.9) | collective-permute-done | bytes 1327136 | tf_op jit(solution)/shard_map/ppermute | solution.py:460
  111.5 1.3 copy-done
  112.8 8.6 %shard_map.250 = bf16[4,8,40,384]{3,2,1,0:T(8,128)(2,1)S(1)} custom-call(s32[2]{0:T(128)S(1)} %copy-done.10, f32[4,496,128]{2,1,0:T(8,128)S(1)} %get-tuple-element.39.field_ref, bf16[4,27,16,384]{3,2,1,0:T(8,128)(2,1)S(1)} %bitcast.35, bf16[4,27,16,384]{3,2,1,0:T(8,128)(2,1)S(1)} %bitcast.36, f32[64,128]{1,0:T(8,128)S(1)} %bitcast.38, ...), custom_call_target="tpu_custom_call" | custom-call | tf_op jit(solution)/shard_map/pallas_call | solution.py:324
  121.4 17.9 %all_to_all.38 = bf16[4,8,40,384]{3,2,1,0:T(8,128)(2,1)S(1)} all-to-all(bf16[4,8,40,384]{3,2,1,0:T(8,128)(2,1)S(1)} %shard_map.250), channel_id=1, replica_groups=mesh['tm'=4,'space'=64] {'tm'}, dimensions={0} | all-to-all | bytes 1966080 | tf_op jit(solution)/shard_map/all_to_all | solution.py:484
  (91 shorter events, 7.5 us)
Async XLA Ops:
  9.5 12.9 %collective-permute-start.1 = (bf16[16,384]{1,0:T(8,128)(2,1)}, bf16[16,384]{1,0:T(8,128)(2,1)S(1)}, u32[]{:S(2)}, u32[]{:S(2)}) collective-permute-start(bf16[16,384]{1,0:T(8,128)(2,1)} %get-tuple-element.29), channel_id=1, source_target_pairs={{0,1},{1,2},{2,3},{3,4},{4,5},{5,6},{6,7},{7,8},{8,9},{9,10},{10,1... | collective-permute-start | bytes 36872 | tf_op jit(solution)/shard_map/ppermute | solution.py:379
  9.5 12.9 %collective-permute-start.2 = (bf16[16,384]{1,0:T(8,128)(2,1)}, bf16[16,384]{1,0:T(8,128)(2,1)S(1)}, u32[]{:S(2)}, u32[]{:S(2)}) collective-permute-start(bf16[16,384]{1,0:T(8,128)(2,1)} %get-tuple-element.30), channel_id=1, source_target_pairs={{0,63},{1,0},{2,1},{3,2},{4,3},{5,4},{6,5},{7,6},{8,7},{9,8},{10,9... | collective-permute-start | bytes 36872 | tf_op jit(solution)/shard_map/ppermute | solution.py:379
  13.4 16.6 %all-to-all-start = ((f32[32,1,128]{2,1,0:T(1,128)}), f32[32,1,128]{2,1,0:T(1,128)S(1)}, u32[]{:S(2)}, u32[]{:S(2)}) async-start(f32[32,1,128]{2,1,0:T(1,128)} %bitcast.49), calls=%async_computation | async-start | bytes 32768 | tf_op jit(solution)/shard_map/all_to_all | solution.py:380
  19.5 29.2 %copy-start.16 = (f32[384]{0:T(512)S(1)}, f32[384]{0:T(512)}, u32[]{:S(2)}) copy-start(f32[384]{0:T(512)} %param.27) | copy-start | bytes 4612
  19.5 29.2 %copy-start.17 = (f32[384]{0:T(512)S(1)}, f32[384]{0:T(512)}, u32[]{:S(2)}) copy-start(f32[384]{0:T(512)} %param.28) | copy-start | bytes 4612
  19.5 29.2 %copy-start.18 = (f32[384]{0:T(512)S(1)}, f32[384]{0:T(512)}, u32[]{:S(2)}) copy-start(f32[384]{0:T(512)} %param.30) | copy-start | bytes 4612
  19.5 29.2 %copy-start.19 = (f32[384]{0:T(512)S(1)}, f32[384]{0:T(512)}, u32[]{:S(2)}) copy-start(f32[384]{0:T(512)} %param.31) | copy-start | bytes 4612
  19.5 29.2 %copy-start.20 = (f32[384]{0:T(512)S(1)}, f32[384]{0:T(512)}, u32[]{:S(2)}) copy-start(f32[384]{0:T(512)} %param.32) | copy-start | bytes 4612
  19.5 29.2 %copy-start.15 = (f32[384]{0:T(512)S(1)}, f32[384]{0:T(512)}, u32[]{:S(2)}) copy-start(f32[384]{0:T(512)} %param.34) | copy-start | bytes 4612
  19.6 40.8 %copy-start.3 = (bf16[336,384]{1,0:T(8,128)(2,1)S(1)}, bf16[336,384]{1,0:T(8,128)(2,1)}, u32[]{:S(2)}) copy-start(bf16[336,384]{1,0:T(8,128)(2,1)} %constant.49.clone.rows_ref) | copy-start | bytes 774148
  19.7 10.4 %collective-permute-start = (bf16[48,384]{1,0:T(8,128)(2,1)S(1)}, bf16[48,384]{1,0:T(8,128)(2,1)S(1)}, u32[]{:S(2)}, u32[]{:S(2)}) collective-permute-start(bf16[48,384]{1,0:T(8,128)(2,1)S(1)} %pad.12), channel_id=1, source_target_pairs={{0,0},{1,1},{2,2},{3,3},{4,4},{5,5},{6,6},{7,7},{8,8},{9,9},{10,10... | collective-permute-start | bytes 110600 | tf_op jit(solution)/shard_map/ppermute | solution.py:364
  22.2 40.1 %copy-start.9 = (bf16[112,96]{1,0:T(8,128)(2,1)S(1)}, bf16[112,96]{1,0:T(8,128)(2,1)}, u32[]{:S(2)}) copy-start(bf16[112,96]{1,0:T(8,128)(2,1)} %constant.50.clone.rows_ref) | copy-start | bytes 64516
  22.5 9.3 %collective-permute-start.3 = (bf16[88,384]{1,0:T(8,128)(2,1)S(1)}, bf16[88,384]{1,0:T(8,128)(2,1)S(1)}, u32[]{:S(2)}, u32[]{:S(2)}) collective-permute-start(bf16[88,384]{1,0:T(8,128)(2,1)S(1)} %pad_maximum_fusion.1), channel_id=1, source_target_pairs={{0,8},{1,9},{2,10},{3,11},{4,12},{5,13},{6,14},{7,15},{8,16},{9,17... | collective-permute-start | bytes 202760 | tf_op jit(solution)/shard_map/ppermute | solution.py:382
  29.9 4.4 %collective-permute-start.4 = (bf16[88,384]{1,0:T(8,128)(2,1)S(1)}, bf16[88,384]{1,0:T(8,128)(2,1)S(1)}, u32[]{:S(2)}, u32[]{:S(2)}) collective-permute-start(bf16[88,384]{1,0:T(8,128)(2,1)S(1)} %pad_maximum_fusion.2), channel_id=1, source_target_pairs={{0,56},{1,57},{2,58},{3,59},{4,60},{5,61},{6,62},{7,63},{8,0},{9,1... | collective-permute-start | bytes 202760 | tf_op jit(solution)/shard_map/ppermute | solution.py:383
  35.2 25.1 %all-to-all-start.1 = ((bf16[8,96,384]{2,1,0:T(8,128)(2,1)}), bf16[8,96,384]{2,1,0:T(8,128)(2,1)S(1)}, u32[]{:S(2)}, u32[]{:S(2)}) async-start(bf16[8,96,384]{2,1,0:T(8,128)(2,1)} %broadcast_in_dim.2), calls=%async_computation.1 | async-start | bytes 1179648 | tf_op jit(solution)/shard_map/all_to_all | solution.py:389
  44.3 24.1 %collective-permute-start.5 = (bf16[528,384]{1,0:T(8,128)(2,1)S(1)}, bf16[528,384]{1,0:T(8,128)(2,1)S(1)}, u32[]{:S(2)}, u32[]{:S(2)}) collective-permute-start(bf16[528,384]{1,0:T(8,128)(2,1)S(1)} %constant_dynamic-update-slice_fusion.lat0_ref), channel_id=1, source_target_pairs={{0,64},{64,128},{128,192},{192,0},{1,65},{65,129},{129,193},{193,1... | collective-permute-start | bytes 1216520 | tf_op jit(solution)/shard_map/ppermute | solution.py:390
  44.3 24.1 %collective-permute-start.6 = (bf16[528,384]{1,0:T(8,128)(2,1)S(1)}, bf16[528,384]{1,0:T(8,128)(2,1)S(1)}, u32[]{:S(2)}, u32[]{:S(2)}) collective-permute-start(bf16[528,384]{1,0:T(8,128)(2,1)S(1)} %constant_dynamic-update-slice_fusion.lat0_ref), channel_id=1, source_target_pairs={{0,128},{64,192},{128,0},{192,64},{1,129},{65,193},{129,1},{193,65... | collective-permute-start | bytes 1216520 | tf_op jit(solution)/shard_map/ppermute | solution.py:390
  46.2 22.1 %collective-permute-start.7 = (bf16[528,384]{1,0:T(8,128)(2,1)S(1)}, bf16[528,384]{1,0:T(8,128)(2,1)S(1)}, u32[]{:S(2)}, u32[]{:S(2)}) collective-permute-start(bf16[528,384]{1,0:T(8,128)(2,1)S(1)} %constant_dynamic-update-slice_fusion.lat0_ref), channel_id=1, source_target_pairs={{0,192},{64,0},{128,64},{192,128},{1,193},{65,1},{129,65},{193,129... | collective-permute-start | bytes 1216520 | tf_op jit(solution)/shard_map/ppermute | solution.py:390
  63.3 15.1 %all-to-all-start.2 = ((bf16[4,336,384]{2,1,0:T(8,128)(2,1)}), bf16[4,336,384]{2,1,0:T(8,128)(2,1)S(1)}, u32[]{:S(2)}, u32[]{:S(2)}) async-start(bf16[4,336,384]{2,1,0:T(8,128)(2,1)} %get-tuple-element.34), calls=%async_computation.2 | async-start | bytes 2064384 | tf_op jit(solution)/shard_map/all_to_all | solution.py:409
  67.6 40.6 %all-gather.3.cloned.1.call-start = ((), (), s32[]{:S(2)}) async-start(), calls=%async_computation.5 | async-start | bytes 1658880 | tf_op jit(solution)/shard_map/all_gather | solution.py:458
  78.4 2.6 %collective-permute-start.8 = (bf16[4,336,384]{2,1,0:T(8,128)(2,1)S(1)}, bf16[4,336,384]{2,1,0:T(8,128)(2,1)S(1)}, u32[]{:S(2)}, u32[]{:S(2)}) collective-permute-start(bf16[4,336,384]{2,1,0:T(8,128)(2,1)S(1)} %all-to-all-done.2), channel_id=1, source_target_pairs={{0,1},{1,0},{2,3},{3,2},{4,5},{5,4},{6,7},{7,6},{8,9},{9,8},{10,11... | collective-permute-start | bytes 3096584 | tf_op jit(solution)/shard_map/ppermute | solution.py:434
  81.1 30.4 %copy-start.5 = (f32[128,128]{1,0:T(8,128)S(1)}, f32[128,128]{1,0:T(8,128)}, u32[]{:S(2)}) copy-start(f32[128,128]{1,0:T(8,128)} %constant.57.clone.squares_t_ref) | copy-start | bytes 196612
  81.1 30.4 %copy-start.8 = (bf16[128,128]{1,0:T(8,128)(2,1)S(1)}, bf16[128,128]{1,0:T(8,128)(2,1)}, u32[]{:S(2)}) copy-start(bf16[128,128]{1,0:T(8,128)(2,1)} %constant.58.clone.order_ref) | copy-start | bytes 98308
  108.2 3.3 %collective-permute-start.9 = (bf16[4,432,384]{2,1,0:T(8,128)(2,1)}, bf16[4,432,384]{2,1,0:T(8,128)(2,1)S(1)}, u32[]{:S(2)}, u32[]{:S(2)}) collective-permute-start(bf16[4,432,384]{2,1,0:T(8,128)(2,1)} %bitcast.34), channel_id=1, source_target_pairs={{0,1},{1,0},{2,3},{3,2},{4,5},{5,4},{6,7},{7,6},{8,9},{9,8},{10,11... | collective-permute-start | bytes 3981320 | tf_op jit(solution)/shard_map/ppermute | solution.py:460
  (14 other events, 137.5 us)
Sparse Core Ops, SparseCore 0:
  70.2 24.1 all-gather.2
